TPU v7x, 32 devices: a whole 2x2x4 slice. The times are simulated.
32 devices in a mesh: dp: 16 (over z, y, core), tensor: 2 (over x).
Axes of the slice: x: 2, y: 2, z: 4, core: 2. Of those that a mesh axis runs over, the one named last changes fastest.
Arguments:
- hidden_in: bfloat16 [16384, 1536], P(('dp', 'tensor')), may hold values from -6 to 6
- segment: int32 [16384], P('dp'), may hold values from -1 to 1, as said below
- norm_gain: bfloat16 [1536], P('dp'), may hold values from 0.5 to 1.5
- in_gate: bfloat16 [1536, 3072], P('dp', 'tensor'), may hold values from -0.15625 to 0.15625
- in_value: bfloat16 [1536, 3072], P('dp', 'tensor'), may hold values from -0.15625 to 0.15625
- in_shared: bfloat16 [1536, 256], P('dp'), may hold values from -0.15625 to 0.15625
- in_step: bfloat16 [1536, 48], P('dp', 'tensor'), may hold values from -0.15625 to 0.15625
- value_taps: float32 [4, 3072], P(None, 'tensor'), may hold values from -3 to 3
- shared_taps: float32 [4, 256], replicated, may hold values from -3 to 3
- step_bias: float32 [48], P('tensor'), may hold values from -6 to -2
- decay_log: float32 [48], P('tensor'), may hold values from 0 to 2.77
- skip_gain: float32 [48], P('tensor'), may hold values from 0.5 to 1.5
- gate_gain: float32 [3072], P('tensor'), may hold values from 0.5 to 1.5
- out_proj: bfloat16 [3072, 1536], P('tensor', 'dp'), may hold values from -0.109375 to 0.109375
- cotangent: bfloat16 [16384, 1536], P(('dp', 'tensor')), may hold values from -6 to 6
Outputs:
- block_out: bfloat16 [16384, 1536], P(('dp', 'tensor'))
- input_grad: bfloat16 [16384, 1536], P(('dp', 'tensor'))
- norm_grad: float32 [1536], P('dp')
- gate_grad: float32 [1536, 3072], P('dp', 'tensor')
- value_grad: float32 [1536, 3072], P('dp', 'tensor')
- shared_grad: float32 [1536, 256], P('dp')
- step_grad: float32 [1536, 48], P('dp', 'tensor')
- taps_grad: float32 [4, 3072], P(None, 'tensor')
- sharetaps_grad: float32 [4, 256], replicated
- bias_grad: float32 [48], P('tensor')
- decay_grad: float32 [48], P('tensor')
- skip_grad: float32 [48], P('tensor')
- gating_grad: float32 [3072], P('tensor')
- proj_grad: float32 [3072, 1536], P('tensor', 'dp')
Inputs may be any that keep to these rules, and one draw needn't show every extreme that they name: `segment`: within each pack of 1024 rows: one or two sequences numbered 0 and 1 in order, each starting at a block boundary, the first at the pack's first row; a sequence's rows are consecutive, its live rows first and then -1 up to the end of its last block; the blocks after the last sequence hold -1. One sequence of every pack covers the last block of the pack's first half and the first block of its second half. A sequence has at most 1024 live rows, and some pack's has that many.
All inputs are finite; a program needn't handle non-finite values.
Results may differ from a plain program's by a relative error of at most 0.012.
Values may be sent and summed in bfloat16 or wider, within the bound.
No kernel may reach another device: no remote copies, remote signals or barrier semaphores. Data moves between devices by JAX's collectives and lax.ppermute only.
A program may use at most 192 MiB of HBM per device.

v0:
```python
import functools

import jax
import jax.numpy as jnp
from jax import lax
from jax.experimental import pallas as pl
from jax.experimental.pallas import tpu as pltpu
from jax.sharding import PartitionSpec as P

HEAD_DIM = 64
STATE = 128
KERNEL = 4
QLEN = 256
INNER = 3072
EPSILON = 1e-05
TILE = 256
SIDE = 384
WIDE_TILE = 512
LANES = 128
HALF = QLEN // 2
PER = TILE // HEAD_DIM

BF = jnp.bfloat16
F32 = jnp.float32
HIGH = lax.Precision.HIGHEST
ROOM = 53 * 1024 * 1024
WEIGHT = 3


def dot(left, right, left_dim=1, right_dim=0, precision=None):
    return lax.dot_general(
        left,
        right,
        (((left_dim,), (right_dim,)), ((), ())),
        preferred_element_type=F32,
        precision=precision,
    )


def iota(shape, dim):
    return lax.broadcasted_iota(jnp.int32, shape, dim)


def split_dot(values, chooser):
    high = values.astype(BF)
    rest = (values - high.astype(F32)).astype(BF)
    return dot(high, chooser) + dot(rest, chooser)


def whole(shape):
    return pl.BlockSpec(shape, lambda *_: (0,) * len(shape))


def smem():
    return pl.BlockSpec(memory_space=pltpu.SMEM)


def call(
    body,
    grid,
    in_specs,
    out_specs,
    out_shape,
    scratch,
    flops,
    moved,
    *args,
    deps=(),
    prefetch=0,
    aliases=None,
):
    count = len(args)

    def held(*refs):
        body(*refs[:count], *refs[count + len(deps) :])

    anywhere = [pl.BlockSpec(memory_space=pl.ANY)] * len(deps)
    return pl.pallas_call(
        held,
        grid_spec=pltpu.PrefetchScalarGridSpec(
            num_scalar_prefetch=prefetch,
            grid=grid,
            in_specs=list(in_specs) + anywhere,
            out_specs=out_specs,
            scratch_shapes=scratch,
        ),
        out_shape=[jax.ShapeDtypeStruct(shape, kind) for shape, kind in out_shape],
        input_output_aliases=aliases or {},
        compiler_params=pltpu.CompilerParams(vmem_limit_bytes=ROOM),
        cost_estimate=pl.CostEstimate(
            flops=flops * WEIGHT, bytes_accessed=moved, transcendentals=0
        ),
    )(*args, *deps)


def tied(value, *deps):
    anywhere = pl.BlockSpec(memory_space=pl.ANY)
    return pl.pallas_call(
        lambda *refs: None,
        in_specs=[anywhere] * (1 + len(deps)),
        out_specs=anywhere,
        out_shape=jax.ShapeDtypeStruct(value.shape, value.dtype),
        input_output_aliases={0: 0},
        compiler_params=pltpu.CompilerParams(vmem_limit_bytes=ROOM),
    )(value, *deps)


def silu_slope(sigma, inputs):
    return sigma * (1.0 + inputs * (1.0 - sigma))


def expand(narrow):
    first = iota((QLEN, LANES), 1) < HEAD_DIM
    parts = []
    for pair in range(PER // 2):
        left = jnp.broadcast_to(narrow[:, 2 * pair : 2 * pair + 1], (QLEN, LANES))
        right = jnp.broadcast_to(narrow[:, 2 * pair + 1 : 2 * pair + 2], (QLEN, LANES))
        parts.append(jnp.where(first, left, right))
    return jnp.concatenate(parts, axis=1)


def head_rows(narrow):
    return jnp.concatenate(
        [jnp.broadcast_to(narrow[:, h : h + 1], (HEAD_DIM, STATE)) for h in range(PER)], axis=0
    )


def lane_masks():
    first = iota((1, LANES), 1) < HEAD_DIM
    return (first.astype(BF), jnp.logical_not(first).astype(BF))


def fill_weight(out_ref, rows_ref, pieces):
    at = 0
    for piece in pieces:
        count, height = piece.shape[0], piece.shape[1]
        for i in range(count):
            start = pl.multiple_of(rows_ref[at], 16) if height % 16 == 0 else rows_ref[at]
            out_ref[pl.ds(start, height), :] = piece[i]
            at += 1


def conv_sum(ext, taps):
    total = taps[KERNEL - 1 : KERNEL, :] * ext[8 : 8 + QLEN, :]
    for lag in range(1, KERNEL):
        total = total + taps[KERNEL - 1 - lag : KERNEL - lag, :] * ext[8 - lag : 8 - lag + QLEN, :]
    return total


def norm_body(
    half_blocks,
    pieces_total,
    gain_lane,
    rows_ref,
    place,
    keep,
    own,
    got,
    taps,
    bias,
    decay,
    *refs,
):
    pieces = refs[:pieces_total]
    (
        feat,
        feat_t,
        shared,
        b_out,
        c_out,
        gram,
        gram_t,
        cols,
        pack,
        rowpack,
        side_w,
        gain,
        hold,
        ext,
    ) = refs[pieces_total:]
    b = pl.program_id(0)
    mine = (b // half_blocks) == place[0]

    @pl.when(b == 0)
    def _():
        fill_weight(side_w, rows_ref, pieces)
        edge = gain_lane // LANES * LANES
        spread = side_w[:, edge : edge + LANES].astype(F32).T
        gain[...] = spread[gain_lane - edge : gain_lane - edge + 1, :]

    @pl.when(mine)
    def _():
        hold[...] = own[...].astype(F32)

    @pl.when(jnp.logical_not(mine))
    def _():
        hold[...] = got[...].astype(F32)

    rows = hold[...]
    inverse = lax.rsqrt(jnp.mean(rows * rows, axis=1, keepdims=True) + EPSILON)
    normed = (rows * inverse * gain[...]).astype(BF)
    feat[...] = normed
    feat_t[...] = normed.T
    side = dot(normed, side_w[...])
    pre = side[:, :TILE]
    shared[...] = pre

    @pl.when(b == 0)
    def _():
        ext[...] = jnp.zeros_like(ext)

    ext[0:8, :] = ext[QLEN : QLEN + 8, :] * keep[b]
    ext[8 : 8 + QLEN, :] = pre
    conv = conv_sum(ext, taps)
    act = (conv * jax.nn.sigmoid(conv)).astype(BF)
    b_low = act[:, :STATE]
    c_low = act[:, STATE:]
    b_out[...] = b_low
    c_out[...] = c_low
    lower = iota((QLEN, QLEN), 0) >= iota((QLEN, QLEN), 1)
    upper = iota((QLEN, QLEN), 0) <= iota((QLEN, QLEN), 1)
    gram[0] = jnp.where(lower, dot(c_low, b_low, 1, 1), 0.0)
    gram_t[0] = jnp.where(upper, dot(b_low, c_low, 1, 1), 0.0)
    raw = side[:, TILE:] + bias[...]
    step = jnp.maximum(raw, 0.0) + jnp.log1p(jnp.exp(-jnp.abs(raw)))
    logdec = step * -jnp.exp(decay[...])
    cum = dot(lower.astype(F32), logdec, precision=HIGH)
    cols[0] = raw
    cols[1] = step
    cols[2] = logdec
    cum_t = cum.T
    step_t = step.T
    for j in range(pack.shape[0]):
        heads = slice(PER * j, PER * j + PER)
        pack[j] = jnp.concatenate([cum[:, heads], step[:, heads]], axis=1)
        rowpack[j, 0] = jnp.concatenate([cum_t[heads, :], step_t[heads, :]], axis=0)


def value_body(
    pieces_total,
    blocks,
    past,
    rows_ref,
    keep,
    feat,
    *refs,
):
    pieces = refs[:pieces_total]
    refs = refs[: pieces_total + 7] + refs[pieces_total + 7 + past :]
    (
        taps,
        skip,
        pack,
        rowpack,
        b_ref,
        c_ref,
        gram,
        weight,
        pre_out,
        act_out,
        slope_out,
        out_rows,
        entry,
        pre,
        ext,
        state,
    ) = refs[pieces_total:]
    fill_weight(weight, rows_ref, pieces)
    masks = lane_masks()
    for b in range(blocks):
        span = slice(b * QLEN, (b + 1) * QLEN)
        pre[...] = dot(feat[span, :], weight[...])
        pre_out[span, :] = pre[...].astype(BF)
        if b == 0:
            ext[0:8, :] = jnp.zeros((8, TILE), F32)
            state[...] = jnp.zeros_like(state)
        else:
            ext[0:8, :] = ext[QLEN : QLEN + 8, :] * keep[b]
        ext[8 : 8 + QLEN, :] = pre[...]
        conv = conv_sum(ext, taps)
        sigma = jax.nn.sigmoid(conv)
        act_low = (conv * sigma).astype(BF)
        act_out[span, :] = act_low
        slope_out[span, :] = silu_slope(sigma, conv).astype(BF)
        act = act_low.astype(F32)
        narrow = pack[0, span, :]
        cum = narrow[:, :PER]
        step = narrow[:, PER:]
        last = cum[QLEN - 1 : QLEN, :]
        stepped = (act * expand(step)).astype(BF)
        scaled = (act * expand(jnp.exp(last - cum) * step)).astype(BF)
        row_cum = rowpack[0, b]
        parts = []
        for pair in range(PER // 2):
            lanes = slice(pair * LANES, (pair + 1) * LANES)
            tops, lows, values = [], [], []
            for k in range(2):
                h = 2 * pair + k
                col = cum[:, h : h + 1]
                row = row_cum[h : h + 1, :]
                e00 = jnp.exp(jnp.minimum(col[:HALF] - row[:, :HALF], 0.0))
                e10 = jnp.exp(col[HALF:] - row[:, :HALF])
                e11 = jnp.exp(jnp.minimum(col[HALF:] - row[:, HALF:], 0.0))
                tops.append((gram[b, :HALF, :HALF] * e00).astype(BF))
                lows.append((gram[b, HALF:, :HALF] * e10).astype(BF))
                lows.append((gram[b, HALF:, HALF:] * e11).astype(BF))
                values.append(stepped[:, lanes] * masks[k])
            top = dot(
                jnp.concatenate(tops, axis=1),
                jnp.concatenate([v[:HALF] for v in values], axis=0),
            )
            low = dot(jnp.concatenate(lows, axis=1), jnp.concatenate(values, axis=0))
            parts.append(jnp.concatenate([top, low], axis=0))
        within = jnp.concatenate(parts, axis=1)
        held = state[...]
        entry[b] = held
        across = dot(c_ref[span, :], held.astype(BF), 1, 1)
        core = within + across * expand(jnp.exp(cum))
        out_rows[span, :] = core + act * skip[...]
        if b + 1 < blocks:
            fresh = dot(scaled, b_ref[span, :], 0, 0)
            state[...] = keep[b + 1] * (head_rows(jnp.exp(last)) * held + fresh)


def gate_body(pieces_total, rows_ref, feat, *refs):
    pieces = refs[:pieces_total]
    out_rows, _, weight, gate_out, squares = refs[pieces_total:]
    fill_weight(weight, rows_ref, pieces)

    @pl.when(pl.program_id(0) == 0)
    def _():
        squares[...] = jnp.zeros_like(squares)

    for b in range(feat.shape[0] // QLEN):
        span = slice(b * QLEN, (b + 1) * QLEN)
        gate = dot(feat[span, :], weight[...])
        gate_out[span, :] = gate.astype(BF)
        product = out_rows[span, :] * (gate * jax.nn.sigmoid(gate))
        power = product * product
        total = squares[span, :]
        for at in range(0, power.shape[1], LANES):
            total = total + power[:, at : at + LANES]
        squares[span, :] = total


def mask_body(half_blocks, place, own, got, live, out, out_t):
    b = pl.program_id(0)
    mine = (b // half_blocks) == place[0]

    @pl.when(mine)
    def _():
        out[...] = own[...] * live[...]

    @pl.when(jnp.logical_not(mine))
    def _():
        out[...] = got[...] * live[...]

    out_t[...] = out[...].T


def proj_body(place, left, out_rows, gate_ref, scale_ref, gain, gated_out, *outs):
    for b in range(gated_out.shape[0] // QLEN):
        span = slice(b * QLEN, (b + 1) * QLEN)
        gate = gate_ref[span, :].astype(F32)
        product = out_rows[span, :] * (gate * jax.nn.sigmoid(gate))
        gated_out[span, :] = (product * scale_ref[span, :] * gain[...]).astype(BF)
    emit_outer(place, dot(left[...], gated_out[...]), outs)


def branch_body(pieces_total, place, rows_ref, gated, grad, *refs):
    pieces = refs[:pieces_total]
    weight, send, mine, row_dot = refs[pieces_total:]
    s = pl.program_id(0)

    @pl.when(s == 0)
    def _():
        fill_weight(weight, rows_ref, pieces)

    branch = dot(gated[...], weight[...], 1, 1)
    row_dot[...] = jnp.sum(branch * grad[...].astype(F32), axis=1, keepdims=True)

    @pl.when(s < pl.num_programs(0) // 2)
    def _():
        send[...] = branch.astype(BF)

    @pl.when(s >= pl.num_programs(0) // 2)
    def _():
        mine[...] = branch


def gating_body(
    place,
    grad,
    weight,
    out_ref,
    gate_ref,
    act_ref,
    scale_ref,
    row_dot,
    gain,
    feat_t,
    _,
    core,
    gate_grad,
    sums,
    *outs,
):
    gating = jnp.zeros(gain.shape, F32)
    skipping = jnp.zeros(gain.shape, F32)
    for b in range(grad.shape[0] // QLEN):
        span = slice(b * QLEN, (b + 1) * QLEN)
        grad_gated = dot(grad[span, :], weight[...])
        gate = gate_ref[span, :].astype(F32)
        sigma = jax.nn.sigmoid(gate)
        act = gate * sigma
        out_rows = out_ref[span, :]
        scale = scale_ref[span, :]
        normal = out_rows * act * scale
        gating = gating + jnp.sum(grad_gated * normal, axis=0, keepdims=True)
        grad_product = scale * (
            grad_gated * gain[...] - normal * (row_dot[span, :] * (1.0 / INNER))
        )
        grad_out = grad_product * act
        core[span, :] = grad_out.astype(BF)
        gate_grad[span, :] = (grad_product * out_rows * silu_slope(sigma, gate)).astype(BF)
        skipping = skipping + jnp.sum(
            grad_out * act_ref[span, :].astype(F32), axis=0, keepdims=True
        )
    sums[...] = jnp.concatenate([gating, skipping], axis=0)
    emit_outer(place, dot(feat_t[...], gate_grad[...]), outs)


def scan_body(
    blocks,
    summed,
    outer_outs,
    place,
    keep,
    feat_t,
    slope_ref,
    core_ref,
    act_ref,
    pre_ref,
    out_ref,
    skip,
    taps,
    pack,
    rowpack,
    b_ref,
    c_ref,
    gram_t,
    entry,
    *refs,
):
    past = refs[:3] if summed else ()
    own = len(refs) - 9 - outer_outs
    outs = refs[own : own + outer_outs]
    grad_pre, taps_grad, gram_grad, b_grad, c_grad, stats = refs[own + outer_outs : -3]
    ext, tail, carry = refs[-3:]

    @pl.when(pl.program_id(0) == 0)
    def _():
        if past:
            gram_grad[...] = past[0][...]
            b_grad[...] = past[1][...]
            c_grad[...] = past[2][...]
        else:
            gram_grad[...] = jnp.zeros_like(gram_grad)
            b_grad[...] = jnp.zeros_like(b_grad)
            c_grad[...] = jnp.zeros_like(c_grad)

    masks = lane_masks()
    owner = iota((TILE, LANES), 0) // HEAD_DIM
    lane = iota((TILE, LANES), 1)
    chooser = [(lane == owner + PER * q).astype(BF) for q in range(4)]
    final_row = iota((QLEN, LANES), 0) == QLEN - 1
    ones = jnp.ones((8, STATE), BF)
    tap_sums = [jnp.zeros((1, TILE), F32) for _ in range(KERNEL)]
    for b in reversed(range(blocks)):
        span = slice(b * QLEN, (b + 1) * QLEN)
        final = b == blocks - 1
        grad_low = core_ref[span, :]
        grad = grad_low.astype(F32)
        act = act_ref[span, :].astype(F32)
        narrow = pack[0, span, :]
        cum = narrow[:, :PER]
        step = narrow[:, PER:]
        last = cum[QLEN - 1 : QLEN, :]
        step_wide = expand(step)
        stepped = (act * step_wide).astype(BF)
        row_cum = rowpack[0, b]
        parts = []
        upper_sum = None
        lower_sum = None
        for pair in range(PER // 2):
            lanes = slice(pair * LANES, (pair + 1) * LANES)
            grad_pair = grad_low[:, lanes]
            tops, lows, grads = [], [], []
            for k in range(2):
                h = 2 * pair + k
                col = cum[:, h : h + 1]
                row = row_cum[h : h + 1, :]
                e00 = jnp.exp(jnp.minimum(row[:, :HALF] - col[:HALF], 0.0))
                e01 = jnp.exp(row[:, HALF:] - col[:HALF])
                e11 = jnp.exp(jnp.minimum(row[:, HALF:] - col[HALF:], 0.0))
                value = stepped[:, lanes] * masks[k]
                upper = dot(value[:HALF], grad_pair, 1, 1) * jnp.concatenate([e00, e01], axis=1)
                lower = dot(value[HALF:], grad_pair[HALF:], 1, 1) * e11
                upper_sum = upper if upper_sum is None else upper_sum + upper
                lower_sum = lower if lower_sum is None else lower_sum + lower
                tops.append((gram_t[b, :HALF, :HALF] * e00).astype(BF))
                tops.append((gram_t[b, :HALF, HALF:] * e01).astype(BF))
                lows.append((gram_t[b, HALF:, HALF:] * e11).astype(BF))
                grads.append(grad_pair * masks[k])
            top = dot(jnp.concatenate(tops, axis=1), jnp.concatenate(grads, axis=0))
            low = dot(
                jnp.concatenate(lows, axis=1),
                jnp.concatenate([g[HALF:] for g in grads], axis=0),
            )
            parts.append(jnp.concatenate([top, low], axis=0))
        gram_grad[b, :HALF, :] += upper_sum
        gram_grad[b, HALF:, HALF:] += lower_sum
        mixed = jnp.concatenate(parts, axis=1)
        between = out_ref[span, :] - act * skip[...]
        flows = stepped.astype(F32) * mixed
        grad_value = step_wide * mixed + skip[...] * grad
        held = entry[b]
        across_low = (grad * expand(jnp.exp(cum))).astype(BF)
        c_grad[span, :] += dot(across_low, held.astype(BF))
        totals = split_dot(grad * between, chooser[1])
        if not final:
            states = carry[...]
            states_low = states.astype(BF)
            weights = expand(jnp.exp(last - cum) * step)
            pulled = dot(b_ref[span, :], states_low, 1, 1) * weights
            grad_value = grad_value + pulled
            weighted = act * pulled
            scaled = (act * weights).astype(BF)
            b_grad[span, :] += dot(scaled, states_low)
            totals = totals + split_dot(flows + weighted, chooser[0])
            totals = totals + split_dot(weighted, chooser[2])
            passed = head_rows(jnp.exp(last)) * states
            spread = passed * held
            high = spread.astype(BF)
            rest = (spread - high.astype(F32)).astype(BF)
            summed = dot(ones, high, 1, 1) + dot(ones, rest, 1, 1)
            last_sum = split_dot(summed, chooser[3])
            totals = totals + jnp.where(final_row, last_sum[0:1, :], 0.0)
        else:
            totals = totals + split_dot(flows, chooser[0])
        stats[0, span, :] = totals[:, : 4 * PER]
        if b > 0:
            fresh = dot(across_low, c_ref[span, :], 0, 0)
            carry[...] = keep[b] * (fresh if final else fresh + passed)
        if b > 0:
            ext[0:8, :] = pre_ref[b * QLEN - 16 : b * QLEN, :].astype(F32)[8:, :] * keep[b]
        else:
            ext[0:8, :] = jnp.zeros((8, TILE), F32)
        ext[8 : 8 + QLEN, :] = pre_ref[span, :].astype(F32)
        slope = grad_value * slope_ref[span, :].astype(F32)
        for lag in range(KERNEL):
            tap_sums[KERNEL - 1 - lag] = tap_sums[KERNEL - 1 - lag] + jnp.sum(
                slope * ext[8 - lag : 8 - lag + QLEN, :], axis=0, keepdims=True
            )
        if final:
            tail[QLEN : QLEN + 8, :] = jnp.zeros((8, TILE), F32)
        else:
            tail[QLEN : QLEN + 8, :] = tail[0:8, :] * keep[b + 1]
        tail[0:QLEN, :] = slope
        pulled_back = taps[KERNEL - 1 : KERNEL, :] * slope
        for lag in range(1, KERNEL):
            pulled_back = (
                pulled_back
                + taps[KERNEL - 1 - lag : KERNEL - lag, :] * tail[lag : lag + QLEN, :]
            )
        grad_pre[span, :] = pulled_back.astype(BF)
    taps_grad[...] = jnp.concatenate(tap_sums, axis=0)
    emit_outer(place, dot(feat_t[...], grad_pre[...]), outs)


def side_body(
    blocks,
    tiles_total,
    aliased,
    place,
    keep,
    feat_hbm,
    gram_grad,
    b_grad,
    c_grad,
    b_ref,
    c_ref,
    shared,
    taps,
    cols,
    decay,
    *refs,
):
    stats = refs[:tiles_total]
    outs = refs[tiles_total + 1 + aliased : -10]
    out, taps_grad, sums, ext, tail, feat_t, first, second, feat_sem, sems = refs[-10:]
    loading = pltpu.make_async_copy(feat_hbm, feat_t, feat_sem)
    loading.start()
    lower = iota((QLEN, QLEN), 0) >= iota((QLEN, QLEN), 1)
    upper = iota((QLEN, QLEN), 0) <= iota((QLEN, QLEN), 1)
    final_row = iota((QLEN, LANES), 0) == QLEN - 1
    rate = jnp.exp(decay[...])
    tap_sums = [jnp.zeros((1, TILE), F32) for _ in range(KERNEL)]
    decay_sum = jnp.zeros((1, LANES), F32)
    bias_sum = jnp.zeros((1, LANES), F32)
    tiles = sum(part.shape[0] for part in stats)
    padding = jnp.zeros((QLEN, LANES - PER * tiles), F32)
    for b in reversed(range(blocks)):
        span = slice(b * QLEN, (b + 1) * QLEN)
        final = b == blocks - 1
        gathered = [
            jnp.concatenate(
                [
                    part[j, span, PER * q : PER * q + PER]
                    for part in stats
                    for j in range(part.shape[0])
                ]
                + [padding],
                axis=1,
            )
            for q in range(4)
        ]
        pulled = gathered[0]
        grad_cum = gathered[1] - pulled + gathered[3]
        grad_cum = grad_cum + jnp.where(
            final_row, jnp.sum(gathered[2], axis=0, keepdims=True), 0.0
        )
        grad_log = dot(upper.astype(F32), grad_cum, precision=HIGH)
        raw = cols[0, span, :]
        step = cols[1, span, :]
        sigma = jax.nn.sigmoid(raw)
        ratio = jnp.where(raw < -20.0, 1.0, sigma / jnp.maximum(step, 1e-30))
        grad_raw = pulled * ratio - rate * grad_log * sigma
        decay_sum = decay_sum + jnp.sum(grad_log * cols[2, span, :], axis=0, keepdims=True)
        bias_sum = bias_sum + jnp.sum(grad_raw, axis=0, keepdims=True)
        out[span, TILE:] = grad_raw.astype(BF)
        gram_low = jnp.where(upper, gram_grad[b], 0.0).astype(BF)
        b_total = b_grad[span, :] + dot(gram_low, c_ref[span, :])
        c_total = c_grad[span, :] + dot(gram_low, b_ref[span, :], 0, 0)
        grad_act = jnp.concatenate([b_total, c_total], axis=1)
        if b > 0:
            ext[0:8, :] = shared[b * QLEN - 8 : b * QLEN, :] * keep[b]
        else:
            ext[0:8, :] = jnp.zeros((8, TILE), F32)
        ext[8 : 8 + QLEN, :] = shared[span, :]
        conv = conv_sum(ext, taps)
        slope = grad_act * silu_slope(jax.nn.sigmoid(conv), conv)
        for lag in range(KERNEL):
            tap_sums[KERNEL - 1 - lag] = tap_sums[KERNEL - 1 - lag] + jnp.sum(
                slope * ext[8 - lag : 8 - lag + QLEN, :], axis=0, keepdims=True
            )
        if final:
            tail[QLEN : QLEN + 8, :] = jnp.zeros((8, TILE), F32)
        else:
            tail[QLEN : QLEN + 8, :] = tail[0:8, :] * keep[b + 1]
        tail[0:QLEN, :] = slope
        pulled_back = taps[KERNEL - 1 : KERNEL, :] * slope
        for lag in range(1, KERNEL):
            pulled_back = (
                pulled_back
                + taps[KERNEL - 1 - lag : KERNEL - lag, :] * tail[lag : lag + QLEN, :]
            )
        out[span, :TILE] = pulled_back.astype(BF)
    taps_grad[...] = jnp.concatenate(tap_sums, axis=0)
    sums[...] = jnp.concatenate([decay_sum, bias_sum], axis=0)
    loading.wait()
    held = (first, second)[: len(outs)]
    emit_outer(place, dot(feat_t[...], out[...]), held)
    moves = []
    for i, (target, source) in enumerate(zip(outs, held)):
        start = target.shape[-1] - SIDE
        view = target.at[..., pl.ds(start, SIDE)]
        moves.append(pltpu.make_async_copy(source, view, sems.at[i]))
    for move in moves:
        move.start()
    for move in moves:
        move.wait()


def emit_outer(place, total, outs):
    if len(outs) == 1:
        outs[0][...] = total.astype(outs[0].dtype)
        return
    mine, send = outs
    low = total.astype(BF).reshape(mine.shape[0], 2, mine.shape[1], total.shape[1])

    @pl.when(place[0] == 0)
    def _():
        mine[...] = low[:, 0]
        send[...] = low[:, 1]

    @pl.when(place[0] == 1)
    def _():
        mine[...] = low[:, 1]
        send[...] = low[:, 0]


def outer_body(place, left, right, *outs):
    emit_outer(place, dot(left[...], right[...]), outs)


def back_body(place, grads, weights, out):
    out[...] = dot(grads[...], weights[...], 1, 1).astype(out.dtype)


def input_body(mine, got, hidden, cot, gain, out):
    total = (mine[...] + got[...].astype(F32)) * gain[...]
    rows = hidden[...].astype(F32)
    inverse = lax.rsqrt(jnp.mean(rows * rows, axis=1, keepdims=True) + EPSILON)
    hat = rows * inverse
    spread = jnp.mean(total * hat, axis=1, keepdims=True)
    out[...] = (cot[...].astype(F32) + (total - hat * spread) * inverse).astype(BF)


def out_body(mine, got, hidden, live, out):
    out[...] = (
        hidden[...].astype(F32) + live[...] * (mine[...] + got[...].astype(F32))
    ).astype(BF)


class Links:
    def __init__(self, devices, shard_rows):
        self.devices = devices
        self.height = shard_rows
        self.paired = devices % 4 == 0 and shard_rows % 16 == 0
        self.ring = max(devices // 4, 1)
        spot = lax.axis_index("dp")
        self.a, self.b, self.c = spot // 4, (spot // 2) % 2, spot % 2
        self.spot = spot

    def moved(self, rule):
        pairs = []
        for a in range(self.ring):
            for b in range(2):
                for c in range(2):
                    ta, tb, tc = rule(a, b, c)
                    pairs.append(((a * 2 + b) * 2 + c, (ta * 2 + tb) * 2 + tc))
        return pairs

    def over_core(self, x):
        return lax.ppermute(x, "dp", self.moved(lambda a, b, c: (a, b, 1 - c)))

    def over_pair(self, x):
        return lax.ppermute(x, "dp", self.moved(lambda a, b, c: (a, 1 - b, c)))

    def over_ring(self, x, k):
        return lax.ppermute(x, "dp", self.moved(lambda a, b, c: ((a + k) % self.ring, b, c)))

    def gather_fast(self, shard):
        if not self.paired:
            return [lax.all_gather(shard, "dp", axis=0, tiled=True)[None]], (shard,)
        near = [k for k in range(1, self.ring) if k in (1, self.ring - 1)]
        far = [k for k in range(1, self.ring) if k not in near]
        held = {0: shard}
        other = {0: self.over_pair(shard)}
        for k in near:
            held[k] = self.over_ring(shard, k)
        later = tied(shard, other[0], *[held[k] for k in near])
        for k in far:
            held[k] = self.over_ring(later, k)
        for k in near + far:
            other[k] = self.over_pair(held[k])
        pieces = [held[k] for k in range(self.ring)] + [other[k] for k in range(self.ring)]
        pieces = pieces + [self.over_core(x) for x in pieces]
        return [x[None] for x in pieces], (held[(near + far)[-1]], other[near[0]])

    def ring_parts(self, shard):
        if not self.paired:
            return [shard]
        return [shard] + [self.over_ring(shard, k) for k in range(1, self.ring)]

    def ring_stack(self, parts, *deps):
        if not self.paired:
            return parts[0]
        return jnp.stack(parts[:-1] + [tied(parts[-1], *deps)])

    def gather_rest(self, held, *deps):
        if not self.paired:
            return [lax.all_gather(held, "dp", axis=0, tiled=True)[None]]
        other = tied(self.over_pair(held), *deps)
        return [held, other, self.over_core(held), self.over_core(other)]

    def ring_halves(self, parts):
        if not self.paired:
            return [parts[0]]
        cut = max(self.ring // 2, 1)
        return [jnp.stack(parts[:cut])] + ([jnp.stack(parts[cut:])] if parts[cut:] else [])

    def pair_halves(self, halves):
        return [self.over_pair(h) for h in halves] if self.paired else []

    def join_halves(self, halves, others):
        if not self.paired:
            return [lax.all_gather(halves[0], "dp", axis=0, tiled=True)[None]]
        pieces = halves + others
        return pieces + [self.over_core(x) for x in pieces]

    def starts(self):
        if not self.paired:
            return jnp.zeros((1,), jnp.int32)
        rows = []
        for c in (self.c, 1 - self.c):
            for b in (self.b, 1 - self.b):
                for k in range(self.ring):
                    a = lax.rem(self.a - k + self.ring, self.ring)
                    rows.append(((a * 2 + b) * 2 + c) * self.height)
        return jnp.stack(rows).astype(jnp.int32)

    def scatter_core(self, parts, *deps):
        if not self.paired:
            return parts
        mine, send = parts
        send = tied(send, *deps) if deps else send
        shape = (self.ring, 2) + mine.shape[1:]
        got = self.over_core(send)
        mine, got = mine.reshape(shape), got.reshape(shape)
        away = self.pick(mine, 1 - self.b, 1).astype(F32) + self.pick(got, 1 - self.b, 1).astype(F32)
        return [away.astype(BF), mine, got]

    def pick(self, x, i, dim):
        return lax.dynamic_index_in_dim(x, i, dim, keepdims=False)

    def scatter_pair(self, parts, *deps):
        if not self.paired:
            return parts
        away, mine, got = parts
        near = tied(self.over_pair(away), *deps) if deps else self.over_pair(away)

        total = self.pick(mine, self.b, 1).astype(F32) + self.pick(got, self.b, 1).astype(F32)
        return [(total + near.astype(F32)).astype(BF)]

    def over_rings(self, x):
        groups = [
            [(a * 2 + b) * 2 + c for a in range(self.ring)] for b in range(2) for c in range(2)
        ]
        return lax.all_to_all(x, "dp", 0, 0, tiled=True, axis_index_groups=groups)

    def scatter_ring(self, parts, *deps):
        if not self.paired:
            return lax.psum_scatter(parts[0], "dp", scatter_dimension=0, tiled=True)
        moved = self.over_rings(parts[0])
        if deps:
            moved = tied(moved, *deps)
        return jnp.sum(moved.astype(F32), axis=0)

    def reduce(self, x, first, second):
        if not self.paired:
            return lax.psum(x, "dp")
        x = tied(x + self.over_core(x), first)
        x = tied(x + self.over_pair(x), second)
        total = x
        for k in range(1, self.ring):
            total = total + self.over_ring(x, k)
        return total


def over_tensor(x):
    return lax.ppermute(x, "tensor", [(0, 1), (1, 0)])


def on_device(
    hidden_in,
    segment,
    norm_gain,
    in_gate,
    in_value,
    in_shared,
    in_step,
    value_taps,
    shared_taps,
    step_bias,
    decay_log,
    skip_gain,
    gate_gain,
    out_proj,
    cotangent,
    devices,
):
    half_rows, width = hidden_in.shape
    rows = segment.shape[0]
    blocks = rows // QLEN
    half_blocks = half_rows // QLEN
    wide = in_value.shape[1]
    tiles = wide // TILE
    heads = step_bias.shape[0]
    height = in_value.shape[0]
    links = Links(devices, height)
    tensor = lax.axis_index("tensor")
    place = jnp.reshape(tensor, (1,)).astype(jnp.int32)
    core = jnp.reshape(links.c, (1,)).astype(jnp.int32)

    firsts = segment[::QLEN]
    keep = jnp.concatenate(
        [jnp.zeros((1,), F32), (firsts[1:] == firsts[:-1]).astype(F32)]
    )
    live = (segment >= 0).astype(F32)[:, None]
    live_own = lax.dynamic_slice_in_dim(live, tensor * half_rows, half_rows)
    pad = SIDE - 2 * STATE - heads - 1
    value_shard = jnp.concatenate(
        [in_value, in_shared, in_step, norm_gain[:, None], jnp.zeros((height, pad), BF)], axis=1
    )
    hidden_got = over_tensor(hidden_in)
    starts = links.starts()
    value_pieces, value_last = links.gather_fast(value_shard)
    gate_shard = tied(in_gate, *value_last)
    gate_ring = links.ring_parts(gate_shard)
    cot_sent = tied(cotangent, hidden_got)
    cot_got = over_tensor(cot_sent)

    bias_row = jnp.pad(step_bias, (0, LANES - heads)).reshape(1, LANES)
    decay_row = jnp.pad(decay_log, (0, LANES - heads)).reshape(1, LANES)
    skip_row = jnp.repeat(skip_gain, HEAD_DIM).reshape(1, wide)
    gate_row = gate_gain.reshape(1, wide)

    block_rows = lambda n: pl.BlockSpec((QLEN, n), lambda b, *_: (b, 0))
    half_spec = pl.BlockSpec((QLEN, width), lambda b, *_: (b % half_blocks, 0))
    (
        feat,
        feat_t,
        shared,
        b_low,
        c_low,
        gram,
        gram_t,
        cols,
        pack,
        rowpack,
        all_w,
        gain_row,
    ) = call(
        functools.partial(norm_body, half_blocks, len(value_pieces), 2 * STATE + heads),
        (blocks,),
        [
            smem(),
            smem(),
            smem(),
            half_spec,
            half_spec,
            whole((KERNEL, TILE)),
            whole((1, LANES)),
            whole((1, LANES)),
        ]
        + [
            pl.BlockSpec(p.shape[:2] + (SIDE,), lambda b: (0, 0, wide // SIDE))
            for p in value_pieces
        ],
        [
            block_rows(width),
            pl.BlockSpec((width, QLEN), lambda b: (0, b)),
            block_rows(TILE),
            block_rows(STATE),
            block_rows(STATE),
            pl.BlockSpec((1, QLEN, QLEN), lambda b: (b, 0, 0)),
            pl.BlockSpec((1, QLEN, QLEN), lambda b: (b, 0, 0)),
            pl.BlockSpec((3, QLEN, LANES), lambda b: (0, b, 0)),
            pl.BlockSpec((tiles, QLEN, 2 * PER), lambda b: (0, b, 0)),
            pl.BlockSpec((tiles, 1, 2 * PER, QLEN), lambda b: (0, b, 0, 0)),
            pl.BlockSpec((width, SIDE), lambda b: (0, 2 * wide // SIDE)),
            whole((1, width)),
        ],
        [
            ((rows, width), BF),
            ((width, rows), BF),
            ((rows, TILE), F32),
            ((rows, STATE), BF),
            ((rows, STATE), BF),
            ((blocks, QLEN, QLEN), F32),
            ((blocks, QLEN, QLEN), F32),
            ((3, rows, LANES), F32),
            ((tiles, rows, 2 * PER), F32),
            ((tiles, blocks, 2 * PER, QLEN), F32),
            ((width, 2 * wide + SIDE), BF),
            ((1, width), F32),
        ],
        [pltpu.VMEM((QLEN, width), F32), pltpu.VMEM((QLEN + 8, TILE), F32)],
        2 * rows * width * SIDE,
        20 * rows * width,
        starts,
        place,
        keep,
        hidden_in,
        hidden_got,
        shared_taps,
        bias_row,
        decay_row,
        *value_pieces,
        deps=(gate_shard, cot_sent),
    )

    def tile_cols(n, first=0):
        return pl.BlockSpec((n, TILE), lambda j: (0, j + first))

    def pack_spec(first):
        return pl.BlockSpec((1, rows, 2 * PER), lambda j: (j + first, 0, 0))

    def rowpack_spec(first):
        return pl.BlockSpec((1, blocks, 2 * PER, QLEN), lambda j: (j + first, 0, 0, 0))

    def entry_spec(first):
        return pl.BlockSpec((blocks, TILE, STATE), lambda j: (0, j + first, 0))

    def piece_tiles(pieces, first=0):
        return [
            pl.BlockSpec(p.shape[:2] + (TILE,), lambda j: (0, 0, j + first)) for p in pieces
        ]

    def value_part(first, count, past, deps):
        anywhere = [pl.BlockSpec(memory_space=pl.ANY)] * len(past)
        at = 3 + len(value_pieces) + 7
        return call(
            functools.partial(value_body, len(value_pieces), blocks, len(past)),
            (count,),
            [smem(), smem(), whole((rows, width))]
            + piece_tiles(value_pieces, first)
            + [
                tile_cols(KERNEL, first),
                tile_cols(1, first),
                pack_spec(first),
                rowpack_spec(first),
                whole((rows, STATE)),
                whole((rows, STATE)),
                whole((blocks, QLEN, QLEN)),
            ]
            + anywhere,
            [tile_cols(n, first) for n in (width, rows, rows, rows, rows)] + [entry_spec(first)],
            [
                ((width, 2 * wide + SIDE), BF),
                ((rows, wide), BF),
                ((rows, wide), BF),
                ((rows, wide), BF),
                ((rows, wide), F32),
                ((blocks, wide, STATE), F32),
            ],
            [
                pltpu.VMEM((QLEN, TILE), F32),
                pltpu.VMEM((QLEN + 8, TILE), F32),
                pltpu.VMEM((TILE, STATE), F32),
            ],
            4 * rows * width * count * TILE,
            20 * rows * count * TILE,
            starts,
            keep,
            feat,
            *value_pieces,
            value_taps,
            skip_row,
            pack,
            rowpack,
            b_low,
            c_low,
            gram,
            *past,
            deps=deps,
            aliases={at + i: i for i in range(len(past))},
        )

    cut = tiles // 3
    scanned = value_part(0, cut, (all_w,), ())
    gate_held = links.ring_stack(gate_ring, scanned[2])
    proj_shard = tied(out_proj.T, gate_held)
    proj_ring = links.ring_parts(proj_shard)
    scanned = value_part(cut, tiles - cut, scanned, (gate_held, proj_shard))
    all_w, pre_low, act_low, slope_low, out_rows, entry = scanned
    gate_pieces = links.gather_rest(gate_held, act_low, cot_got, *proj_ring[1:])
    proj_halves = links.ring_halves(proj_ring)
    proj_others = links.pair_halves(proj_halves)

    grad, grad_t = call(
        functools.partial(mask_body, half_blocks),
        (blocks,),
        [smem(), half_spec, half_spec, block_rows(1)],
        [block_rows(width), pl.BlockSpec((width, QLEN), lambda b: (0, b))],
        [((rows, width), BF), ((width, rows), BF)],
        [],
        rows * width,
        8 * rows * width,
        place,
        cotangent,
        cot_got,
        live.astype(BF),
        deps=(entry,),
    )

    broad = wide // WIDE_TILE

    def broad_cols(n, first=0):
        return pl.BlockSpec((n, WIDE_TILE), lambda j: (0, j + first))

    all_w, gate, squares = call(
        functools.partial(gate_body, len(gate_pieces)),
        (broad,),
        [smem(), whole((rows, width))]
        + [pl.BlockSpec(p.shape[:2] + (WIDE_TILE,), lambda j: (0, 0, j)) for p in gate_pieces]
        + [broad_cols(rows), pl.BlockSpec(memory_space=pl.ANY)],
        [broad_cols(width, broad), broad_cols(rows), whole((rows, LANES))],
        [((width, 2 * wide + SIDE), BF), ((rows, wide), BF), ((rows, LANES), F32)],
        [],
        2 * rows * width * wide,
        12 * rows * wide,
        starts,
        feat,
        *gate_pieces,
        out_rows,
        all_w,
        aliases={3 + len(gate_pieces): 0},
    )
    square_sum = jnp.sum(squares, axis=1).reshape(8, rows // 8)
    square_sum = square_sum + over_tensor(tied(square_sum, *proj_others[:1]))
    scale = lax.rsqrt(square_sum / INNER + EPSILON).reshape(rows, 1)

    def outer_outs(columns, step, first=0, paired=links.paired, kind=F32):
        if paired:
            spec = pl.BlockSpec((devices // 2, height, step), lambda j: (0, 0, j + first))
            return [spec] * 2, [((devices // 2, height, columns), BF)] * 2
        spec = pl.BlockSpec((width, step), lambda j: (0, j + first))
        return [spec], [((width, columns), kind)]

    both_kind = BF if links.paired else F32
    specs, outs = outer_outs(2 * wide, WIDE_TILE, 0, False, both_kind)
    gated, both_parts = call(
        proj_body,
        (broad,),
        [
            smem(),
            whole((width, rows)),
            broad_cols(rows),
            broad_cols(rows),
            whole((rows, 1)),
            broad_cols(1),
        ],
        [broad_cols(rows)] + specs,
        [((rows, wide), BF)] + outs,
        [],
        2 * rows * width * wide,
        14 * rows * wide,
        core,
        grad_t,
        out_rows,
        gate,
        scale,
        gate_row,
    )
    proj_others = [tied(x, gated) for x in proj_others]
    proj_pieces = links.join_halves(proj_halves, proj_others)

    def swapped(s, place_ref):
        return ((s // half_blocks + 1 - place_ref[0]) % 2) * half_blocks + s % half_blocks

    def swap_rows(n):
        return pl.BlockSpec((QLEN, n), lambda s, p, r: (swapped(s, p), 0))

    proj_w, branch_send, branch_own, row_dot = call(
        functools.partial(branch_body, len(proj_pieces)),
        (blocks,),
        [swap_rows(wide), swap_rows(width)] + [whole(p.shape) for p in proj_pieces],
        [
            whole((width, wide)),
            pl.BlockSpec((QLEN, width), lambda s, p, r: (jnp.minimum(s, half_blocks - 1), 0)),
            pl.BlockSpec((QLEN, width), lambda s, p, r: (jnp.maximum(s - half_blocks, 0), 0)),
            swap_rows(1),
        ],
        [
            ((width, wide), BF),
            ((half_rows, width), BF),
            ((half_rows, width), F32),
            ((rows, 1), F32),
        ],
        [],
        2 * rows * width * wide,
        8 * rows * wide,
        place,
        starts,
        gated,
        grad,
        *proj_pieces,
        prefetch=2,
    )
    row_total = row_dot.reshape(8, rows // 8)
    row_total = (row_total + over_tensor(row_total)).reshape(rows, 1)
    branch_got = over_tensor(branch_send)

    specs, outs = outer_outs(2 * wide, WIDE_TILE, broad, False, both_kind)
    core_grad, all_grad, channel_sums, both_parts = call(
        gating_body,
        (broad,),
        [
            smem(),
            whole((rows, width)),
            broad_cols(width),
            broad_cols(rows),
            broad_cols(rows),
            broad_cols(rows),
            whole((rows, 1)),
            whole((rows, 1)),
            broad_cols(1),
            whole((width, rows)),
            pl.BlockSpec(memory_space=pl.ANY),
        ],
        [broad_cols(rows), broad_cols(rows, broad), broad_cols(2)] + specs,
        [((rows, wide), BF), ((rows, 2 * wide + SIDE), BF), ((2, wide), F32)] + outs,
        [],
        4 * rows * width * wide,
        14 * rows * wide,
        core,
        grad,
        proj_w,
        out_rows,
        gate,
        act_low,
        scale,
        row_total,
        gate_row,
        feat_t,
        both_parts,
        aliases={10: 3},
    )
    both_sum = lax.psum_scatter(both_parts, "dp", scatter_dimension=0, tiled=True).astype(F32)
    proj_sum, gate_sum = both_sum[:, :wide], both_sum[:, wide:]

    def scan_part(first, count, past, grads, parts, columns, deps):
        summed = [whole((blocks, QLEN, QLEN)), whole((rows, STATE)), whole((rows, STATE))]
        specs, outs = outer_outs(columns, TILE, 0 if not parts else first)
        anywhere = [pl.BlockSpec(memory_space=pl.ANY)] * (1 + len(parts))
        at = 16 + len(past)
        return call(
            functools.partial(scan_body, blocks, bool(past), len(specs)),
            (count,),
            [smem(), smem(), whole((width, rows))]
            + [tile_cols(n, first) for n in (rows, rows, rows, rows, rows, 1, KERNEL)]
            + [
                pack_spec(first),
                rowpack_spec(first),
                whole((rows, STATE)),
                whole((rows, STATE)),
                whole((blocks, QLEN, QLEN)),
                entry_spec(first),
            ]
            + (summed if past else [])
            + anywhere,
            specs
            + [tile_cols(rows, first), tile_cols(KERNEL)]
            + summed
            + [pl.BlockSpec((1, rows, 4 * PER), lambda j: (j, 0, 0))],
            outs
            + [
                ((rows, 2 * wide + SIDE), BF),
                ((KERNEL, count * TILE), F32),
                ((blocks, QLEN, QLEN), F32),
                ((rows, STATE), F32),
                ((rows, STATE), F32),
                ((count, rows, 4 * PER), F32),
            ],
            [
                pltpu.VMEM((QLEN + 8, TILE), F32),
                pltpu.VMEM((QLEN + 8, TILE), F32),
                pltpu.VMEM((TILE, STATE), F32),
            ],
            6 * rows * width * count * TILE,
            20 * rows * count * TILE,
            core,
            keep,
            feat_t,
            slope_low,
            core_grad,
            act_low,
            pre_low,
            out_rows,
            skip_row,
            value_taps,
            pack,
            rowpack,
            b_low,
            c_low,
            gram_t,
            entry,
            *past,
            grads,
            *parts,
            deps=deps,
            aliases={at: len(specs), **{at + 1 + i: i for i in range(len(parts))}},
        )

    third = -(-tiles // 3)
    early_columns = 2 * third * TILE
    late_columns = wide - early_columns + SIDE
    *early_parts, all_grad, taps_a, gram_grad, b_grad, c_grad, stats_a = scan_part(
        0, third, (), all_grad, (), early_columns, ()
    )
    *early_parts, all_grad, taps_b, gram_grad, b_grad, c_grad, stats_b = scan_part(
        third,
        third,
        (gram_grad, b_grad, c_grad),
        all_grad,
        early_parts,
        early_columns,
        (),
    )
    early_parts = links.scatter_core(early_parts)
    block_out = call(
        out_body,
        (half_blocks,),
        [block_rows(width)] * 3 + [block_rows(1)],
        [block_rows(width)],
        [((half_rows, width), BF)],
        [],
        half_rows * width,
        10 * half_rows * width,
        branch_own,
        branch_got,
        hidden_in,
        live_own,
        deps=(taps_b,),
    )[0]
    *late_parts, all_grad, taps_c, gram_grad, b_grad, c_grad, stats_c = scan_part(
        2 * third,
        tiles - 2 * third,
        (gram_grad, b_grad, c_grad),
        all_grad,
        (),
        late_columns,
        (early_parts[0], block_out),
    )
    early_parts = links.scatter_pair(early_parts)
    taps_part = jnp.concatenate([taps_a, taps_b, taps_c], axis=1)
    stats = [stats_a, stats_b, stats_c]

    anywhere = pl.BlockSpec(memory_space=pl.ANY)
    held_shape = (devices // 2, height, SIDE) if links.paired else (width, SIDE)
    held_kind = BF if links.paired else F32
    at = 12 + len(stats)
    *late_parts, all_grad, sharetaps_part, head_sums = call(
        functools.partial(side_body, blocks, len(stats), len(late_parts)),
        (1,),
        [
            smem(),
            smem(),
            anywhere,
            whole((blocks, QLEN, QLEN)),
            whole((rows, STATE)),
            whole((rows, STATE)),
            whole((rows, STATE)),
            whole((rows, STATE)),
            whole((rows, TILE)),
            whole((KERNEL, TILE)),
            whole((3, rows, LANES)),
            whole((1, LANES)),
        ]
        + [whole(part.shape) for part in stats]
        + [anywhere] * (1 + len(late_parts)),
        [anywhere] * len(late_parts)
        + [
            pl.BlockSpec((rows, SIDE), lambda b: (0, 2 * wide // SIDE)),
            whole((KERNEL, TILE)),
            whole((2, LANES)),
        ],
        [(part.shape, part.dtype) for part in late_parts]
        + [((rows, 2 * wide + SIDE), BF), ((KERNEL, TILE), F32), ((2, LANES), F32)],
        [
            pltpu.VMEM((QLEN + 8, TILE), F32),
            pltpu.VMEM((QLEN + 8, TILE), F32),
            pltpu.VMEM((width, rows), BF),
            pltpu.VMEM(held_shape, held_kind),
            pltpu.VMEM(held_shape, held_kind),
            pltpu.SemaphoreType.DMA,
            pltpu.SemaphoreType.DMA((2,)),
        ],
        3 * rows * width * STATE,
        20 * rows * TILE,
        core,
        keep,
        feat_t,
        gram_grad,
        b_grad,
        c_grad,
        b_low,
        c_low,
        shared,
        shared_taps,
        cols,
        decay_row,
        *stats,
        all_grad,
        *late_parts,
        deps=(early_parts[0],),
        aliases={at: len(late_parts), **{at + 1 + i: i for i in range(len(late_parts))}},
    )

    def back(other, kind, deps=()):
        full = 2 * wide + SIDE

        def at(j, p):
            return ((1 - p[0]) if other else p[0], 0)

        return call(
            back_body,
            (width // WIDE_TILE,),
            [
                pl.BlockSpec((half_rows, full), at),
                pl.BlockSpec((WIDE_TILE, full), lambda j, p: (j, 0)),
            ],
            [pl.BlockSpec((half_rows, WIDE_TILE), lambda j, p: (0, j))],
            [((half_rows, width), kind)],
            [],
            2 * rows * width * wide,
            16 * rows * wide,
            place,
            all_grad,
            all_w,
            deps=deps,
            prefetch=1,
        )[0]

    late_parts = links.scatter_core(late_parts, early_parts[0])
    back_send = back(True, BF)
    early_sum = links.scatter_ring(early_parts, back_send)
    back_got = over_tensor(back_send)
    back_own = back(False, F32, (late_parts[0],))
    late_parts = links.scatter_pair(late_parts, back_own)
    input_grad = call(
        input_body,
        (half_blocks,),
        [block_rows(width)] * 4 + [whole((1, width))],
        [block_rows(width)],
        [((half_rows, width), BF)],
        [],
        half_rows * width,
        12 * half_rows * width,
        back_own,
        back_got,
        hidden_in,
        cotangent,
        gain_row,
    )[0]
    late_sum = links.scatter_ring(late_parts, input_grad)

    head_row = jnp.concatenate(
        [
            sharetaps_part.reshape(-1),
            head_sums[0, :heads],
            head_sums[1, :heads],
            jnp.sum(channel_sums[1].reshape(heads, HEAD_DIM), axis=1),
            jnp.zeros((wide - KERNEL * TILE - 3 * heads,), F32),
        ]
    ).reshape(1, wide)
    small = jnp.concatenate([taps_part, channel_sums[0:1], head_row], axis=0)
    small = links.reduce(small, back_send, back_own)
    sharetaps = small[5:6, : KERNEL * TILE]
    sharetaps = sharetaps + over_tensor(sharetaps)

    rest = wide - early_columns
    value_sum = jnp.concatenate([early_sum, late_sum[:, :rest]], axis=1)
    side_sum = late_sum[:, rest : rest + 2 * STATE + heads]
    side_shard = jnp.concatenate([in_shared, in_step], axis=1)
    norm_part = (
        jnp.sum(gate_sum * in_gate.astype(F32), axis=1, keepdims=True)
        + jnp.sum(value_sum * in_value.astype(F32), axis=1, keepdims=True)
        + jnp.sum(side_sum * side_shard.astype(F32), axis=1, keepdims=True)
    ) / norm_gain.astype(F32)[:, None]
    mixed = jnp.concatenate(
        [late_sum[:, rest : rest + 2 * STATE], jnp.broadcast_to(norm_part, (height, LANES))], axis=1
    )
    mixed = mixed + over_tensor(mixed)

    share = KERNEL * TILE
    return (
        block_out,
        input_grad,
        mixed[:, 2 * STATE],
        gate_sum,
        value_sum,
        mixed[:, : 2 * STATE],
        side_sum[:, 2 * STATE :],
        small[0:KERNEL],
        sharetaps.reshape(KERNEL, TILE),
        small[5, share + heads : share + 2 * heads],
        small[5, share : share + heads],
        small[5, share + 2 * heads : share + 3 * heads],
        small[4],
        proj_sum.T,
    )


def solution(mesh):
    in_specs = (
        P(("dp", "tensor"), None),
        P("dp"),
        P("dp"),
        P("dp", "tensor"),
        P("dp", "tensor"),
        P("dp", None),
        P("dp", "tensor"),
        P(None, "tensor"),
        P(),
        P("tensor"),
        P("tensor"),
        P("tensor"),
        P("tensor"),
        P("tensor", "dp"),
        P(("dp", "tensor"), None),
    )
    out_specs = (
        P(("dp", "tensor"), None),
        P(("dp", "tensor"), None),
        P("dp"),
        P("dp", "tensor"),
        P("dp", "tensor"),
        P("dp", None),
        P("dp", "tensor"),
        P(None, "tensor"),
        P(),
        P("tensor"),
        P("tensor"),
        P("tensor"),
        P("tensor"),
        P("tensor", "dp"),
    )
    return jax.shard_map(
        functools.partial(on_device, devices=mesh.shape["dp"]),
        mesh=mesh,
        in_specs=in_specs,
        out_specs=out_specs,
        check_vma=False,
    )
```

profile of v0, /device:TPU:0, one launch (start us, length us, event | category | flops | bytes accessed | tf_op | source)
XLA Modules:
  0.0 385.4 jit_solution(18381357939653062549)
XLA Ops:
  8.2 2.9 collective-permute-start
  12.7 1.1 concatenate.28
  13.8 1.6 collective-permute-start.2
  15.5 2.2 collective-permute-start.4
  17.7 1.5 collective-permute-start.3
  19.3 8.0 %collective-permute-done.2.refs_2_ = bf16[96,1920]{1,0:T(8,128)(2,1)S(1)} collective-permute-done((bf16[96,1920]{1,0:T(8,128)(2,1)S(1)}, bf16[96,1920]{1,0:T(8,128)(2,1)S(1)}, u32[]{:S(2)}, u32[]{:S(2)}) %collective-permute-start.2) | collective-permute-done | bytes 368672 | tf_op jit(solution)/shard_map/ppermute | solution.py:752
  27.2 5.9 %collective-permute-done.4.refs_3_ = bf16[96,1920]{1,0:T(8,128)(2,1)S(1)} collective-permute-done((bf16[96,1920]{1,0:T(8,128)(2,1)S(1)}, bf16[96,1920]{1,0:T(8,128)(2,1)S(1)}, u32[]{:S(2)}, u32[]{:S(2)}) %collective-permute-start.4) | collective-permute-done | bytes 368672 | tf_op jit(solution)/shard_map/ppermute | solution.py:752
  33.9 1.4 collective-permute-start.5
  35.3 1.5 collective-permute-start.6
  37.3 15.3 %collective-permute-done.5.refs_1_ = bf16[96,1920]{1,0:T(8,128)(2,1)S(1)} collective-permute-done((bf16[96,1920]{1,0:T(8,128)(2,1)S(1)}, bf16[96,1920]{1,0:T(8,128)(2,1)S(1)}, u32[]{:S(2)}, u32[]{:S(2)}) %collective-permute-start.5) | collective-permute-done | bytes 368672 | tf_op jit(solution)/shard_map/ppermute | solution.py:752
  52.7 1.6 collective-permute-start.7
  55.3 1.1 copy.127.refs_0_
  57.5 6.3 %collective-permute-done.7 = bf16[96,1920]{1,0:T(8,128)(2,1)} collective-permute-done((bf16[96,1920]{1,0:T(8,128)(2,1)S(1)}, bf16[96,1920]{1,0:T(8,128)(2,1)}, u32[]{:S(2)}, u32[]{:S(2)}) %collective-permute-start.7) | collective-permute-done | bytes 368672 | tf_op jit(solution)/shard_map/ppermute | solution.py:749
  64.5 1.5 collective-permute-start.19
  67.7 12.6 %shard_map.257 = (bf16[1024,1536]{1,0:T(8,128)(2,1)}, bf16[1536,1024]{1,0:T(8,128)(2,1)}, f32[1024,256]{1,0:T(8,128)}, bf16[1024,128]{1,0:T(8,128)(2,1)S(1)}, bf...) custom-call(s32[16]{0:T(128)S(1)} %stack.100.refs_0_.refs_1_, ...), custom_call_target="tpu_custom_call" | custom-call | flops 3623878656 | bytes 31457280 | tf_op jit(solution)/shard_map/pallas_call | solution.py:78
  80.3 12.7 %shard_map.258 = (bf16[1536,3456]{1,0:T(8,128)(2,1)}, bf16[1024,1536]{1,0:T(8,128)(2,1)}, bf16[1024,1536]{1,0:T(8,128)(2,1)}, bf16[1024,1536]{1,0:T(8,128)(2,1)}...) custom-call(s32[16]{0:T(128)S(1)} %stack.100.refs_0_.refs_1_, ...), custom_call_target="tpu_custom_call", output_to_operand_aliasing={{0}: (26, {})} | custom-call | flops 9663676416 | bytes 10485760 | tf_op jit(solution)/shard_map/pallas_call | solution.py:78
  94.1 1.2 pad_maximum_fusion.refs_1_.refs_32_.refs_2_
  95.2 2.8 collective-permute-start.22
  98.0 3.3 collective-permute-start.23
  101.5 1.6 collective-permute-start.20
  103.7 20.9 %shard_map.261 = (bf16[1536,3456]{1,0:T(8,128)(2,1)}, bf16[1024,1536]{1,0:T(8,128)(2,1)}, bf16[1024,1536]{1,0:T(8,128)(2,1)}, bf16[1024,1536]{1,0:T(8,128)(2,1)}...) custom-call(s32[16]{0:T(128)S(1)} %stack.100.refs_0_.refs_1_, ...), custom_call_target="tpu_custom_call", output_to_operand_aliasing={{0}: (26, {}), {1}: (27, {}), {2}: (28, {}), {3}: (29, {}),... | custom-call | flops 19327352832 | bytes 20971520 | tf_op jit(solution)/shard_map/pallas_call | solution.py:78
  124.7 3.6 collective-permute-done.20.refs_0_
  128.3 9.5 %collective-permute-done.1.refs_2_ = bf16[512,1536]{1,0:T(8,128)(2,1)S(1)} collective-permute-done((bf16[512,1536]{1,0:T(8,128)(2,1)S(1)}, bf16[512,1536]{1,0:T(8,128)(2,1)S(1)}, u32[]{:S(2)}, u32[]{:S(2)}) %collective-permute-start.1) | collective-permute-done | bytes 1572896 | tf_op jit(solution)/shard_map/ppermute | solution.py:863
  137.7 1.1 copy-done.15
  140.5 1.4 collective-permute-done.25.refs_5_
  142.0 1.1 copy-done.38
  143.0 12.1 %shard_map.264 = (bf16[1536,3456]{1,0:T(8,128)(2,1)}, bf16[1024,1536]{1,0:T(8,128)(2,1)}, f32[1024,128]{1,0:T(8,128)S(1)}) custom-call(s32[16]{0:T(128)S(1)} %stack.100.refs_0_.refs_1_, bf16[1024,1536]{1,0:T(8,128)(2,1)} %get-tuple-element.82.refs_2_.refs_1_, ...), custom_call_target="tpu_custom_call", output_to_operand_aliasing={{0}: (7, {})} | custom-call | flops 14495514624 | bytes 18874368 | tf_op jit(solution)/shard_map/pallas_call | solution.py:78
  157.8 5.9 %shard_map.262 = (bf16[1024,1536]{1,0:T(8,128)(2,1)}, bf16[1536,1024]{1,0:T(8,128)(2,1)}) custom-call(s32[1]{0:T(128)} %bitcast.refs_1_.refs_0_, bf16[512,1536]{1,0:T(8,128)(2,1)} %refs_3_.3, bf16[512,1536]{1,0:T(8,128)(2,1)} %copy-done.15, bf16[1024,1]{1,0:T(8,128)(2,1)S(1)} %convert_element_type.113.refs_3_, f32[4,1536,128]{2,1,0:T(8,128)} %get-tuple-element.95.refs_4_.refs_15_), custom_call_target="tpu_custom_call" | custom-call | flops 4718592 | bytes 12582912 | tf_op jit(solution)/shard_map/pallas_call | solution.py:78
  163.9 12.0 %shard_map.266 = (bf16[1024,1536]{1,0:T(8,128)(2,1)}, bf16[1536,3072]{1,0:T(8,128)(2,1)}) custom-call(s32[1]{0:T(128)} %bitcast.17.refs_0_, bf16[1536,1024]{1,0:T(8,128)(2,1)} %get-tuple-element.96.refs_1_, f32[1024,1536]{1,0:T(8,128)} %get-tuple-element.97.refs_6_.refs_2_.refs_3_.refs_7_, bf16[1024,1536]{1,0:T(8,128)(2,1)} %get-tuple-element.100.refs_3_.refs_4_, ...), custom_call_target="tpu_custom_call" | custom-call | flops 14495514624 | bytes 22020096 | tf_op jit(solution)/shard_map/pallas_call | solution.py:78
  176.8 1.2 collective-permute-done.32.refs_11_
  179.7 13.3 %shard_map.269 = (bf16[1536,1536]{1,0:T(8,128)(2,1)}, bf16[512,1536]{1,0:T(8,128)(2,1)}, f32[512,1536]{1,0:T(8,128)}, f32[1024,1]{1,0:T(8,128)S(1)}) custom-call(s32[1]{0:T(128)} %bitcast.refs_1_.refs_0_, s32[16]{0:T(128)S(1)} %stack.100.refs_0_.refs_1_, bf16[1024,1536]{1,0:T(8,128)(2,1)} %get-tuple-element.102.refs_1_.refs_2_, ...), custom_call_target="tpu_custom_call" | custom-call | flops 14495514624 | bytes 12582912 | tf_op jit(solution)/shard_map/pallas_call | solution.py:78
  193.2 1.6 collective-permute-start.34
  194.7 2.1 collective-permute-done.34
  196.8 1.0 copy.106.refs_7_
  197.9 21.0 %shard_map.270 = (bf16[1024,1536]{1,0:T(8,128)(2,1)}, bf16[1024,3456]{1,0:T(8,128)(2,1)}, f32[2,1536]{1,0:T(2,128)S(1)}, bf16[1536,3072]{1,0:T(8,128)(2,1)}) custom-call(s32[1]{0:T(128)} %bitcast.17.refs_0_, bf16[1024,1536]{1,0:T(8,128)(2,1)} %get-tuple-element.103.refs_3_.refs_1_, ...), custom_call_target="tpu_custom_call", output_to_operand_aliasing={{3}: (10, {})} | custom-call | flops 28991029248 | bytes 22020096 | tf_op jit(solution)/shard_map/pallas_call | solution.py:78
  218.9 1.6 collective-permute-start.33
  220.4 18.1 %shard_map.271 = (bf16[8,96,1024]{2,1,0:T(8,128)(2,1)}, bf16[8,96,1024]{2,1,0:T(8,128)(2,1)}, bf16[1024,3456]{1,0:T(8,128)(2,1)}, f32[4,512]{1,0:T(4,128)S(1)}, ...) custom-call(s32[1]{0:T(128)} %bitcast.17.refs_0_, ...), custom_call_target="tpu_custom_call", output_to_operand_aliasing={{2}: (16, {})} | custom-call | flops 14495514624 | bytes 10485760 | tf_op jit(solution)/shard_map/pallas_call | solution.py:78
  238.5 19.8 %shard_map.272 = (bf16[8,96,1024]{2,1,0:T(8,128)(2,1)}, bf16[8,96,1024]{2,1,0:T(8,128)(2,1)}, bf16[1024,3456]{1,0:T(8,128)(2,1)}, f32[4,512]{1,0:T(4,128)S(1)}, ...) custom-call(s32[1]{0:T(128)} %bitcast.17.refs_0_, ...), custom_call_target="tpu_custom_call", output_to_operand_aliasing={{2}: (19, {}), {0}: (20, {}), {1}: (21, {})} | custom-call | flops 14495514624 | bytes 10485760 | tf_op jit(solution)/shard_map/pallas_call | solution.py:78
  258.9 1.1 copy-done.18
  260.1 4.1 %shard_map.273.refs_21_ = bf16[512,1536]{1,0:T(8,128)(2,1)} custom-call(f32[512,1536]{1,0:T(8,128)} %get-tuple-element.104.refs_0_, bf16[512,1536]{1,0:T(8,128)(2,1)} %copy-done.18, bf16[512,1536]{1,0:T(8,128)(2,1)} %refs_2_.3, f32[512,1]{1,0:T(8,128)S(1)} %copy.107.refs_3_, f32[4,512]{1,0:T(4,128)S(1)} %get-tuple-element.121.refs_4_), custom_call_target="tpu_custom_call" | custom-call | flops 2359296 | bytes 7864320 | tf_op jit(solution)/shard_map/pallas_call | solution.py:78
  264.2 1.5 fusion.2.refs_20_
  265.7 1.6 collective-permute-start.36
  267.3 19.0 %shard_map.274 = (bf16[8,96,896]{2,1,0:T(8,128)(2,1)}, bf16[8,96,896]{2,1,0:T(8,128)(2,1)}, bf16[1024,3456]{1,0:T(8,128)(2,1)}, f32[4,512]{1,0:T(4,128)S(1)}, f3...) custom-call(s32[1]{0:T(128)} %bitcast.17.refs_0_, ...), custom_call_target="tpu_custom_call", output_to_operand_aliasing={{2}: (19, {})} | custom-call | flops 14495514624 | bytes 10485760 | tf_op jit(solution)/shard_map/pallas_call | solution.py:78
  286.2 2.5 fusion.refs_18_.refs_1_
  288.7 5.4 %all-to-all-start.1 = ((bf16[4,96,1024]{2,1,0:T(8,128)(2,1)}), bf16[4,96,1024]{2,1,0:T(8,128)(2,1)S(1)}, u32[]{:S(2)}, u32[]{:S(2)}) async-start(bf16[4,96,1024]{2,1,0:T(8,128)(2,1)} %fusion.refs_18_.refs_1_), calls=%async_computation.2 | async-start | bytes 1572864 | tf_op jit(solution)/shard_map/all_to_all | solution.py:841
  294.2 13.9 %shard_map.275 = (bf16[8,96,896]{2,1,0:T(8,128)(2,1)}, bf16[8,96,896]{2,1,0:T(8,128)(2,1)}, bf16[1024,3456]{1,0:T(8,128)(2,1)}, f32[4,256]{1,0:T(4,128)S(1)}, f32[2,128]{1,0:T(2,128)S(1)}) custom-call(s32[1]{0:T(128)} %bitcast.17.refs_0_, f32[4]{0:T(128)S(1)} %add_convert_fusion.2.refs_2_.refs_1_, ...), custom_call_target="tpu_custom_call", output_to_operand_aliasing={{2}: (15, {}), {0}: (16, {}), {1}: (17, {})} | custom-call | flops 1811939328 | bytes 5242880 | tf_op jit(solution)/shard_map/pallas_call | solution.py:78
  308.8 10.5 %shard_map.278.refs_1_ = bf16[512,1536]{1,0:T(8,128)(2,1)} custom-call(s32[1]{0:T(128)} %bitcast.refs_1_.refs_0_, bf16[1024,3456]{1,0:T(8,128)(2,1)} %get-tuple-element.139.refs_1_, bf16[1536,3456]{1,0:T(8,128)(2,1)} %get-tuple-element.140.refs_2_), custom_call_target="tpu_custom_call" | custom-call | flops 14495514624 | bytes 25165824 | tf_op jit(solution)/shard_map/pallas_call | solution.py:78
  319.3 2.1 collective-permute-start.42
  321.5 2.0 collective-permute-done.42
  323.5 1.3 copy-done.16
  324.8 1.3 fusion.3.refs_3_
  326.1 2.1 collective-permute-start.39
  328.2 10.7 %shard_map.277.refs_0_.refs_1_ = f32[512,1536]{1,0:T(8,128)} custom-call(s32[1]{0:T(128)} %bitcast.refs_1_.refs_0_, bf16[1024,3456]{1,0:T(8,128)(2,1)} %get-tuple-element.139.refs_1_, bf16[1536,3456]{1,0:T(8,128)(2,1)} %get-tuple-element.140.refs_2_, bf16[4,96,896]{2,1,0:T(8,128)(2,1)S(1)} %fusion.3.refs_3_), custom_call_target="tpu_custom_call" | custom-call | flops 14495514624 | bytes 25165824 | tf_op jit(solution)/shard_map/pallas_call | solution.py:78
  338.9 2.0 collective-permute-start.43
  340.9 2.3 collective-permute-start.44
  343.2 1.6 collective-permute-start.45
  344.8 2.2 fusion.1
  347.0 3.5 all-to-all-start
  352.7 5.2 %collective-permute-done.46 = f32[1,1024]{1,0:T(1,128)S(1)} collective-permute-done((f32[1,1024]{1,0:T(1,128)S(1)}, f32[1,1024]{1,0:T(1,128)S(1)}, u32[]{:S(2)}, u32[]{:S(2)}) %collective-permute-start.46) | collective-permute-done | bytes 4128 | tf_op jit(solution)/shard_map/ppermute | solution.py:863
  358.5 4.9 %shard_map.279.refs_1_ = bf16[512,1536]{1,0:T(8,128)(2,1)} custom-call(f32[512,1536]{1,0:T(8,128)} %shard_map.277.refs_0_.refs_1_, bf16[512,1536]{1,0:T(8,128)(2,1)} %collective-permute-done.38.refs_1_, bf16[512,1536]{1,0:T(8,128)(2,1)} %refs_2_.3, bf16[512,1536]{1,0:T(8,128)(2,1)} %refs_3_.3, f32[1,1536]{1,0:T(1,128)S(1)} %get-tuple-element.143.refs_4_), custom_call_target="tpu_custom_call" | custom-call | flops 2359296 | bytes 9437184 | tf_op jit(solution)/shard_map/pallas_call | solution.py:78
  363.4 4.0 %all-to-all-done.refs_0_ = bf16[4,96,896]{2,1,0:T(8,128)(2,1)S(1)} async-done(((bf16[4,96,896]{2,1,0:T(8,128)(2,1)}), bf16[4,96,896]{2,1,0:T(8,128)(2,1)S(1)}, u32[]{:S(2)}, u32[]{:S(2)}) %all-to-all-start) | async-done | bytes 688160 | tf_op jit(solution)/shard_map/all_to_all | solution.py:841
  368.4 1.0 multiply_reduce_fusion
  369.5 2.0 multiply_reduce_fusion.1
  372.6 4.2 %collective-permute-done.40 = f32[96,384]{1,0:T(8,128)S(1)} collective-permute-done((f32[96,384]{1,0:T(8,128)S(1)}, f32[96,384]{1,0:T(8,128)S(1)}, u32[]{:S(2)}, u32[]{:S(2)}) %collective-permute-start.40) | collective-permute-done | bytes 147488 | tf_op jit(solution)/shard_map/ppermute | solution.py:863
  (231 shorter events, 24.7 us)
Async XLA Ops:
  7.2 362.2 %reduce-scatter.2.cloned.1.call-start = ((), (), s32[]{:S(2)}) async-start(), calls=%async_computation.3 | async-start | bytes 10027008 | tf_op jit(solution)/shard_map/reduce_scatter | solution.py:1222
  8.2 55.6 %collective-permute-start = (bf16[512,1536]{1,0:T(8,128)(2,1)}, bf16[512,1536]{1,0:T(8,128)(2,1)}, u32[]{:S(2)}, u32[]{:S(2)}) collective-permute-start(bf16[512,1536]{1,0:T(8,128)(2,1)} %refs_2_.3), channel_id=1, source_target_pairs={{0,1},{1,0},{2,3},{3,2},{4,5},{5,4},{6,7},{7,6},{8,9},{9,8},{10,11... | collective-permute-start | bytes 4718600 | tf_op jit(solution)/shard_map/ppermute | solution.py:863
  13.8 41.4 %copy-start.20 = (bf16[96,1920]{1,0:T(8,128)(2,1)}, bf16[96,1920]{1,0:T(8,128)(2,1)S(1)}, u32[]{:S(2)}) copy-start(bf16[96,1920]{1,0:T(8,128)(2,1)S(1)} %concatenate.28) | copy-start | bytes 1105924
  13.8 41.4 %copy-start.32 = (s32[1024]{0:T(1024)S(1)}, s32[1024]{0:T(1024)}, u32[]{:S(2)}) copy-start(s32[1024]{0:T(1024)} %param.16) | copy-start | bytes 12292
  13.8 41.5 %copy-start.13 = (bf16[512,1536]{1,0:T(8,128)(2,1)S(1)}, bf16[512,1536]{1,0:T(8,128)(2,1)}, u32[]{:S(2)}) copy-start(bf16[512,1536]{1,0:T(8,128)(2,1)} %refs_3_.3) | copy-start | bytes 4718596
  13.8 13.4 %collective-permute-start.2 = (bf16[96,1920]{1,0:T(8,128)(2,1)S(1)}, bf16[96,1920]{1,0:T(8,128)(2,1)S(1)}, u32[]{:S(2)}, u32[]{:S(2)}) collective-permute-start(bf16[96,1920]{1,0:T(8,128)(2,1)S(1)} %concatenate.28), channel_id=1, source_target_pairs={{0,8},{2,10},{4,12},{6,14},{8,16},{10,18},{12,20},{14,22},{16,24},... | collective-permute-start | bytes 1105928 | tf_op jit(solution)/shard_map/ppermute | solution.py:752
  15.5 17.7 %collective-permute-start.4 = (bf16[96,1920]{1,0:T(8,128)(2,1)S(1)}, bf16[96,1920]{1,0:T(8,128)(2,1)S(1)}, u32[]{:S(2)}, u32[]{:S(2)}) collective-permute-start(bf16[96,1920]{1,0:T(8,128)(2,1)S(1)} %concatenate.28), channel_id=1, source_target_pairs={{0,24},{2,26},{4,28},{6,30},{8,0},{10,2},{12,4},{14,6},{16,8},{18,... | collective-permute-start | bytes 1105928 | tf_op jit(solution)/shard_map/ppermute | solution.py:752
  17.7 15.4 %collective-permute-start.3 = (bf16[96,1920]{1,0:T(8,128)(2,1)S(1)}, bf16[96,1920]{1,0:T(8,128)(2,1)S(1)}, u32[]{:S(2)}, u32[]{:S(2)}) collective-permute-start(bf16[96,1920]{1,0:T(8,128)(2,1)S(1)} %concatenate.28), channel_id=1, source_target_pairs={{0,4},{2,6},{4,0},{6,2},{8,12},{10,14},{12,8},{14,10},{16,20},{18,... | collective-permute-start | bytes 1105928 | tf_op jit(solution)/shard_map/ppermute | solution.py:749
  19.2 18.1 %collective-permute-start.9 = (bf16[96,1920]{1,0:T(8,128)(2,1)S(1)}, bf16[96,1920]{1,0:T(8,128)(2,1)S(1)}, u32[]{:S(2)}, u32[]{:S(2)}) collective-permute-start(bf16[96,1920]{1,0:T(8,128)(2,1)S(1)} %concatenate.28), channel_id=1, source_target_pairs={{0,2},{2,0},{4,6},{6,4},{8,10},{10,8},{12,14},{14,12},{16,18},{18,... | collective-permute-start | bytes 1105928 | tf_op jit(solution)/shard_map/ppermute | solution.py:746
  27.2 5.9 %copy-start.26 = (bf16[96,1920]{1,0:T(8,128)(2,1)}, bf16[96,1920]{1,0:T(8,128)(2,1)S(1)}, u32[]{:S(2)}) copy-start(bf16[96,1920]{1,0:T(8,128)(2,1)S(1)} %collective-permute-done.2.refs_2_) | copy-start | bytes 1105924
  33.9 22.9 %copy-start.6 = (bf16[96,1920]{1,0:T(8,128)(2,1)}, bf16[96,1920]{1,0:T(8,128)(2,1)S(1)}, u32[]{:S(2)}) copy-start(bf16[96,1920]{1,0:T(8,128)(2,1)S(1)} %collective-permute-done.3.refs_1_) | copy-start | bytes 1105924
  33.9 18.8 %collective-permute-start.5 = (bf16[96,1920]{1,0:T(8,128)(2,1)S(1)}, bf16[96,1920]{1,0:T(8,128)(2,1)S(1)}, u32[]{:S(2)}, u32[]{:S(2)}) collective-permute-start(bf16[96,1920]{1,0:T(8,128)(2,1)S(1)} %shard_map.255), channel_id=1, source_target_pairs={{0,16},{2,18},{4,20},{6,22},{8,24},{10,26},{12,28},{14,30},{16,0},... | collective-permute-start | bytes 1105928 | tf_op jit(solution)/shard_map/ppermute | solution.py:752
  35.3 17.4 %collective-permute-start.6 = (bf16[96,1920]{1,0:T(8,128)(2,1)}, bf16[96,1920]{1,0:T(8,128)(2,1)}, u32[]{:S(2)}, u32[]{:S(2)}) collective-permute-start(bf16[96,1920]{1,0:T(8,128)(2,1)} %copy-done.26), channel_id=1, source_target_pairs={{0,4},{2,6},{4,0},{6,2},{8,12},{10,14},{12,8},{14,10},{16,20},{18,... | collective-permute-start | bytes 1105928 | tf_op jit(solution)/shard_map/ppermute | solution.py:749
  36.8 19.9 %collective-permute-start.8 = (bf16[96,1920]{1,0:T(8,128)(2,1)}, bf16[96,1920]{1,0:T(8,128)(2,1)}, u32[]{:S(2)}, u32[]{:S(2)}) collective-permute-start(bf16[96,1920]{1,0:T(8,128)(2,1)} %copy-done.27), channel_id=1, source_target_pairs={{0,4},{2,6},{4,0},{6,2},{8,12},{10,14},{12,8},{14,10},{16,20},{18,... | collective-permute-start | bytes 1105928 | tf_op jit(solution)/shard_map/ppermute | solution.py:749
  37.3 15.3 %copy-start.41 = (bf16[96,1920]{1,0:T(8,128)(2,1)}, bf16[96,1920]{1,0:T(8,128)(2,1)S(1)}, u32[]{:S(2)}) copy-start(bf16[96,1920]{1,0:T(8,128)(2,1)S(1)} %collective-permute-done.9) | copy-start | bytes 1105924
  37.3 19.7 %collective-permute-start.10 = (bf16[96,1920]{1,0:T(8,128)(2,1)}, bf16[96,1920]{1,0:T(8,128)(2,1)}, u32[]{:S(2)}, u32[]{:S(2)}) collective-permute-start(bf16[96,1920]{1,0:T(8,128)(2,1)} %copy-done.26), channel_id=1, source_target_pairs={{0,2},{2,0},{4,6},{6,4},{8,10},{10,8},{12,14},{14,12},{16,18},{18,... | collective-permute-start | bytes 1105928 | tf_op jit(solution)/shard_map/ppermute | solution.py:746
  52.6 11.8 %copy-start.7 = (bf16[96,1920]{1,0:T(8,128)(2,1)}, bf16[96,1920]{1,0:T(8,128)(2,1)S(1)}, u32[]{:S(2)}) copy-start(bf16[96,1920]{1,0:T(8,128)(2,1)S(1)} %collective-permute-done.5.refs_1_) | copy-start | bytes 1105924
  52.6 4.7 %collective-permute-start.12 = (bf16[96,1920]{1,0:T(8,128)(2,1)}, bf16[96,1920]{1,0:T(8,128)(2,1)}, u32[]{:S(2)}, u32[]{:S(2)}) collective-permute-start(bf16[96,1920]{1,0:T(8,128)(2,1)} %copy-done.27), channel_id=1, source_target_pairs={{0,2},{2,0},{4,6},{6,4},{8,10},{10,8},{12,14},{14,12},{16,18},{18,... | collective-permute-start | bytes 1105928 | tf_op jit(solution)/shard_map/ppermute | solution.py:746
  52.7 11.1 %collective-permute-start.7 = (bf16[96,1920]{1,0:T(8,128)(2,1)S(1)}, bf16[96,1920]{1,0:T(8,128)(2,1)}, u32[]{:S(2)}, u32[]{:S(2)}) collective-permute-start(bf16[96,1920]{1,0:T(8,128)(2,1)S(1)} %collective-permute-done.5.refs_1_), channel_id=1, source_target_pairs={{0,4},{2,6},{4,0},{6,2},{8,12},{10,14},{12,8},{14,10},{16,20},{18,... | collective-permute-start | bytes 1105928 | tf_op jit(solution)/shard_map/ppermute | solution.py:749
  55.3 9.1 %copy-start.35 = (f32[24]{0:T(128)S(1)}, f32[24]{0:T(128)}, u32[]{:S(2)}) copy-start(f32[24]{0:T(128)} %param.25) | copy-start | bytes 292
  55.3 9.1 %copy-start.36 = (f32[24]{0:T(128)S(1)}, f32[24]{0:T(128)}, u32[]{:S(2)}) copy-start(f32[24]{0:T(128)} %param.24) | copy-start | bytes 292
  56.7 7.8 %collective-permute-start.13 = (bf16[96,1920]{1,0:T(8,128)(2,1)S(1)}, bf16[96,1920]{1,0:T(8,128)(2,1)S(1)}, u32[]{:S(2)}, u32[]{:S(2)}) collective-permute-start(bf16[96,1920]{1,0:T(8,128)(2,1)S(1)} %collective-permute-done.3.refs_1_), channel_id=1, source_target_pairs={{0,2},{2,0},{4,6},{6,4},{8,10},{10,8},{12,14},{14,12},{16,18},{18,... | collective-permute-start | bytes 1105928 | tf_op jit(solution)/shard_map/ppermute | solution.py:746
  57.0 9.1 %collective-permute-start.11 = (bf16[96,1920]{1,0:T(8,128)(2,1)S(1)}, bf16[96,1920]{1,0:T(8,128)(2,1)S(1)}, u32[]{:S(2)}, u32[]{:S(2)}) collective-permute-start(bf16[96,1920]{1,0:T(8,128)(2,1)S(1)} %collective-permute-done.5.refs_1_), channel_id=1, source_target_pairs={{0,2},{2,0},{4,6},{6,4},{8,10},{10,8},{12,14},{14,12},{16,18},{18,... | collective-permute-start | bytes 1105928 | tf_op jit(solution)/shard_map/ppermute | solution.py:746
  57.3 9.3 %collective-permute-start.14 = (bf16[96,1920]{1,0:T(8,128)(2,1)}, bf16[96,1920]{1,0:T(8,128)(2,1)S(1)}, u32[]{:S(2)}, u32[]{:S(2)}) collective-permute-start(bf16[96,1920]{1,0:T(8,128)(2,1)} %collective-permute-done.6.refs_2_), channel_id=1, source_target_pairs={{0,2},{2,0},{4,6},{6,4},{8,10},{10,8},{12,14},{14,12},{16,18},{18,... | collective-permute-start | bytes 1105928 | tf_op jit(solution)/shard_map/ppermute | solution.py:746
  63.8 3.0 collective-permute-start.16
  63.8 3.0 collective-permute-start.15
  64.5 28.5 %collective-permute-start.19 = (bf16[96,1536]{1,0:T(8,128)(2,1)S(1)}, bf16[96,1536]{1,0:T(8,128)(2,1)S(1)}, u32[]{:S(2)}, u32[]{:S(2)}) collective-permute-start(bf16[96,1536]{1,0:T(8,128)(2,1)S(1)} %shard_map.256.refs_24_), channel_id=1, source_target_pairs={{0,24},{2,26},{4,28},{6,30},{8,0},{10,2},{12,4},{14,6},{16,8},{18,... | collective-permute-start | bytes 884744 | tf_op jit(solution)/shard_map/ppermute | solution.py:752
  66.1 27.0 %collective-permute-start.17 = (bf16[96,1536]{1,0:T(8,128)(2,1)S(1)}, bf16[96,1536]{1,0:T(8,128)(2,1)S(1)}, u32[]{:S(2)}, u32[]{:S(2)}) collective-permute-start(bf16[96,1536]{1,0:T(8,128)(2,1)S(1)} %shard_map.256.refs_24_), channel_id=1, source_target_pairs={{0,8},{2,10},{4,12},{6,14},{8,16},{10,18},{12,20},{14,22},{16,24},... | collective-permute-start | bytes 884744 | tf_op jit(solution)/shard_map/ppermute | solution.py:752
  66.6 26.5 %collective-permute-start.18 = (bf16[96,1536]{1,0:T(8,128)(2,1)S(1)}, bf16[96,1536]{1,0:T(8,128)(2,1)S(1)}, u32[]{:S(2)}, u32[]{:S(2)}) collective-permute-start(bf16[96,1536]{1,0:T(8,128)(2,1)S(1)} %shard_map.256.refs_24_), channel_id=1, source_target_pairs={{0,16},{2,18},{4,20},{6,22},{8,24},{10,26},{12,28},{14,30},{16,0},... | collective-permute-start | bytes 884744 | tf_op jit(solution)/shard_map/ppermute | solution.py:752
  67.7 12.6 %copy-start.12 = (f32[4,1536]{1,0:T(4,128)S(1)}, f32[4,1536]{1,0:T(4,128)}, u32[]{:S(2)}) copy-start(f32[4,1536]{1,0:T(4,128)} %refs_9_.6) | copy-start | bytes 73732
  94.0 9.1 %copy-start.14 = (bf16[512,1536]{1,0:T(8,128)(2,1)S(1)}, bf16[512,1536]{1,0:T(8,128)(2,1)}, u32[]{:S(2)}) copy-start(bf16[512,1536]{1,0:T(8,128)(2,1)} %shard_map.254.refs_25_) | copy-start | bytes 4718596
  95.2 8.4 %copy-start.2 = (bf16[96,1536]{1,0:T(8,128)(2,1)}, bf16[96,1536]{1,0:T(8,128)(2,1)S(1)}, u32[]{:S(2)}) copy-start(bf16[96,1536]{1,0:T(8,128)(2,1)S(1)} %shard_map.260.refs_33_) | copy-start | bytes 884740
  95.2 29.3 %collective-permute-start.22 = (bf16[96,1536]{1,0:T(8,128)(2,1)S(1)}, bf16[96,1536]{1,0:T(8,128)(2,1)S(1)}, u32[]{:S(2)}, u32[]{:S(2)}) collective-permute-start(bf16[96,1536]{1,0:T(8,128)(2,1)S(1)} %shard_map.260.refs_33_), channel_id=1, source_target_pairs={{0,16},{2,18},{4,20},{6,22},{8,24},{10,26},{12,28},{14,30},{16,0},... | collective-permute-start | bytes 884744 | tf_op jit(solution)/shard_map/ppermute | solution.py:752
  98.0 26.6 %collective-permute-start.23 = (bf16[96,1536]{1,0:T(8,128)(2,1)S(1)}, bf16[96,1536]{1,0:T(8,128)(2,1)S(1)}, u32[]{:S(2)}, u32[]{:S(2)}) collective-permute-start(bf16[96,1536]{1,0:T(8,128)(2,1)S(1)} %shard_map.260.refs_33_), channel_id=1, source_target_pairs={{0,24},{2,26},{4,28},{6,30},{8,0},{10,2},{12,4},{14,6},{16,8},{18,... | collective-permute-start | bytes 884744 | tf_op jit(solution)/shard_map/ppermute | solution.py:752
  101.3 23.3 %collective-permute-start.21 = (bf16[96,1536]{1,0:T(8,128)(2,1)S(1)}, bf16[96,1536]{1,0:T(8,128)(2,1)S(1)}, u32[]{:S(2)}, u32[]{:S(2)}) collective-permute-start(bf16[96,1536]{1,0:T(8,128)(2,1)S(1)} %shard_map.260.refs_33_), channel_id=1, source_target_pairs={{0,8},{2,10},{4,12},{6,14},{8,16},{10,18},{12,20},{14,22},{16,24},... | collective-permute-start | bytes 884744 | tf_op jit(solution)/shard_map/ppermute | solution.py:752
  101.5 26.8 %collective-permute-start.20 = (bf16[4,96,1536]{2,1,0:T(8,128)(2,1)}, bf16[4,96,1536]{2,1,0:T(8,128)(2,1)S(1)}, u32[]{:S(2)}, u32[]{:S(2)}) collective-permute-start(bf16[4,96,1536]{2,1,0:T(8,128)(2,1)} %pad_maximum_fusion.refs_1_.refs_32_.refs_2_), channel_id=1, source_target_pairs={{0,4},{2,6},{4,0},{6,2},{8,12},{10,14},{12,8},{14,10},{16,20},{18,... | collective-permute-start | bytes 3538952 | tf_op jit(solution)/shard_map/ppermute | solution.py:749
  103.1 34.6 %collective-permute-start.1 = (bf16[512,1536]{1,0:T(8,128)(2,1)S(1)}, bf16[512,1536]{1,0:T(8,128)(2,1)S(1)}, u32[]{:S(2)}, u32[]{:S(2)}) collective-permute-start(bf16[512,1536]{1,0:T(8,128)(2,1)S(1)} %copy-done.14), channel_id=1, source_target_pairs={{0,1},{1,0},{2,3},{3,2},{4,5},{5,4},{6,7},{7,6},{8,9},{9,8},{10,11... | collective-permute-start | bytes 4718600 | tf_op jit(solution)/shard_map/ppermute | solution.py:863
  124.6 16.0 %collective-permute-start.24 = (bf16[4,96,1536]{2,1,0:T(8,128)(2,1)}, bf16[4,96,1536]{2,1,0:T(8,128)(2,1)S(1)}, u32[]{:S(2)}, u32[]{:S(2)}) collective-permute-start(bf16[4,96,1536]{2,1,0:T(8,128)(2,1)} %pad_maximum_fusion.refs_1_.refs_32_.refs_2_), channel_id=1, source_target_pairs={{0,2},{2,0},{4,6},{6,4},{8,10},{10,8},{12,14},{14,12},{16,18},{18,... | collective-permute-start | bytes 3538952 | tf_op jit(solution)/shard_map/ppermute | solution.py:746
  128.3 9.5 %copy-start.23 = (bf16[4,96,1536]{2,1,0:T(8,128)(2,1)}, bf16[4,96,1536]{2,1,0:T(8,128)(2,1)S(1)}, u32[]{:S(2)}) copy-start(bf16[4,96,1536]{2,1,0:T(8,128)(2,1)S(1)} %collective-permute-done.20.refs_0_) | copy-start | bytes 3538948
  138.9 3.1 collective-permute-start.25
  139.9 17.4 %copy-start.25 = (bf16[2,96,1536]{2,1,0:T(8,128)(2,1)}, bf16[2,96,1536]{2,1,0:T(8,128)(2,1)S(1)}, u32[]{:S(2)}) copy-start(bf16[2,96,1536]{2,1,0:T(8,128)(2,1)S(1)} %pad_maximum_fusion.1.refs_4_) | copy-start | bytes 1769476
  139.9 15.4 %collective-permute-start.26 = (bf16[2,96,1536]{2,1,0:T(8,128)(2,1)S(1)}, bf16[2,96,1536]{2,1,0:T(8,128)(2,1)S(1)}, u32[]{:S(2)}, u32[]{:S(2)}) collective-permute-start(bf16[2,96,1536]{2,1,0:T(8,128)(2,1)S(1)} %pad_maximum_fusion.1.refs_4_), channel_id=1, source_target_pairs={{0,4},{2,6},{4,0},{6,2},{8,12},{10,14},{12,8},{14,10},{16,20},{18,... | collective-permute-start | bytes 1769480 | tf_op jit(solution)/shard_map/ppermute | solution.py:749
  155.3 8.3 %collective-permute-start.27 = (f32[8,128]{1,0:T(8,128)S(1)}, f32[8,128]{1,0:T(8,128)S(1)}, u32[]{:S(2)}, u32[]{:S(2)}) collective-permute-start(f32[8,128]{1,0:T(8,128)S(1)} %shard_map.265), channel_id=1, source_target_pairs={{0,1},{1,0},{2,3},{3,2},{4,5},{5,4},{6,7},{7,6},{8,9},{9,8},{10,11... | collective-permute-start | bytes 12296 | tf_op jit(solution)/shard_map/ppermute | solution.py:863
  156.8 19.1 %collective-permute-start.28 = (bf16[2,96,1536]{2,1,0:T(8,128)(2,1)}, bf16[2,96,1536]{2,1,0:T(8,128)(2,1)S(1)}, u32[]{:S(2)}, u32[]{:S(2)}) collective-permute-start(bf16[2,96,1536]{2,1,0:T(8,128)(2,1)} %pad_maximum_fusion.2.refs_5_), channel_id=1, source_target_pairs={{0,4},{2,6},{4,0},{6,2},{8,12},{10,14},{12,8},{14,10},{16,20},{18,... | collective-permute-start | bytes 1769480 | tf_op jit(solution)/shard_map/ppermute | solution.py:749
  157.3 19.5 %collective-permute-start.30 = (bf16[2,96,1536]{2,1,0:T(8,128)(2,1)}, bf16[2,96,1536]{2,1,0:T(8,128)(2,1)}, u32[]{:S(2)}, u32[]{:S(2)}) collective-permute-start(bf16[2,96,1536]{2,1,0:T(8,128)(2,1)} %pad_maximum_fusion.2.refs_5_), channel_id=1, source_target_pairs={{0,2},{2,0},{4,6},{6,4},{8,10},{10,8},{12,14},{14,12},{16,18},{18,... | collective-permute-start | bytes 1769480 | tf_op jit(solution)/shard_map/ppermute | solution.py:746
  157.3 19.5 %collective-permute-start.29 = (bf16[2,96,1536]{2,1,0:T(8,128)(2,1)S(1)}, bf16[2,96,1536]{2,1,0:T(8,128)(2,1)}, u32[]{:S(2)}, u32[]{:S(2)}) collective-permute-start(bf16[2,96,1536]{2,1,0:T(8,128)(2,1)S(1)} %pad_maximum_fusion.1.refs_4_), channel_id=1, source_target_pairs={{0,2},{2,0},{4,6},{6,4},{8,10},{10,8},{12,14},{14,12},{16,18},{18,... | collective-permute-start | bytes 1769480 | tf_op jit(solution)/shard_map/ppermute | solution.py:746
  175.9 2.1 collective-permute-start.32
  176.7 2.1 collective-permute-start.31
  193.2 3.7 collective-permute-start.34
  218.9 40.0 %collective-permute-start.33 = (bf16[512,1536]{1,0:T(8,128)(2,1)}, bf16[512,1536]{1,0:T(8,128)(2,1)S(1)}, u32[]{:S(2)}, u32[]{:S(2)}) collective-permute-start(bf16[512,1536]{1,0:T(8,128)(2,1)} %get-tuple-element.105), channel_id=1, source_target_pairs={{0,1},{1,0},{2,3},{3,2},{4,5},{5,4},{6,7},{7,6},{8,9},{9,8},{10,11... | collective-permute-start | bytes 4718600 | tf_op jit(solution)/shard_map/ppermute | solution.py:863
  258.3 5.8 %collective-permute-start.35 = (bf16[8,96,1024]{2,1,0:T(8,128)(2,1)}, bf16[8,96,1024]{2,1,0:T(8,128)(2,1)}, u32[]{:S(2)}, u32[]{:S(2)}) collective-permute-start(bf16[8,96,1024]{2,1,0:T(8,128)(2,1)} %get-tuple-element.127), channel_id=1, source_target_pairs={{0,2},{2,0},{4,6},{6,4},{8,10},{10,8},{12,14},{14,12},{16,18},{18,... | collective-permute-start | bytes 4718600 | tf_op jit(solution)/shard_map/ppermute | solution.py:746
  265.7 20.6 %collective-permute-start.36 = (bf16[4,96,1024]{2,1,0:T(8,128)(2,1)S(1)}, bf16[4,96,1024]{2,1,0:T(8,128)(2,1)S(1)}, u32[]{:S(2)}, u32[]{:S(2)}) collective-permute-start(bf16[4,96,1024]{2,1,0:T(8,128)(2,1)S(1)} %fusion.2.refs_20_), channel_id=1, source_target_pairs={{0,4},{2,6},{4,0},{6,2},{8,12},{10,14},{12,8},{14,10},{16,20},{18,... | collective-permute-start | bytes 2359304 | tf_op jit(solution)/shard_map/ppermute | solution.py:749
  288.7 34.8 %all-to-all-start.1 = ((bf16[4,96,1024]{2,1,0:T(8,128)(2,1)}), bf16[4,96,1024]{2,1,0:T(8,128)(2,1)S(1)}, u32[]{:S(2)}, u32[]{:S(2)}) async-start(bf16[4,96,1024]{2,1,0:T(8,128)(2,1)} %fusion.refs_18_.refs_1_), calls=%async_computation.2 | async-start | bytes 1572864 | tf_op jit(solution)/shard_map/all_to_all | solution.py:841
  308.2 11.1 %collective-permute-start.41 = (f32[6,1536]{1,0:T(8,128)S(1)}, f32[6,1536]{1,0:T(8,128)S(1)}, u32[]{:S(2)}, u32[]{:S(2)}) collective-permute-start(f32[6,1536]{1,0:T(8,128)S(1)} %pad_maximum_fusion.5), channel_id=1, source_target_pairs={{0,2},{2,0},{4,6},{6,4},{8,10},{10,8},{12,14},{14,12},{16,18},{18,... | collective-permute-start | bytes 110600 | tf_op jit(solution)/shard_map/ppermute | solution.py:746
  308.3 15.2 %collective-permute-start.37 = (bf16[8,96,896]{2,1,0:T(8,128)(2,1)}, bf16[8,96,896]{2,1,0:T(8,128)(2,1)}, u32[]{:S(2)}, u32[]{:S(2)}) collective-permute-start(bf16[8,96,896]{2,1,0:T(8,128)(2,1)} %shard_map.276), channel_id=1, source_target_pairs={{0,2},{2,0},{4,6},{6,4},{8,10},{10,8},{12,14},{14,12},{16,18},{18,... | collective-permute-start | bytes 4128776 | tf_op jit(solution)/shard_map/ppermute | solution.py:746
  319.3 4.2 %collective-permute-start.42 = (f32[6,1536]{1,0:T(8,128)S(1)}, f32[6,1536]{1,0:T(8,128)S(1)}, u32[]{:S(2)}, u32[]{:S(2)}) collective-permute-start(f32[6,1536]{1,0:T(8,128)S(1)} %shard_map.283), channel_id=1, source_target_pairs={{0,4},{2,6},{4,0},{6,2},{8,12},{10,14},{12,8},{14,10},{16,20},{18,... | collective-permute-start | bytes 110600 | tf_op jit(solution)/shard_map/ppermute | solution.py:749
  321.4 37.1 %collective-permute-start.38 = (bf16[512,1536]{1,0:T(8,128)(2,1)}, bf16[512,1536]{1,0:T(8,128)(2,1)}, u32[]{:S(2)}, u32[]{:S(2)}) collective-permute-start(bf16[512,1536]{1,0:T(8,128)(2,1)} %shard_map.278.refs_1_), channel_id=1, source_target_pairs={{0,1},{1,0},{2,3},{3,2},{4,5},{5,4},{6,7},{7,6},{8,9},{9,8},{10,11... | collective-permute-start | bytes 4718600 | tf_op jit(solution)/shard_map/ppermute | solution.py:863
  326.1 18.7 %collective-permute-start.39 = (bf16[4,96,896]{2,1,0:T(8,128)(2,1)S(1)}, bf16[4,96,896]{2,1,0:T(8,128)(2,1)S(1)}, u32[]{:S(2)}, u32[]{:S(2)}) collective-permute-start(bf16[4,96,896]{2,1,0:T(8,128)(2,1)S(1)} %fusion.3.refs_3_), channel_id=1, source_target_pairs={{0,4},{2,6},{4,0},{6,2},{8,12},{10,14},{12,8},{14,10},{16,20},{18,... | collective-permute-start | bytes 2064392 | tf_op jit(solution)/shard_map/ppermute | solution.py:749
  338.9 11.7 %collective-permute-start.43 = (f32[6,1536]{1,0:T(8,128)S(1)}, f32[6,1536]{1,0:T(8,128)S(1)}, u32[]{:S(2)}, u32[]{:S(2)}) collective-permute-start(f32[6,1536]{1,0:T(8,128)S(1)} %shard_map.284), channel_id=1, source_target_pairs={{0,8},{2,10},{4,12},{6,14},{8,16},{10,18},{12,20},{14,22},{16,24},... | collective-permute-start | bytes 110600 | tf_op jit(solution)/shard_map/ppermute | solution.py:752
  340.9 9.8 %collective-permute-start.44 = (f32[6,1536]{1,0:T(8,128)S(1)}, f32[6,1536]{1,0:T(8,128)S(1)}, u32[]{:S(2)}, u32[]{:S(2)}) collective-permute-start(f32[6,1536]{1,0:T(8,128)S(1)} %shard_map.284), channel_id=1, source_target_pairs={{0,16},{2,18},{4,20},{6,22},{8,24},{10,26},{12,28},{14,30},{16,0},... | collective-permute-start | bytes 110600 | tf_op jit(solution)/shard_map/ppermute | solution.py:752
  343.2 7.4 %collective-permute-start.45 = (f32[6,1536]{1,0:T(8,128)S(1)}, f32[6,1536]{1,0:T(8,128)S(1)}, u32[]{:S(2)}, u32[]{:S(2)}) collective-permute-start(f32[6,1536]{1,0:T(8,128)S(1)} %shard_map.284), channel_id=1, source_target_pairs={{0,24},{2,26},{4,28},{6,30},{8,0},{10,2},{12,4},{14,6},{16,8},{18,... | collective-permute-start | bytes 110600 | tf_op jit(solution)/shard_map/ppermute | solution.py:752
  347.0 20.4 %all-to-all-start = ((bf16[4,96,896]{2,1,0:T(8,128)(2,1)}), bf16[4,96,896]{2,1,0:T(8,128)(2,1)S(1)}, u32[]{:S(2)}, u32[]{:S(2)}) async-start(bf16[4,96,896]{2,1,0:T(8,128)(2,1)} %fusion.1), calls=%async_computation | async-start | bytes 1376256 | tf_op jit(solution)/shard_map/all_to_all | solution.py:841
  350.7 7.2 %collective-permute-start.46 = (f32[1,1024]{1,0:T(1,128)S(1)}, f32[1,1024]{1,0:T(1,128)S(1)}, u32[]{:S(2)}, u32[]{:S(2)}) collective-permute-start(f32[1,1024]{1,0:T(1,128)S(1)} %slice.93), channel_id=1, source_target_pairs={{0,1},{1,0},{2,3},{3,2},{4,5},{5,4},{6,7},{7,6},{8,9},{9,8},{10,11... | collective-permute-start | bytes 12296 | tf_op jit(solution)/shard_map/ppermute | solution.py:863
  371.6 5.2 %collective-permute-start.40 = (f32[96,384]{1,0:T(8,128)S(1)}, f32[96,384]{1,0:T(8,128)S(1)}, u32[]{:S(2)}, u32[]{:S(2)}) collective-permute-start(f32[96,384]{1,0:T(8,128)S(1)} %pad_maximum_fusion.4), channel_id=1, source_target_pairs={{0,1},{1,0},{2,3},{3,2},{4,5},{5,4},{6,7},{7,6},{8,9},{9,8},{10,11... | collective-permute-start | bytes 442376 | tf_op jit(solution)/shard_map/ppermute | solution.py:863
  (33 other events, 58.7 us)
Sparse Core Ops, SparseCore 0:
  219.0 115.4 reduce-scatter.1
where the time goes:
time: 393 us; the launch traced here: 385 us
  Pallas kernels  211 us (54%)
  waiting for transfers between devices  69.7 us (18%)
  starting transfers between devices  52.2 us (13%)
  local copies, waits for them, and re-layouts  22.9 us (6%)
  between operations  15.3 us (4%)
  other arithmetic  13.7 us (3%)
    pallas_call x16, Pallas kernels, call(): pl.pallas_call(held, grid_spec=pltpu.PrefetchScalarGridSpec(num_scalar_pr...  211 us
    ppermute x12, waiting for transfers between devices, over_ring(): lax.ppermute(x, 'dp', self.moved(lambda a, b, c: ((a + k) % self.ring, b,...  29.2 us
    ppermute x8, waiting for transfers between devices, over_tensor(): return lax.ppermute(x, 'tensor', [(0, 1), (1, 0)])  21 us
    ppermute x12, starting transfers between devices, over_ring(): lax.ppermute(x, 'dp', self.moved(lambda a, b, c: ((a + k) % self.ring, b,...  19.7 us
    unnamed x102, local copies, waits for them, and re-layouts  14.2 us
    ppermute x10, starting transfers between devices, over_pair(): return lax.ppermute(x, 'dp', self.moved(lambda a, b, c: (a, 1 - b, c)))  13.6 us
    ppermute x10, waiting for transfers between devices, over_pair(): return lax.ppermute(x, 'dp', self.moved(lambda a, b, c: (a, 1 - b, c)))  12 us
    all_to_all x2, starting transfers between devices, over_rings(): return lax.all_to_all(x, 'dp', 0, 0, tiled=True, axis_index_groups=groups)  8.9 us
  transfers between devices with their start and end apart: 50, of which 14 were waited for; matrix products, arithmetic and copies ran while one was open for 5% of the time, Pallas kernels for 46%

commit v1 on v0

--- a/solution.py
+++ b/solution.py
@@ -800,15 +800,18 @@
         pieces = halves + others
         return pieces + [self.over_core(x) for x in pieces]
 
-    def starts(self):
+    def ring_gather(self, shard):
+        if not self.paired:
+            return shard
+        return self.over_rings(jnp.broadcast_to(shard[None], (self.ring,) + shard.shape))
+
+    def starts(self, rings):
         if not self.paired:
             return jnp.zeros((1,), jnp.int32)
         rows = []
         for c in (self.c, 1 - self.c):
             for b in (self.b, 1 - self.b):
-                for k in range(self.ring):
-                    a = lax.rem(self.a - k + self.ring, self.ring)
-                    rows.append(((a * 2 + b) * 2 + c) * self.height)
+                rows += [((a * 2 + b) * 2 + c) * self.height for a in rings]
         return jnp.stack(rows).astype(jnp.int32)
 
     def scatter_core(self, parts, *deps):
@@ -905,12 +908,13 @@
         [in_value, in_shared, in_step, norm_gain[:, None], jnp.zeros((height, pad), BF)], axis=1
     )
     hidden_got = over_tensor(hidden_in)
-    starts = links.starts()
+    ring = range(links.ring)
+    starts = links.starts([lax.rem(links.a - k + links.ring, links.ring) for k in ring])
+    ordered = links.starts(ring)
     value_pieces, value_last = links.gather_fast(value_shard)
     gate_shard = tied(in_gate, *value_last)
-    gate_ring = links.ring_parts(gate_shard)
-    cot_sent = tied(cotangent, hidden_got)
-    cot_got = over_tensor(cot_sent)
+    gate_ring = links.ring_gather(gate_shard)
+    cot_got = over_tensor(cotangent)
 
     bias_row = jnp.pad(step_bias, (0, LANES - heads)).reshape(1, LANES)
     decay_row = jnp.pad(decay_log, (0, LANES - heads)).reshape(1, LANES)
@@ -989,7 +993,7 @@
         bias_row,
         decay_row,
         *value_pieces,
-        deps=(gate_shard, cot_sent),
+        deps=(gate_shard,),
     )
 
     def tile_cols(n, first=0):
@@ -1061,7 +1065,7 @@
 
     cut = tiles // 3
     scanned = value_part(0, cut, (all_w,), ())
-    gate_held = links.ring_stack(gate_ring, scanned[2])
+    gate_held = tied(gate_ring, scanned[2])
     proj_shard = tied(out_proj.T, gate_held)
     proj_ring = links.ring_parts(proj_shard)
     scanned = value_part(cut, tiles - cut, scanned, (gate_held, proj_shard))
@@ -1102,7 +1106,7 @@
         [],
         2 * rows * width * wide,
         12 * rows * wide,
-        starts,
+        ordered,
         feat,
         *gate_pieces,
         out_rows,
@@ -1285,20 +1289,11 @@
             aliases={at: len(specs), **{at + 1 + i: i for i in range(len(parts))}},
         )
 
-    third = -(-tiles // 3)
-    early_columns = 2 * third * TILE
+    early = 2 * -(-tiles // 3)
+    early_columns = early * TILE
     late_columns = wide - early_columns + SIDE
     *early_parts, all_grad, taps_a, gram_grad, b_grad, c_grad, stats_a = scan_part(
-        0, third, (), all_grad, (), early_columns, ()
-    )
-    *early_parts, all_grad, taps_b, gram_grad, b_grad, c_grad, stats_b = scan_part(
-        third,
-        third,
-        (gram_grad, b_grad, c_grad),
-        all_grad,
-        early_parts,
-        early_columns,
-        (),
+        0, early, (), all_grad, (), early_columns, ()
     )
     early_parts = links.scatter_core(early_parts)
     block_out = call(
@@ -1314,11 +1309,11 @@
         branch_got,
         hidden_in,
         live_own,
-        deps=(taps_b,),
+        deps=(taps_a,),
     )[0]
     *late_parts, all_grad, taps_c, gram_grad, b_grad, c_grad, stats_c = scan_part(
-        2 * third,
-        tiles - 2 * third,
+        early,
+        tiles - early,
         (gram_grad, b_grad, c_grad),
         all_grad,
         (),
@@ -1326,8 +1321,8 @@
         (early_parts[0], block_out),
     )
     early_parts = links.scatter_pair(early_parts)
-    taps_part = jnp.concatenate([taps_a, taps_b, taps_c], axis=1)
-    stats = [stats_a, stats_b, stats_c]
+    taps_part = jnp.concatenate([taps_a, taps_c], axis=1)
+    stats = [stats_a, stats_c]
 
     anywhere = pl.BlockSpec(memory_space=pl.ANY)
     held_shape = (devices // 2, height, SIDE) if links.paired else (width, SIDE)
@@ -1448,7 +1443,7 @@
         ]
     ).reshape(1, wide)
     small = jnp.concatenate([taps_part, channel_sums[0:1], head_row], axis=0)
-    small = links.reduce(small, back_send, back_own)
+    small = links.reduce(small, back_send, late_parts[0])
     sharetaps = small[5:6, : KERNEL * TILE]
     sharetaps = sharetaps + over_tensor(sharetaps)
 

time: 393 us -> 379 us (0.964)
  Pallas kernels: 211 us -> 204 us
    ppermute x8, waiting for transfers between devices: 21 us -> 11 us  [over_tensor(): return lax.ppermute(x, 'tensor', [(0, 1), (1, 0)])]
    ppermute x10, waiting for transfers between devices: 12 us -> 19.6 us  [over_pair(): return lax.ppermute(x, 'dp', self.moved(lambda a, b, c: (a, 1 - b, c)))]
    pallas_call x16 -> x15, Pallas kernels: 211 us -> 204 us  [call(): pl.pallas_call(held, grid_spec=pltpu.PrefetchScalarGridSpec(num_scalar_pr...]
    ppermute x12 -> x9, starting transfers between devices: 19.7 us -> 15.1 us  [over_ring(): lax.ppermute(x, 'dp', self.moved(lambda a, b, c: ((a + k) % self.ring, b,...]
    ppermute x10, starting transfers between devices: 13.6 us -> 9.02 us  [over_pair(): return lax.ppermute(x, 'dp', self.moved(lambda a, b, c: (a, 1 - b, c)))]
    unnamed x102 -> x93, local copies, waits for them, and re-layouts: 14.2 us -> 9.92 us
    ppermute x8, starting transfers between devices: 7.46 us -> 11.5 us  [over_tensor(): return lax.ppermute(x, 'tensor', [(0, 1), (1, 0)])]
    all_to_all x2 -> x3, starting transfers between devices: 8.9 us -> 12.9 us  [over_rings(): return lax.all_to_all(x, 'dp', 0, 0, tiled=True, axis_index_groups=groups)]
  transfers between devices with their start and end apart: 50 -> 48, of which waited for: 14 -> 19; matrix products, arithmetic and copies ran while one was open for 5% -> 5% of each run, Pallas kernels for 46% -> 46%
where the time goes in v1:
time: 379 us; the launch traced here: 371 us
  Pallas kernels  204 us (54%)
  waiting for transfers between devices  67.9 us (18%)
  starting transfers between devices  51 us (13%)
  local copies, waits for them, and re-layouts  19.9 us (5%)
  between operations  15.4 us (4%)
  other arithmetic  13.4 us (4%)
    pallas_call x15, Pallas kernels, call(): pl.pallas_call(held, grid_spec=pltpu.PrefetchScalarGridSpec(num_scalar_pr...  204 us
    ppermute x9, waiting for transfers between devices, over_ring(): lax.ppermute(x, 'dp', self.moved(lambda a, b, c: ((a + k) % self.ring, b,...  29.2 us
    ppermute x10, waiting for transfers between devices, over_pair(): return lax.ppermute(x, 'dp', self.moved(lambda a, b, c: (a, 1 - b, c)))  19.6 us
    ppermute x9, starting transfers between devices, over_ring(): lax.ppermute(x, 'dp', self.moved(lambda a, b, c: ((a + k) % self.ring, b,...  15.1 us
    all_to_all x3, starting transfers between devices, over_rings(): return lax.all_to_all(x, 'dp', 0, 0, tiled=True, axis_index_groups=groups)  12.9 us
    ppermute x8, starting transfers between devices, over_tensor(): return lax.ppermute(x, 'tensor', [(0, 1), (1, 0)])  11.5 us
    ppermute x8, waiting for transfers between devices, over_tensor(): return lax.ppermute(x, 'tensor', [(0, 1), (1, 0)])  11 us
    unnamed x93, local copies, waits for them, and re-layouts  9.92 us
  transfers between devices with their start and end apart: 48, of which 19 were waited for; matrix products, arithmetic and copies ran while one was open for 5% of the time, Pallas kernels for 46%

profile of v1, /device:TPU:0, one launch (start us, length us, event | category | flops | bytes accessed | tf_op | source)
XLA Modules:
  0.0 371.3 jit_solution(11345784188683698314)
XLA Ops:
  8.1 2.9 collective-permute-start.1
  12.7 1.1 concatenate.28
  13.8 1.6 collective-permute-start.2
  15.4 2.2 collective-permute-start.4
  17.7 1.5 collective-permute-start.3
  19.2 8.0 %collective-permute-done.2.refs_2_ = bf16[96,1920]{1,0:T(8,128)(2,1)S(1)} collective-permute-done((bf16[96,1920]{1,0:T(8,128)(2,1)S(1)}, bf16[96,1920]{1,0:T(8,128)(2,1)S(1)}, u32[]{:S(2)}, u32[]{:S(2)}) %collective-permute-start.2) | collective-permute-done | bytes 368672 | tf_op jit(solution)/shard_map/ppermute | solution.py:752
  27.2 5.9 %collective-permute-done.4.refs_3_ = bf16[96,1920]{1,0:T(8,128)(2,1)S(1)} collective-permute-done((bf16[96,1920]{1,0:T(8,128)(2,1)S(1)}, bf16[96,1920]{1,0:T(8,128)(2,1)S(1)}, u32[]{:S(2)}, u32[]{:S(2)}) %collective-permute-start.4) | collective-permute-done | bytes 368672 | tf_op jit(solution)/shard_map/ppermute | solution.py:752
  33.8 1.4 collective-permute-start.5
  35.3 1.5 collective-permute-start.6
  37.3 15.3 %collective-permute-done.5.refs_1_ = bf16[96,1920]{1,0:T(8,128)(2,1)S(1)} collective-permute-done((bf16[96,1920]{1,0:T(8,128)(2,1)S(1)}, bf16[96,1920]{1,0:T(8,128)(2,1)S(1)}, u32[]{:S(2)}, u32[]{:S(2)}) %collective-permute-start.5) | collective-permute-done | bytes 368672 | tf_op jit(solution)/shard_map/ppermute | solution.py:752
  53.1 1.5 collective-permute-start.7
  54.8 1.1 broadcast_in_dim.95
  55.9 4.4 %all-to-all-start = ((bf16[4,96,1536]{2,1,0:T(8,128)(2,1)}), bf16[4,96,1536]{2,1,0:T(8,128)(2,1)}, u32[]{:S(2)}, u32[]{:S(2)}) async-start(bf16[4,96,1536]{2,1,0:T(8,128)(2,1)} %broadcast_in_dim.95), calls=%async_computation | async-start | bytes 2359296 | tf_op jit(solution)/shard_map/all_to_all | solution.py:844
  61.6 2.3 collective-permute-done.7
  64.7 1.1 collective-permute-done.15
  66.5 12.7 %shard_map.256 = (bf16[1024,1536]{1,0:T(8,128)(2,1)}, bf16[1536,1024]{1,0:T(8,128)(2,1)}, f32[1024,256]{1,0:T(8,128)}, bf16[1024,128]{1,0:T(8,128)(2,1)S(1)}, bf...) custom-call(s32[16]{0:T(128)S(1)} %stack.136.refs_0_.refs_1_, ...), custom_call_target="tpu_custom_call" | custom-call | flops 3623878656 | bytes 31457280 | tf_op jit(solution)/shard_map/pallas_call | solution.py:78
  79.3 12.6 %shard_map.257 = (bf16[1536,3456]{1,0:T(8,128)(2,1)}, bf16[1024,1536]{1,0:T(8,128)(2,1)}, bf16[1024,1536]{1,0:T(8,128)(2,1)}, bf16[1024,1536]{1,0:T(8,128)(2,1)}...) custom-call(s32[16]{0:T(128)S(1)} %stack.136.refs_0_.refs_1_, ...), custom_call_target="tpu_custom_call", output_to_operand_aliasing={{0}: (26, {})} | custom-call | flops 9663676416 | bytes 10485760 | tf_op jit(solution)/shard_map/pallas_call | solution.py:78
  91.9 1.5 collective-permute-start.19
  93.4 1.5 collective-permute-start.20
  94.9 1.0 collective-permute-start.18
  96.5 20.9 %shard_map.260 = (bf16[1536,3456]{1,0:T(8,128)(2,1)}, bf16[1024,1536]{1,0:T(8,128)(2,1)}, bf16[1024,1536]{1,0:T(8,128)(2,1)}, bf16[1024,1536]{1,0:T(8,128)(2,1)}...) custom-call(s32[16]{0:T(128)S(1)} %stack.136.refs_0_.refs_1_, ...), custom_call_target="tpu_custom_call", output_to_operand_aliasing={{0}: (26, {}), {1}: (27, {}), {2}: (28, {}), {3}: (29, {}),... | custom-call | flops 19327352832 | bytes 20971520 | tf_op jit(solution)/shard_map/pallas_call | solution.py:78
  117.6 5.7 %collective-permute-done.17.refs_0_ = bf16[4,96,1536]{2,1,0:T(8,128)(2,1)S(1)} collective-permute-done((bf16[4,96,1536]{2,1,0:T(8,128)(2,1)}, bf16[4,96,1536]{2,1,0:T(8,128)(2,1)S(1)}, u32[]{:S(2)}, u32[]{:S(2)}) %collective-permute-start.17) | collective-permute-done | bytes 1179680 | tf_op jit(solution)/shard_map/ppermute | solution.py:749
  123.3 1.0 copy-done.21
  125.1 6.0 %shard_map.261 = (bf16[1024,1536]{1,0:T(8,128)(2,1)}, bf16[1536,1024]{1,0:T(8,128)(2,1)}) custom-call(s32[1]{0:T(128)} %bitcast.refs_1_.refs_0_, bf16[512,1536]{1,0:T(8,128)(2,1)} %refs_3_.3, bf16[512,1536]{1,0:T(8,128)(2,1)} %collective-permute-done.refs_2_, bf16[1024,1]{1,0:T(8,128)(2,1)S(1)} %convert_element_type.113.refs_3_, ...), custom_call_target="tpu_custom_call" | custom-call | flops 4718592 | bytes 12582912 | tf_op jit(solution)/shard_map/pallas_call | solution.py:78
  132.6 12.0 %shard_map.263 = (bf16[1536,3456]{1,0:T(8,128)(2,1)}, bf16[1024,1536]{1,0:T(8,128)(2,1)}, f32[1024,128]{1,0:T(8,128)S(1)}) custom-call(s32[16]{0:T(128)S(1)} %stack.153.refs_0_, bf16[1024,1536]{1,0:T(8,128)(2,1)} %get-tuple-element.74.refs_2_.refs_1_, bf16[4,96,1536]{2,1,0:T(8,128)(2,1)} %shard_map.258.refs_1_.refs_32_.refs_2_, ...), custom_call_target="tpu_custom_call", output_to_operand_aliasing={{0}: (7, {})} | custom-call | flops 14495514624 | bytes 18874368 | tf_op jit(solution)/shard_map/pallas_call | solution.py:78
  144.8 2.6 collective-permute-done.23.refs_1_.refs_0_
  150.0 1.0 collective-permute-done.24
  151.3 12.0 %shard_map.265 = (bf16[1024,1536]{1,0:T(8,128)(2,1)}, bf16[1536,3072]{1,0:T(8,128)(2,1)}) custom-call(s32[1]{0:T(128)} %bitcast.17.refs_0_, bf16[1536,1024]{1,0:T(8,128)(2,1)} %get-tuple-element.88.refs_1_, f32[1024,1536]{1,0:T(8,128)} %get-tuple-element.89.refs_6_.refs_2_.refs_3_.refs_7_, bf16[1024,1536]{1,0:T(8,128)(2,1)} %get-tuple-element.92.refs_3_.refs_4_, ...), custom_call_target="tpu_custom_call" | custom-call | flops 14495514624 | bytes 22020096 | tf_op jit(solution)/shard_map/pallas_call | solution.py:78
  164.2 1.2 collective-permute-done.29.refs_11_
  167.0 13.3 %shard_map.268 = (bf16[1536,1536]{1,0:T(8,128)(2,1)}, bf16[512,1536]{1,0:T(8,128)(2,1)}, f32[512,1536]{1,0:T(8,128)}, f32[1024,1]{1,0:T(8,128)S(1)}) custom-call(s32[1]{0:T(128)} %bitcast.refs_1_.refs_0_, s32[16]{0:T(128)S(1)} %stack.136.refs_0_.refs_1_, bf16[1024,1536]{1,0:T(8,128)(2,1)} %get-tuple-element.94.refs_1_.refs_2_, ...), custom_call_target="tpu_custom_call" | custom-call | flops 14495514624 | bytes 12582912 | tf_op jit(solution)/shard_map/pallas_call | solution.py:78
  180.5 1.4 collective-permute-start.31
  182.0 2.2 collective-permute-done.31
  184.2 1.0 copy.102.refs_7_
  185.2 20.8 %shard_map.269 = (bf16[1024,1536]{1,0:T(8,128)(2,1)}, bf16[1024,3456]{1,0:T(8,128)(2,1)}, f32[2,1536]{1,0:T(2,128)S(1)}, bf16[1536,3072]{1,0:T(8,128)(2,1)}) custom-call(s32[1]{0:T(128)} %bitcast.17.refs_0_, bf16[1024,1536]{1,0:T(8,128)(2,1)} %get-tuple-element.95.refs_3_.refs_1_, ...), custom_call_target="tpu_custom_call", output_to_operand_aliasing={{3}: (10, {})} | custom-call | flops 28991029248 | bytes 22020096 | tf_op jit(solution)/shard_map/pallas_call | solution.py:78
  206.1 1.4 collective-permute-start.30
  207.5 30.7 %shard_map.270 = (bf16[8,96,1024]{2,1,0:T(8,128)(2,1)}, bf16[8,96,1024]{2,1,0:T(8,128)(2,1)}, bf16[1024,3456]{1,0:T(8,128)(2,1)}, f32[4,1024]{1,0:T(4,128)S(1)},...) custom-call(s32[1]{0:T(128)} %bitcast.17.refs_0_, ...), custom_call_target="tpu_custom_call", output_to_operand_aliasing={{2}: (16, {})} | custom-call | flops 28991029248 | bytes 20971520 | tf_op jit(solution)/shard_map/pallas_call | solution.py:78
  238.7 2.9 collective-permute-done.30.refs_1_
  241.6 1.2 copy-done.16
  242.8 4.1 %shard_map.271.refs_21_ = bf16[512,1536]{1,0:T(8,128)(2,1)} custom-call(f32[512,1536]{1,0:T(8,128)} %get-tuple-element.96.refs_0_, bf16[512,1536]{1,0:T(8,128)(2,1)} %copy-done.16, bf16[512,1536]{1,0:T(8,128)(2,1)} %refs_2_.3, f32[512,1]{1,0:T(8,128)S(1)} %copy.103.refs_3_, f32[4,1024]{1,0:T(4,128)S(1)} %get-tuple-element.107.refs_4_), custom_call_target="tpu_custom_call" | custom-call | flops 2359296 | bytes 7864320 | tf_op jit(solution)/shard_map/pallas_call | solution.py:78
  246.9 1.4 fusion.2.refs_20_
  249.3 19.0 %shard_map.272 = (bf16[8,96,896]{2,1,0:T(8,128)(2,1)}, bf16[8,96,896]{2,1,0:T(8,128)(2,1)}, bf16[1024,3456]{1,0:T(8,128)(2,1)}, f32[4,512]{1,0:T(4,128)S(1)}, f3...) custom-call(s32[1]{0:T(128)} %bitcast.17.refs_0_, ...), custom_call_target="tpu_custom_call", output_to_operand_aliasing={{2}: (19, {})} | custom-call | flops 14495514624 | bytes 10485760 | tf_op jit(solution)/shard_map/pallas_call | solution.py:78
  268.2 1.6 collective-permute-done.33
  269.8 2.4 fusion.refs_17_.refs_1_
  272.3 5.0 %all-to-all-start.2 = ((bf16[4,96,1024]{2,1,0:T(8,128)(2,1)}), bf16[4,96,1024]{2,1,0:T(8,128)(2,1)S(1)}, u32[]{:S(2)}, u32[]{:S(2)}) async-start(bf16[4,96,1024]{2,1,0:T(8,128)(2,1)} %fusion.refs_17_.refs_1_), calls=%async_computation.3 | async-start | bytes 1572864 | tf_op jit(solution)/shard_map/all_to_all | solution.py:844
  277.3 13.8 %shard_map.273 = (bf16[8,96,896]{2,1,0:T(8,128)(2,1)}, bf16[8,96,896]{2,1,0:T(8,128)(2,1)}, bf16[1024,3456]{1,0:T(8,128)(2,1)}, f32[4,256]{1,0:T(4,128)S(1)}, f32[2,128]{1,0:T(2,128)S(1)}) custom-call(s32[1]{0:T(128)} %bitcast.17.refs_0_, f32[4]{0:T(128)S(1)} %add_convert_fusion.2.refs_2_.refs_1_, ...), custom_call_target="tpu_custom_call", output_to_operand_aliasing={{2}: (14, {}), {0}: (15, {}), {1}: (16, {})} | custom-call | flops 1811939328 | bytes 5242880 | tf_op jit(solution)/shard_map/pallas_call | solution.py:78
  291.8 10.3 %shard_map.276.refs_1_ = bf16[512,1536]{1,0:T(8,128)(2,1)} custom-call(s32[1]{0:T(128)} %bitcast.refs_1_.refs_0_, bf16[1024,3456]{1,0:T(8,128)(2,1)} %get-tuple-element.124.refs_1_, bf16[1536,3456]{1,0:T(8,128)(2,1)} %get-tuple-element.125.refs_2_), custom_call_target="tpu_custom_call" | custom-call | flops 14495514624 | bytes 25165824 | tf_op jit(solution)/shard_map/pallas_call | solution.py:78
  302.8 1.5 collective-permute-start.35
  304.2 2.0 collective-permute-done.39
  306.3 1.3 copy-done.13
  307.7 1.3 fusion.3.refs_3_
  309.6 10.7 %shard_map.275.refs_0_.refs_1_ = f32[512,1536]{1,0:T(8,128)} custom-call(s32[1]{0:T(128)} %bitcast.refs_1_.refs_0_, bf16[1024,3456]{1,0:T(8,128)(2,1)} %get-tuple-element.124.refs_1_, bf16[1536,3456]{1,0:T(8,128)(2,1)} %get-tuple-element.125.refs_2_, bf16[4,96,896]{2,1,0:T(8,128)(2,1)S(1)} %fusion.3.refs_3_), custom_call_target="tpu_custom_call" | custom-call | flops 14495514624 | bytes 25165824 | tf_op jit(solution)/shard_map/pallas_call | solution.py:78
  320.3 5.4 %collective-permute-done.36.refs_0_ = bf16[4,96,896]{2,1,0:T(8,128)(2,1)S(1)} collective-permute-done((bf16[4,96,896]{2,1,0:T(8,128)(2,1)S(1)}, bf16[4,96,896]{2,1,0:T(8,128)(2,1)S(1)}, u32[]{:S(2)}, u32[]{:S(2)}) %collective-permute-start.36) | collective-permute-done | bytes 688160 | tf_op jit(solution)/shard_map/ppermute | solution.py:749
  325.7 2.2 fusion.1.refs_1_
  327.9 1.7 collective-permute-start.40
  329.6 2.8 collective-permute-start.41
  332.4 1.3 collective-permute-start.42
  333.7 3.5 all-to-all-start.1
  337.4 1.8 collective-permute-done.35.refs_1_
  339.2 4.9 %shard_map.277.refs_1_ = bf16[512,1536]{1,0:T(8,128)(2,1)} custom-call(f32[512,1536]{1,0:T(8,128)} %shard_map.275.refs_0_.refs_1_, bf16[512,1536]{1,0:T(8,128)(2,1)} %collective-permute-done.35.refs_1_, bf16[512,1536]{1,0:T(8,128)(2,1)} %refs_2_.3, bf16[512,1536]{1,0:T(8,128)(2,1)} %refs_3_.3, f32[1,1536]{1,0:T(1,128)S(1)} %get-tuple-element.128.refs_4_), custom_call_target="tpu_custom_call" | custom-call | flops 2359296 | bytes 9437184 | tf_op jit(solution)/shard_map/pallas_call | solution.py:78
  344.1 1.5 collective-permute-start.43
  348.4 4.9 %all-to-all-done.1.refs_0_ = bf16[4,96,896]{2,1,0:T(8,128)(2,1)S(1)} async-done(((bf16[4,96,896]{2,1,0:T(8,128)(2,1)}), bf16[4,96,896]{2,1,0:T(8,128)(2,1)S(1)}, u32[]{:S(2)}, u32[]{:S(2)}) %all-to-all-start.1) | async-done | bytes 688160 | tf_op jit(solution)/shard_map/all_to_all | solution.py:844
  355.4 2.0 multiply_reduce_fusion.1
  357.5 1.6 collective-permute-start.37
  360.0 2.7 collective-permute-done.37
  (217 shorter events, 26.4 us)
Async XLA Ops:
  8.1 57.6 %collective-permute-start.1 = (bf16[512,1536]{1,0:T(8,128)(2,1)}, bf16[512,1536]{1,0:T(8,128)(2,1)}, u32[]{:S(2)}, u32[]{:S(2)}) collective-permute-start(bf16[512,1536]{1,0:T(8,128)(2,1)} %refs_2_.3), channel_id=1, source_target_pairs={{0,1},{1,0},{2,3},{3,2},{4,5},{5,4},{6,7},{7,6},{8,9},{9,8},{10,11... | collective-permute-start | bytes 4718600 | tf_op jit(solution)/shard_map/ppermute | solution.py:866
  12.7 42.0 %copy-start.19 = (bf16[96,1536]{1,0:T(8,128)(2,1)S(1)}, bf16[96,1536]{1,0:T(8,128)(2,1)}, u32[]{:S(2)}) copy-start(bf16[96,1536]{1,0:T(8,128)(2,1)} %param.18) | copy-start | bytes 884740
  13.8 40.9 %copy-start.17 = (bf16[96,1920]{1,0:T(8,128)(2,1)}, bf16[96,1920]{1,0:T(8,128)(2,1)S(1)}, u32[]{:S(2)}) copy-start(bf16[96,1920]{1,0:T(8,128)(2,1)S(1)} %concatenate.28) | copy-start | bytes 1105924
  13.8 13.4 %collective-permute-start.2 = (bf16[96,1920]{1,0:T(8,128)(2,1)S(1)}, bf16[96,1920]{1,0:T(8,128)(2,1)S(1)}, u32[]{:S(2)}, u32[]{:S(2)}) collective-permute-start(bf16[96,1920]{1,0:T(8,128)(2,1)S(1)} %concatenate.28), channel_id=1, source_target_pairs={{0,8},{2,10},{4,12},{6,14},{8,16},{10,18},{12,20},{14,22},{16,24},... | collective-permute-start | bytes 1105928 | tf_op jit(solution)/shard_map/ppermute | solution.py:752
  15.4 17.7 %collective-permute-start.4 = (bf16[96,1920]{1,0:T(8,128)(2,1)S(1)}, bf16[96,1920]{1,0:T(8,128)(2,1)S(1)}, u32[]{:S(2)}, u32[]{:S(2)}) collective-permute-start(bf16[96,1920]{1,0:T(8,128)(2,1)S(1)} %concatenate.28), channel_id=1, source_target_pairs={{0,24},{2,26},{4,28},{6,30},{8,0},{10,2},{12,4},{14,6},{16,8},{18,... | collective-permute-start | bytes 1105928 | tf_op jit(solution)/shard_map/ppermute | solution.py:752
  17.7 15.4 %collective-permute-start.3 = (bf16[96,1920]{1,0:T(8,128)(2,1)S(1)}, bf16[96,1920]{1,0:T(8,128)(2,1)S(1)}, u32[]{:S(2)}, u32[]{:S(2)}) collective-permute-start(bf16[96,1920]{1,0:T(8,128)(2,1)S(1)} %concatenate.28), channel_id=1, source_target_pairs={{0,4},{2,6},{4,0},{6,2},{8,12},{10,14},{12,8},{14,10},{16,20},{18,... | collective-permute-start | bytes 1105928 | tf_op jit(solution)/shard_map/ppermute | solution.py:749
  19.2 18.1 %collective-permute-start.9 = (bf16[96,1920]{1,0:T(8,128)(2,1)S(1)}, bf16[96,1920]{1,0:T(8,128)(2,1)S(1)}, u32[]{:S(2)}, u32[]{:S(2)}) collective-permute-start(bf16[96,1920]{1,0:T(8,128)(2,1)S(1)} %concatenate.28), channel_id=1, source_target_pairs={{0,2},{2,0},{4,6},{6,4},{8,10},{10,8},{12,14},{14,12},{16,18},{18,... | collective-permute-start | bytes 1105928 | tf_op jit(solution)/shard_map/ppermute | solution.py:746
  27.2 5.9 %copy-start.23 = (bf16[96,1920]{1,0:T(8,128)(2,1)}, bf16[96,1920]{1,0:T(8,128)(2,1)S(1)}, u32[]{:S(2)}) copy-start(bf16[96,1920]{1,0:T(8,128)(2,1)S(1)} %collective-permute-done.2.refs_2_) | copy-start | bytes 1105924
  33.8 20.9 %copy-start.5 = (bf16[96,1920]{1,0:T(8,128)(2,1)}, bf16[96,1920]{1,0:T(8,128)(2,1)S(1)}, u32[]{:S(2)}) copy-start(bf16[96,1920]{1,0:T(8,128)(2,1)S(1)} %collective-permute-done.3.refs_1_) | copy-start | bytes 1105924
  33.8 18.8 %collective-permute-start.5 = (bf16[96,1920]{1,0:T(8,128)(2,1)S(1)}, bf16[96,1920]{1,0:T(8,128)(2,1)S(1)}, u32[]{:S(2)}, u32[]{:S(2)}) collective-permute-start(bf16[96,1920]{1,0:T(8,128)(2,1)S(1)} %shard_map.254), channel_id=1, source_target_pairs={{0,16},{2,18},{4,20},{6,22},{8,24},{10,26},{12,28},{14,30},{16,0},... | collective-permute-start | bytes 1105928 | tf_op jit(solution)/shard_map/ppermute | solution.py:752
  35.3 17.4 %collective-permute-start.6 = (bf16[96,1920]{1,0:T(8,128)(2,1)}, bf16[96,1920]{1,0:T(8,128)(2,1)S(1)}, u32[]{:S(2)}, u32[]{:S(2)}) collective-permute-start(bf16[96,1920]{1,0:T(8,128)(2,1)} %copy-done.23), channel_id=1, source_target_pairs={{0,4},{2,6},{4,0},{6,2},{8,12},{10,14},{12,8},{14,10},{16,20},{18,... | collective-permute-start | bytes 1105928 | tf_op jit(solution)/shard_map/ppermute | solution.py:749
  36.8 16.4 %collective-permute-start.8 = (bf16[96,1920]{1,0:T(8,128)(2,1)}, bf16[96,1920]{1,0:T(8,128)(2,1)S(1)}, u32[]{:S(2)}, u32[]{:S(2)}) collective-permute-start(bf16[96,1920]{1,0:T(8,128)(2,1)} %copy-done.24), channel_id=1, source_target_pairs={{0,4},{2,6},{4,0},{6,2},{8,12},{10,14},{12,8},{14,10},{16,20},{18,... | collective-permute-start | bytes 1105928 | tf_op jit(solution)/shard_map/ppermute | solution.py:749
  37.3 17.4 %copy-start.37 = (bf16[96,1920]{1,0:T(8,128)(2,1)}, bf16[96,1920]{1,0:T(8,128)(2,1)S(1)}, u32[]{:S(2)}) copy-start(bf16[96,1920]{1,0:T(8,128)(2,1)S(1)} %collective-permute-done.9) | copy-start | bytes 1105924
  37.3 23.6 %collective-permute-start.10 = (bf16[96,1920]{1,0:T(8,128)(2,1)}, bf16[96,1920]{1,0:T(8,128)(2,1)}, u32[]{:S(2)}, u32[]{:S(2)}) collective-permute-start(bf16[96,1920]{1,0:T(8,128)(2,1)} %copy-done.23), channel_id=1, source_target_pairs={{0,2},{2,0},{4,6},{6,4},{8,10},{10,8},{12,14},{14,12},{16,18},{18,... | collective-permute-start | bytes 1105928 | tf_op jit(solution)/shard_map/ppermute | solution.py:746
  52.6 8.3 %copy-start.6 = (bf16[96,1920]{1,0:T(8,128)(2,1)}, bf16[96,1920]{1,0:T(8,128)(2,1)S(1)}, u32[]{:S(2)}) copy-start(bf16[96,1920]{1,0:T(8,128)(2,1)S(1)} %collective-permute-done.5.refs_1_) | copy-start | bytes 1105924
  52.6 8.3 %collective-permute-start.12 = (bf16[96,1920]{1,0:T(8,128)(2,1)}, bf16[96,1920]{1,0:T(8,128)(2,1)}, u32[]{:S(2)}, u32[]{:S(2)}) collective-permute-start(bf16[96,1920]{1,0:T(8,128)(2,1)} %copy-done.24), channel_id=1, source_target_pairs={{0,2},{2,0},{4,6},{6,4},{8,10},{10,8},{12,14},{14,12},{16,18},{18,... | collective-permute-start | bytes 1105928 | tf_op jit(solution)/shard_map/ppermute | solution.py:746
  52.6 8.8 %collective-permute-start.13 = (bf16[96,1920]{1,0:T(8,128)(2,1)S(1)}, bf16[96,1920]{1,0:T(8,128)(2,1)}, u32[]{:S(2)}, u32[]{:S(2)}) collective-permute-start(bf16[96,1920]{1,0:T(8,128)(2,1)S(1)} %collective-permute-done.3.refs_1_), channel_id=1, source_target_pairs={{0,2},{2,0},{4,6},{6,4},{8,10},{10,8},{12,14},{14,12},{16,18},{18,... | collective-permute-start | bytes 1105928 | tf_op jit(solution)/shard_map/ppermute | solution.py:746
  53.1 10.7 %collective-permute-start.7 = (bf16[96,1920]{1,0:T(8,128)(2,1)S(1)}, bf16[96,1920]{1,0:T(8,128)(2,1)}, u32[]{:S(2)}, u32[]{:S(2)}) collective-permute-start(bf16[96,1920]{1,0:T(8,128)(2,1)S(1)} %collective-permute-done.5.refs_1_), channel_id=1, source_target_pairs={{0,4},{2,6},{4,0},{6,2},{8,12},{10,14},{12,8},{14,10},{16,20},{18,... | collective-permute-start | bytes 1105928 | tf_op jit(solution)/shard_map/ppermute | solution.py:749
  55.9 4.7 %copy-start.32 = (f32[24]{0:T(128)S(1)}, f32[24]{0:T(128)}, u32[]{:S(2)}) copy-start(f32[24]{0:T(128)} %param.26) | copy-start | bytes 292
  55.9 8.1 %copy-start.33 = (f32[24]{0:T(128)S(1)}, f32[24]{0:T(128)}, u32[]{:S(2)}) copy-start(f32[24]{0:T(128)} %param.25) | copy-start | bytes 292
  55.9 8.1 %copy-start.34 = (f32[24]{0:T(128)S(1)}, f32[24]{0:T(128)}, u32[]{:S(2)}) copy-start(f32[24]{0:T(128)} %param.24) | copy-start | bytes 292
  55.9 8.1 %copy-start.12 = (bf16[512,1536]{1,0:T(8,128)(2,1)S(1)}, bf16[512,1536]{1,0:T(8,128)(2,1)}, u32[]{:S(2)}) copy-start(bf16[512,1536]{1,0:T(8,128)(2,1)} %refs_3_.3) | copy-start | bytes 4718596
  55.9 10.6 %copy-start.7 = (f32[4,256]{1,0:T(4,128)S(1)}, f32[4,256]{1,0:T(4,128)}, u32[]{:S(2)}) copy-start(f32[4,256]{1,0:T(4,128)} %refs_9_.5) | copy-start | bytes 12292
  55.9 36.0 %all-to-all-start = ((bf16[4,96,1536]{2,1,0:T(8,128)(2,1)}), bf16[4,96,1536]{2,1,0:T(8,128)(2,1)}, u32[]{:S(2)}, u32[]{:S(2)}) async-start(bf16[4,96,1536]{2,1,0:T(8,128)(2,1)} %broadcast_in_dim.95), calls=%async_computation | async-start | bytes 2359296 | tf_op jit(solution)/shard_map/all_to_all | solution.py:844
  60.4 295.0 %reduce-scatter.2.cloned.1.call-start = ((), (), s32[]{:S(2)}) async-start(), calls=%async_computation.4 | async-start | bytes 10027008 | tf_op jit(solution)/shard_map/reduce_scatter | solution.py:1226
  60.9 3.1 collective-permute-start.11
  61.0 3.7 collective-permute-start.14
  61.5 3.2 collective-permute-start.16
  63.8 1.9 collective-permute-start.15
  64.0 15.2 %copy-start.9 = (f32[1,128]{1,0:T(1,128)}, f32[1,128]{1,0:T(1,128)S(1)}, u32[]{:S(2)}) copy-start(f32[1,128]{1,0:T(1,128)S(1)} %get-tuple-element.203.refs_7_.refs_11_) | copy-start | bytes 1540
  64.0 53.4 %collective-permute-start = (bf16[512,1536]{1,0:T(8,128)(2,1)S(1)}, bf16[512,1536]{1,0:T(8,128)(2,1)}, u32[]{:S(2)}, u32[]{:S(2)}) collective-permute-start(bf16[512,1536]{1,0:T(8,128)(2,1)S(1)} %copy-done.12), channel_id=1, source_target_pairs={{0,1},{1,0},{2,3},{3,2},{4,5},{5,4},{6,7},{7,6},{8,9},{9,8},{10,11... | collective-permute-start | bytes 4718600 | tf_op jit(solution)/shard_map/ppermute | solution.py:866
  66.5 12.8 %copy-start.11 = (f32[4,1536]{1,0:T(4,128)S(1)}, f32[4,1536]{1,0:T(4,128)}, u32[]{:S(2)}) copy-start(f32[4,1536]{1,0:T(4,128)} %refs_9_.4) | copy-start | bytes 73732
  91.9 25.6 %collective-permute-start.19 = (bf16[96,1536]{1,0:T(8,128)(2,1)S(1)}, bf16[96,1536]{1,0:T(8,128)(2,1)S(1)}, u32[]{:S(2)}, u32[]{:S(2)}) collective-permute-start(bf16[96,1536]{1,0:T(8,128)(2,1)S(1)} %shard_map.259.refs_33_), channel_id=1, source_target_pairs={{0,16},{2,18},{4,20},{6,22},{8,24},{10,26},{12,28},{14,30},{16,0},... | collective-permute-start | bytes 884744 | tf_op jit(solution)/shard_map/ppermute | solution.py:752
  93.4 24.1 %collective-permute-start.20 = (bf16[96,1536]{1,0:T(8,128)(2,1)S(1)}, bf16[96,1536]{1,0:T(8,128)(2,1)S(1)}, u32[]{:S(2)}, u32[]{:S(2)}) collective-permute-start(bf16[96,1536]{1,0:T(8,128)(2,1)S(1)} %shard_map.259.refs_33_), channel_id=1, source_target_pairs={{0,24},{2,26},{4,28},{6,30},{8,0},{10,2},{12,4},{14,6},{16,8},{18,... | collective-permute-start | bytes 884744 | tf_op jit(solution)/shard_map/ppermute | solution.py:752
  94.9 22.7 %collective-permute-start.18 = (bf16[96,1536]{1,0:T(8,128)(2,1)S(1)}, bf16[96,1536]{1,0:T(8,128)(2,1)S(1)}, u32[]{:S(2)}, u32[]{:S(2)}) collective-permute-start(bf16[96,1536]{1,0:T(8,128)(2,1)S(1)} %shard_map.259.refs_33_), channel_id=1, source_target_pairs={{0,8},{2,10},{4,12},{6,14},{8,16},{10,18},{12,20},{14,22},{16,24},... | collective-permute-start | bytes 884744 | tf_op jit(solution)/shard_map/ppermute | solution.py:752
  95.9 27.4 %collective-permute-start.17 = (bf16[4,96,1536]{2,1,0:T(8,128)(2,1)}, bf16[4,96,1536]{2,1,0:T(8,128)(2,1)S(1)}, u32[]{:S(2)}, u32[]{:S(2)}) collective-permute-start(bf16[4,96,1536]{2,1,0:T(8,128)(2,1)} %shard_map.258.refs_1_.refs_32_.refs_2_), channel_id=1, source_target_pairs={{0,4},{2,6},{4,0},{6,2},{8,12},{10,14},{12,8},{14,10},{16,20},{18,... | collective-permute-start | bytes 3538952 | tf_op jit(solution)/shard_map/ppermute | solution.py:749
  117.5 15.1 %collective-permute-start.21 = (bf16[4,96,1536]{2,1,0:T(8,128)(2,1)}, bf16[4,96,1536]{2,1,0:T(8,128)(2,1)}, u32[]{:S(2)}, u32[]{:S(2)}) collective-permute-start(bf16[4,96,1536]{2,1,0:T(8,128)(2,1)} %shard_map.258.refs_1_.refs_32_.refs_2_), channel_id=1, source_target_pairs={{0,2},{2,0},{4,6},{6,4},{8,10},{10,8},{12,14},{14,12},{16,18},{18,... | collective-permute-start | bytes 3538952 | tf_op jit(solution)/shard_map/ppermute | solution.py:746
  124.3 8.3 %collective-permute-start.22 = (bf16[4,96,1536]{2,1,0:T(8,128)(2,1)}, bf16[4,96,1536]{2,1,0:T(8,128)(2,1)}, u32[]{:S(2)}, u32[]{:S(2)}) collective-permute-start(bf16[4,96,1536]{2,1,0:T(8,128)(2,1)} %shard_map.262.refs_3_), channel_id=1, source_target_pairs={{0,2},{2,0},{4,6},{6,4},{8,10},{10,8},{12,14},{14,12},{16,18},{18,... | collective-permute-start | bytes 3538952 | tf_op jit(solution)/shard_map/ppermute | solution.py:746
  125.1 6.0 %copy-start.1 = (bf16[96,1536]{1,0:T(8,128)(2,1)S(1)}, bf16[96,1536]{1,0:T(8,128)(2,1)}, u32[]{:S(2)}) copy-start(bf16[96,1536]{1,0:T(8,128)(2,1)} %copy-done) | copy-start | bytes 884740
  131.9 15.5 %collective-permute-start.23 = (bf16[2,96,1536]{2,1,0:T(8,128)(2,1)}, bf16[2,96,1536]{2,1,0:T(8,128)(2,1)S(1)}, u32[]{:S(2)}, u32[]{:S(2)}) collective-permute-start(bf16[2,96,1536]{2,1,0:T(8,128)(2,1)} %pad_maximum_fusion.refs_4_), channel_id=1, source_target_pairs={{0,4},{2,6},{4,0},{6,2},{8,12},{10,14},{12,8},{14,10},{16,20},{18,... | collective-permute-start | bytes 1769480 | tf_op jit(solution)/shard_map/ppermute | solution.py:749
  147.4 3.6 collective-permute-start.24
  148.8 14.5 %collective-permute-start.25 = (bf16[2,96,1536]{2,1,0:T(8,128)(2,1)}, bf16[2,96,1536]{2,1,0:T(8,128)(2,1)S(1)}, u32[]{:S(2)}, u32[]{:S(2)}) collective-permute-start(bf16[2,96,1536]{2,1,0:T(8,128)(2,1)} %pad_maximum_fusion.1.refs_5_), channel_id=1, source_target_pairs={{0,4},{2,6},{4,0},{6,2},{8,12},{10,14},{12,8},{14,10},{16,20},{18,... | collective-permute-start | bytes 1769480 | tf_op jit(solution)/shard_map/ppermute | solution.py:749
  149.5 14.7 %collective-permute-start.27 = (bf16[2,96,1536]{2,1,0:T(8,128)(2,1)}, bf16[2,96,1536]{2,1,0:T(8,128)(2,1)}, u32[]{:S(2)}, u32[]{:S(2)}) collective-permute-start(bf16[2,96,1536]{2,1,0:T(8,128)(2,1)} %pad_maximum_fusion.1.refs_5_), channel_id=1, source_target_pairs={{0,2},{2,0},{4,6},{6,4},{8,10},{10,8},{12,14},{14,12},{16,18},{18,... | collective-permute-start | bytes 1769480 | tf_op jit(solution)/shard_map/ppermute | solution.py:746
  149.5 14.7 %collective-permute-start.26 = (bf16[2,96,1536]{2,1,0:T(8,128)(2,1)}, bf16[2,96,1536]{2,1,0:T(8,128)(2,1)}, u32[]{:S(2)}, u32[]{:S(2)}) collective-permute-start(bf16[2,96,1536]{2,1,0:T(8,128)(2,1)} %pad_maximum_fusion.refs_4_), channel_id=1, source_target_pairs={{0,2},{2,0},{4,6},{6,4},{8,10},{10,8},{12,14},{14,12},{16,18},{18,... | collective-permute-start | bytes 1769480 | tf_op jit(solution)/shard_map/ppermute | solution.py:746
  163.3 2.1 collective-permute-start.29
  164.2 2.0 collective-permute-start.28
  180.5 3.7 collective-permute-start.31
  206.1 35.6 %collective-permute-start.30 = (bf16[512,1536]{1,0:T(8,128)(2,1)}, bf16[512,1536]{1,0:T(8,128)(2,1)S(1)}, u32[]{:S(2)}, u32[]{:S(2)}) collective-permute-start(bf16[512,1536]{1,0:T(8,128)(2,1)} %get-tuple-element.97), channel_id=1, source_target_pairs={{0,1},{1,0},{2,3},{3,2},{4,5},{5,4},{6,7},{7,6},{8,9},{9,8},{10,11... | collective-permute-start | bytes 4718600 | tf_op jit(solution)/shard_map/ppermute | solution.py:866
  238.2 8.7 %collective-permute-start.32 = (bf16[8,96,1024]{2,1,0:T(8,128)(2,1)}, bf16[8,96,1024]{2,1,0:T(8,128)(2,1)}, u32[]{:S(2)}, u32[]{:S(2)}) collective-permute-start(bf16[8,96,1024]{2,1,0:T(8,128)(2,1)} %get-tuple-element.113), channel_id=1, source_target_pairs={{0,2},{2,0},{4,6},{6,4},{8,10},{10,8},{12,14},{14,12},{16,18},{18,... | collective-permute-start | bytes 4718600 | tf_op jit(solution)/shard_map/ppermute | solution.py:746
  248.4 21.4 %collective-permute-start.33 = (bf16[4,96,1024]{2,1,0:T(8,128)(2,1)S(1)}, bf16[4,96,1024]{2,1,0:T(8,128)(2,1)S(1)}, u32[]{:S(2)}, u32[]{:S(2)}) collective-permute-start(bf16[4,96,1024]{2,1,0:T(8,128)(2,1)S(1)} %fusion.2.refs_20_), channel_id=1, source_target_pairs={{0,4},{2,6},{4,0},{6,2},{8,12},{10,14},{12,8},{14,10},{16,20},{18,... | collective-permute-start | bytes 2359304 | tf_op jit(solution)/shard_map/ppermute | solution.py:749
  272.3 5.0 %copy-start.8 = (f32[4,256]{1,0:T(4,128)S(1)}, f32[4,256]{1,0:T(4,128)}, u32[]{:S(2)}) copy-start(f32[4,256]{1,0:T(4,128)} %refs_9_.5) | copy-start | bytes 12292
  272.3 5.0 %copy-start.10 = (f32[1,128]{1,0:T(1,128)S(1)}, f32[1,128]{1,0:T(1,128)}, u32[]{:S(2)}) copy-start(f32[1,128]{1,0:T(1,128)} %copy-done.9) | copy-start | bytes 1540
  272.3 34.0 %all-to-all-start.2 = ((bf16[4,96,1024]{2,1,0:T(8,128)(2,1)}), bf16[4,96,1024]{2,1,0:T(8,128)(2,1)S(1)}, u32[]{:S(2)}, u32[]{:S(2)}) async-start(bf16[4,96,1024]{2,1,0:T(8,128)(2,1)} %fusion.refs_17_.refs_1_), calls=%async_computation.3 | async-start | bytes 1572864 | tf_op jit(solution)/shard_map/all_to_all | solution.py:844
  291.3 10.8 %collective-permute-start.38 = (f32[6,1536]{1,0:T(8,128)S(1)}, f32[6,1536]{1,0:T(8,128)S(1)}, u32[]{:S(2)}, u32[]{:S(2)}) collective-permute-start(f32[6,1536]{1,0:T(8,128)S(1)} %pad_maximum_fusion.4), channel_id=1, source_target_pairs={{0,2},{2,0},{4,6},{6,4},{8,10},{10,8},{12,14},{14,12},{16,18},{18,... | collective-permute-start | bytes 110600 | tf_op jit(solution)/shard_map/ppermute | solution.py:746
  291.4 15.0 %collective-permute-start.34 = (bf16[8,96,896]{2,1,0:T(8,128)(2,1)}, bf16[8,96,896]{2,1,0:T(8,128)(2,1)}, u32[]{:S(2)}, u32[]{:S(2)}) collective-permute-start(bf16[8,96,896]{2,1,0:T(8,128)(2,1)} %shard_map.274), channel_id=1, source_target_pairs={{0,2},{2,0},{4,6},{6,4},{8,10},{10,8},{12,14},{14,12},{16,18},{18,... | collective-permute-start | bytes 4128776 | tf_op jit(solution)/shard_map/ppermute | solution.py:746
  302.1 4.2 %collective-permute-start.39 = (f32[6,1536]{1,0:T(8,128)S(1)}, f32[6,1536]{1,0:T(8,128)S(1)}, u32[]{:S(2)}, u32[]{:S(2)}) collective-permute-start(f32[6,1536]{1,0:T(8,128)S(1)} %shard_map.281), channel_id=1, source_target_pairs={{0,4},{2,6},{4,0},{6,2},{8,12},{10,14},{12,8},{14,10},{16,20},{18,... | collective-permute-start | bytes 110600 | tf_op jit(solution)/shard_map/ppermute | solution.py:749
  302.8 36.4 %collective-permute-start.35 = (bf16[512,1536]{1,0:T(8,128)(2,1)}, bf16[512,1536]{1,0:T(8,128)(2,1)}, u32[]{:S(2)}, u32[]{:S(2)}) collective-permute-start(bf16[512,1536]{1,0:T(8,128)(2,1)} %shard_map.276.refs_1_), channel_id=1, source_target_pairs={{0,1},{1,0},{2,3},{3,2},{4,5},{5,4},{6,7},{7,6},{8,9},{9,8},{10,11... | collective-permute-start | bytes 4718600 | tf_op jit(solution)/shard_map/ppermute | solution.py:866
  308.9 16.8 %collective-permute-start.36 = (bf16[4,96,896]{2,1,0:T(8,128)(2,1)S(1)}, bf16[4,96,896]{2,1,0:T(8,128)(2,1)S(1)}, u32[]{:S(2)}, u32[]{:S(2)}) collective-permute-start(bf16[4,96,896]{2,1,0:T(8,128)(2,1)S(1)} %fusion.3.refs_3_), channel_id=1, source_target_pairs={{0,4},{2,6},{4,0},{6,2},{8,12},{10,14},{12,8},{14,10},{16,20},{18,... | collective-permute-start | bytes 2064392 | tf_op jit(solution)/shard_map/ppermute | solution.py:749
  327.9 16.2 %collective-permute-start.40 = (f32[6,1536]{1,0:T(8,128)S(1)}, f32[6,1536]{1,0:T(8,128)S(1)}, u32[]{:S(2)}, u32[]{:S(2)}) collective-permute-start(f32[6,1536]{1,0:T(8,128)S(1)} %shard_map.282), channel_id=1, source_target_pairs={{0,8},{2,10},{4,12},{6,14},{8,16},{10,18},{12,20},{14,22},{16,24},... | collective-permute-start | bytes 110600 | tf_op jit(solution)/shard_map/ppermute | solution.py:752
  329.6 14.4 %collective-permute-start.41 = (f32[6,1536]{1,0:T(8,128)S(1)}, f32[6,1536]{1,0:T(8,128)S(1)}, u32[]{:S(2)}, u32[]{:S(2)}) collective-permute-start(f32[6,1536]{1,0:T(8,128)S(1)} %shard_map.282), channel_id=1, source_target_pairs={{0,16},{2,18},{4,20},{6,22},{8,24},{10,26},{12,28},{14,30},{16,0},... | collective-permute-start | bytes 110600 | tf_op jit(solution)/shard_map/ppermute | solution.py:752
  332.4 11.7 %collective-permute-start.42 = (f32[6,1536]{1,0:T(8,128)S(1)}, f32[6,1536]{1,0:T(8,128)S(1)}, u32[]{:S(2)}, u32[]{:S(2)}) collective-permute-start(f32[6,1536]{1,0:T(8,128)S(1)} %shard_map.282), channel_id=1, source_target_pairs={{0,24},{2,26},{4,28},{6,30},{8,0},{10,2},{12,4},{14,6},{16,8},{18,... | collective-permute-start | bytes 110600 | tf_op jit(solution)/shard_map/ppermute | solution.py:752
  333.7 19.6 %all-to-all-start.1 = ((bf16[4,96,896]{2,1,0:T(8,128)(2,1)}), bf16[4,96,896]{2,1,0:T(8,128)(2,1)S(1)}, u32[]{:S(2)}, u32[]{:S(2)}) async-start(bf16[4,96,896]{2,1,0:T(8,128)(2,1)} %fusion.1.refs_1_), calls=%async_computation.1 | async-start | bytes 1376256 | tf_op jit(solution)/shard_map/all_to_all | solution.py:844
  344.1 3.7 collective-permute-start.43
  357.5 5.2 %collective-permute-start.37 = (f32[96,384]{1,0:T(8,128)S(1)}, f32[96,384]{1,0:T(8,128)S(1)}, u32[]{:S(2)}, u32[]{:S(2)}) collective-permute-start(f32[96,384]{1,0:T(8,128)S(1)} %pad_maximum_fusion.3), channel_id=1, source_target_pairs={{0,1},{1,0},{2,3},{3,2},{4,5},{5,4},{6,7},{7,6},{8,9},{9,8},{10,11... | collective-permute-start | bytes 442376 | tf_op jit(solution)/shard_map/ppermute | solution.py:866
  (27 other events, 48.5 us)
Sparse Core Ops, SparseCore 0:
  206.2 111.2 reduce-scatter.1

commit v2 on v1

--- a/solution.py
+++ b/solution.py
@@ -538,13 +538,13 @@
             scaled = (act * weights).astype(BF)
             b_grad[span, :] += dot(scaled, states_low)
             totals = totals + split_dot(flows + weighted, chooser[0])
-            totals = totals + split_dot(weighted, chooser[2])
             passed = head_rows(jnp.exp(last)) * states
             spread = passed * held
             high = spread.astype(BF)
             rest = (spread - high.astype(F32)).astype(BF)
             summed = dot(ones, high, 1, 1) + dot(ones, rest, 1, 1)
-            last_sum = split_dot(summed, chooser[3])
+            row_sum = jnp.broadcast_to(jnp.sum(weighted, axis=0, keepdims=True), (8, TILE))
+            last_sum = split_dot(summed, chooser[3]) + split_dot(row_sum, chooser[2])
             totals = totals + jnp.where(final_row, last_sum[0:1, :], 0.0)
         else:
             totals = totals + split_dot(flows, chooser[0])
@@ -1074,22 +1074,6 @@
     proj_halves = links.ring_halves(proj_ring)
     proj_others = links.pair_halves(proj_halves)
 
-    grad, grad_t = call(
-        functools.partial(mask_body, half_blocks),
-        (blocks,),
-        [smem(), half_spec, half_spec, block_rows(1)],
-        [block_rows(width), pl.BlockSpec((width, QLEN), lambda b: (0, b))],
-        [((rows, width), BF), ((width, rows), BF)],
-        [],
-        rows * width,
-        8 * rows * width,
-        place,
-        cotangent,
-        cot_got,
-        live.astype(BF),
-        deps=(entry,),
-    )
-
     broad = wide // WIDE_TILE
 
     def broad_cols(n, first=0):
@@ -1113,6 +1097,22 @@
         all_w,
         aliases={3 + len(gate_pieces): 0},
     )
+    grad, grad_t = call(
+        functools.partial(mask_body, half_blocks),
+        (blocks,),
+        [smem(), half_spec, half_spec, block_rows(1)],
+        [block_rows(width), pl.BlockSpec((width, QLEN), lambda b: (0, b))],
+        [((rows, width), BF), ((width, rows), BF)],
+        [],
+        rows * width,
+        8 * rows * width,
+        place,
+        cotangent,
+        cot_got,
+        live.astype(BF),
+        deps=(gate,),
+    )
+
     square_sum = jnp.sum(squares, axis=1).reshape(8, rows // 8)
     square_sum = square_sum + over_tensor(tied(square_sum, *proj_others[:1]))
     scale = lax.rsqrt(square_sum / INNER + EPSILON).reshape(rows, 1)

time: 379 us -> 378 us (level)
  no operation moved by 1% of the time
where the time goes in v2:
time: 378 us; the launch traced here: 371 us
  Pallas kernels  203 us (54%)
  waiting for transfers between devices  68.3 us (18%)
  starting transfers between devices  51.1 us (14%)
  local copies, waits for them, and re-layouts  19.7 us (5%)
  between operations  15.5 us (4%)
  other arithmetic  13.4 us (4%)
    pallas_call x15, Pallas kernels, call(): pl.pallas_call(held, grid_spec=pltpu.PrefetchScalarGridSpec(num_scalar_pr...  203 us
    ppermute x9, waiting for transfers between devices, over_ring(): lax.ppermute(x, 'dp', self.moved(lambda a, b, c: ((a + k) % self.ring, b,...  29.2 us
    ppermute x10, waiting for transfers between devices, over_pair(): return lax.ppermute(x, 'dp', self.moved(lambda a, b, c: (a, 1 - b, c)))  19.4 us
    ppermute x9, starting transfers between devices, over_ring(): lax.ppermute(x, 'dp', self.moved(lambda a, b, c: ((a + k) % self.ring, b,...  15.1 us
    all_to_all x3, starting transfers between devices, over_rings(): return lax.all_to_all(x, 'dp', 0, 0, tiled=True, axis_index_groups=groups)  12.9 us
    ppermute x8, starting transfers between devices, over_tensor(): return lax.ppermute(x, 'tensor', [(0, 1), (1, 0)])  10.9 us
    ppermute x8, waiting for transfers between devices, over_tensor(): return lax.ppermute(x, 'tensor', [(0, 1), (1, 0)])  10.9 us
    unnamed x93, local copies, waits for them, and re-layouts  9.76 us
  transfers between devices with their start and end apart: 48, of which 19 were waited for; matrix products, arithmetic and copies ran while one was open for 5% of the time, Pallas kernels for 46%

profile of v2, /device:TPU:0, one launch (start us, length us, event | category | flops | bytes accessed | tf_op | source)
XLA Modules:
  0.0 371.1 jit_solution(4823732816648268777)
XLA Ops:
  8.1 2.9 collective-permute-start.1
  12.7 1.1 concatenate.28
  13.8 1.6 collective-permute-start.2
  15.4 2.2 collective-permute-start.4
  17.7 1.5 collective-permute-start.3
  19.2 8.0 %collective-permute-done.2.refs_2_ = bf16[96,1920]{1,0:T(8,128)(2,1)S(1)} collective-permute-done((bf16[96,1920]{1,0:T(8,128)(2,1)S(1)}, bf16[96,1920]{1,0:T(8,128)(2,1)S(1)}, u32[]{:S(2)}, u32[]{:S(2)}) %collective-permute-start.2) | collective-permute-done | bytes 368672 | tf_op jit(solution)/shard_map/ppermute | solution.py:752
  27.2 5.9 %collective-permute-done.4.refs_3_ = bf16[96,1920]{1,0:T(8,128)(2,1)S(1)} collective-permute-done((bf16[96,1920]{1,0:T(8,128)(2,1)S(1)}, bf16[96,1920]{1,0:T(8,128)(2,1)S(1)}, u32[]{:S(2)}, u32[]{:S(2)}) %collective-permute-start.4) | collective-permute-done | bytes 368672 | tf_op jit(solution)/shard_map/ppermute | solution.py:752
  33.8 1.4 collective-permute-start.5
  35.3 1.5 collective-permute-start.6
  37.3 15.3 %collective-permute-done.5.refs_1_ = bf16[96,1920]{1,0:T(8,128)(2,1)S(1)} collective-permute-done((bf16[96,1920]{1,0:T(8,128)(2,1)S(1)}, bf16[96,1920]{1,0:T(8,128)(2,1)S(1)}, u32[]{:S(2)}, u32[]{:S(2)}) %collective-permute-start.5) | collective-permute-done | bytes 368672 | tf_op jit(solution)/shard_map/ppermute | solution.py:752
  53.1 1.5 collective-permute-start.7
  54.8 1.1 broadcast_in_dim.94
  55.9 4.4 %all-to-all-start = ((bf16[4,96,1536]{2,1,0:T(8,128)(2,1)}), bf16[4,96,1536]{2,1,0:T(8,128)(2,1)}, u32[]{:S(2)}, u32[]{:S(2)}) async-start(bf16[4,96,1536]{2,1,0:T(8,128)(2,1)} %broadcast_in_dim.94), calls=%async_computation | async-start | bytes 2359296 | tf_op jit(solution)/shard_map/all_to_all | solution.py:844
  61.5 2.3 collective-permute-done.7
  64.7 1.1 collective-permute-done.15
  66.5 12.7 %shard_map.256 = (bf16[1024,1536]{1,0:T(8,128)(2,1)}, bf16[1536,1024]{1,0:T(8,128)(2,1)}, f32[1024,256]{1,0:T(8,128)}, bf16[1024,128]{1,0:T(8,128)(2,1)S(1)}, bf...) custom-call(s32[16]{0:T(128)S(1)} %stack.136.refs_0_.refs_1_, ...), custom_call_target="tpu_custom_call" | custom-call | flops 3623878656 | bytes 31457280 | tf_op jit(solution)/shard_map/pallas_call | solution.py:78
  79.3 12.6 %shard_map.257 = (bf16[1536,3456]{1,0:T(8,128)(2,1)}, bf16[1024,1536]{1,0:T(8,128)(2,1)}, bf16[1024,1536]{1,0:T(8,128)(2,1)}, bf16[1024,1536]{1,0:T(8,128)(2,1)}...) custom-call(s32[16]{0:T(128)S(1)} %stack.136.refs_0_.refs_1_, ...), custom_call_target="tpu_custom_call", output_to_operand_aliasing={{0}: (26, {})} | custom-call | flops 9663676416 | bytes 10485760 | tf_op jit(solution)/shard_map/pallas_call | solution.py:78
  91.9 1.5 collective-permute-start.19
  93.4 1.5 collective-permute-start.20
  94.9 1.0 collective-permute-start.18
  96.5 20.9 %shard_map.260 = (bf16[1536,3456]{1,0:T(8,128)(2,1)}, bf16[1024,1536]{1,0:T(8,128)(2,1)}, bf16[1024,1536]{1,0:T(8,128)(2,1)}, bf16[1024,1536]{1,0:T(8,128)(2,1)}...) custom-call(s32[16]{0:T(128)S(1)} %stack.136.refs_0_.refs_1_, ...), custom_call_target="tpu_custom_call", output_to_operand_aliasing={{0}: (26, {}), {1}: (27, {}), {2}: (28, {}), {3}: (29, {}),... | custom-call | flops 19327352832 | bytes 20971520 | tf_op jit(solution)/shard_map/pallas_call | solution.py:78
  117.6 5.7 %collective-permute-done.17.refs_0_ = bf16[4,96,1536]{2,1,0:T(8,128)(2,1)S(1)} collective-permute-done((bf16[4,96,1536]{2,1,0:T(8,128)(2,1)}, bf16[4,96,1536]{2,1,0:T(8,128)(2,1)S(1)}, u32[]{:S(2)}, u32[]{:S(2)}) %collective-permute-start.17) | collective-permute-done | bytes 1179680 | tf_op jit(solution)/shard_map/ppermute | solution.py:749
  123.3 1.0 copy-done.21
  127.5 12.0 %shard_map.262 = (bf16[1536,3456]{1,0:T(8,128)(2,1)}, bf16[1024,1536]{1,0:T(8,128)(2,1)}, f32[1024,128]{1,0:T(8,128)S(1)}) custom-call(s32[16]{0:T(128)S(1)} %stack.153.refs_0_, bf16[1024,1536]{1,0:T(8,128)(2,1)} %get-tuple-element.74.refs_2_.refs_1_, bf16[4,96,1536]{2,1,0:T(8,128)(2,1)} %shard_map.258.refs_1_.refs_32_.refs_2_, ...), custom_call_target="tpu_custom_call", output_to_operand_aliasing={{0}: (7, {})} | custom-call | flops 14495514624 | bytes 18874368 | tf_op jit(solution)/shard_map/pallas_call | solution.py:78
  139.7 1.8 collective-permute-done.23.refs_1_.refs_0_
  144.0 5.9 %shard_map.263 = (bf16[1024,1536]{1,0:T(8,128)(2,1)}, bf16[1536,1024]{1,0:T(8,128)(2,1)}) custom-call(s32[1]{0:T(128)} %bitcast.refs_1_.refs_0_, bf16[512,1536]{1,0:T(8,128)(2,1)} %refs_3_.3, bf16[512,1536]{1,0:T(8,128)(2,1)} %collective-permute-done.refs_2_, bf16[1024,1]{1,0:T(8,128)(2,1)S(1)} %convert_element_type.113.refs_3_, ...), custom_call_target="tpu_custom_call" | custom-call | flops 4718592 | bytes 12582912 | tf_op jit(solution)/shard_map/pallas_call | solution.py:78
  150.2 12.0 %shard_map.265 = (bf16[1024,1536]{1,0:T(8,128)(2,1)}, bf16[1536,3072]{1,0:T(8,128)(2,1)}) custom-call(s32[1]{0:T(128)} %bitcast.17.refs_0_, bf16[1536,1024]{1,0:T(8,128)(2,1)} %get-tuple-element.91.refs_1_, f32[1024,1536]{1,0:T(8,128)} %get-tuple-element.88.refs_6_.refs_2_.refs_3_.refs_7_, bf16[1024,1536]{1,0:T(8,128)(2,1)} %get-tuple-element.90.refs_4_.refs_3_, ...), custom_call_target="tpu_custom_call" | custom-call | flops 14495514624 | bytes 22020096 | tf_op jit(solution)/shard_map/pallas_call | solution.py:78
  163.0 1.2 collective-permute-done.29.refs_11_
  165.9 13.3 %shard_map.268 = (bf16[1536,1536]{1,0:T(8,128)(2,1)}, bf16[512,1536]{1,0:T(8,128)(2,1)}, f32[512,1536]{1,0:T(8,128)}, f32[1024,1]{1,0:T(8,128)S(1)}) custom-call(s32[1]{0:T(128)} %bitcast.refs_1_.refs_0_, s32[16]{0:T(128)S(1)} %stack.136.refs_0_.refs_1_, bf16[1024,1536]{1,0:T(8,128)(2,1)} %get-tuple-element.93.refs_1_.refs_2_, ...), custom_call_target="tpu_custom_call" | custom-call | flops 14495514624 | bytes 12582912 | tf_op jit(solution)/shard_map/pallas_call | solution.py:78
  179.4 1.5 collective-permute-start.31
  181.0 2.1 collective-permute-done.31
  183.1 1.0 copy.102.refs_7_
  184.1 20.8 %shard_map.269 = (bf16[1024,1536]{1,0:T(8,128)(2,1)}, bf16[1024,3456]{1,0:T(8,128)(2,1)}, f32[2,1536]{1,0:T(2,128)S(1)}, bf16[1536,3072]{1,0:T(8,128)(2,1)}) custom-call(s32[1]{0:T(128)} %bitcast.17.refs_0_, bf16[1024,1536]{1,0:T(8,128)(2,1)} %get-tuple-element.94.refs_3_.refs_1_, ...), custom_call_target="tpu_custom_call", output_to_operand_aliasing={{3}: (10, {})} | custom-call | flops 28991029248 | bytes 22020096 | tf_op jit(solution)/shard_map/pallas_call | solution.py:78
  205.0 1.5 collective-permute-start.30
  206.5 30.2 %shard_map.270 = (bf16[8,96,1024]{2,1,0:T(8,128)(2,1)}, bf16[8,96,1024]{2,1,0:T(8,128)(2,1)}, bf16[1024,3456]{1,0:T(8,128)(2,1)}, f32[4,1024]{1,0:T(4,128)S(1)},...) custom-call(s32[1]{0:T(128)} %bitcast.17.refs_0_, ...), custom_call_target="tpu_custom_call", output_to_operand_aliasing={{2}: (16, {})} | custom-call | flops 28991029248 | bytes 20971520 | tf_op jit(solution)/shard_map/pallas_call | solution.py:78
  237.3 3.2 collective-permute-done.30.refs_1_
  240.6 1.2 copy-done.16
  241.7 4.1 %shard_map.271.refs_21_ = bf16[512,1536]{1,0:T(8,128)(2,1)} custom-call(f32[512,1536]{1,0:T(8,128)} %get-tuple-element.95.refs_0_, bf16[512,1536]{1,0:T(8,128)(2,1)} %copy-done.16, bf16[512,1536]{1,0:T(8,128)(2,1)} %refs_2_.3, f32[512,1]{1,0:T(8,128)S(1)} %copy.103.refs_3_, f32[4,1024]{1,0:T(4,128)S(1)} %get-tuple-element.107.refs_4_), custom_call_target="tpu_custom_call" | custom-call | flops 2359296 | bytes 7864320 | tf_op jit(solution)/shard_map/pallas_call | solution.py:78
  245.8 1.5 fusion.2.refs_20_
  247.3 1.4 collective-permute-start.33
  248.7 18.8 %shard_map.272 = (bf16[8,96,896]{2,1,0:T(8,128)(2,1)}, bf16[8,96,896]{2,1,0:T(8,128)(2,1)}, bf16[1024,3456]{1,0:T(8,128)(2,1)}, f32[4,512]{1,0:T(4,128)S(1)}, f3...) custom-call(s32[1]{0:T(128)} %bitcast.17.refs_0_, ...), custom_call_target="tpu_custom_call", output_to_operand_aliasing={{2}: (19, {})} | custom-call | flops 14495514624 | bytes 10485760 | tf_op jit(solution)/shard_map/pallas_call | solution.py:78
  267.5 2.1 collective-permute-done.33
  269.6 2.4 fusion.refs_17_.refs_1_
  272.1 5.0 %all-to-all-start.2 = ((bf16[4,96,1024]{2,1,0:T(8,128)(2,1)}), bf16[4,96,1024]{2,1,0:T(8,128)(2,1)S(1)}, u32[]{:S(2)}, u32[]{:S(2)}) async-start(bf16[4,96,1024]{2,1,0:T(8,128)(2,1)} %fusion.refs_17_.refs_1_), calls=%async_computation.3 | async-start | bytes 1572864 | tf_op jit(solution)/shard_map/all_to_all | solution.py:844
  277.1 13.7 %shard_map.273 = (bf16[8,96,896]{2,1,0:T(8,128)(2,1)}, bf16[8,96,896]{2,1,0:T(8,128)(2,1)}, bf16[1024,3456]{1,0:T(8,128)(2,1)}, f32[4,256]{1,0:T(4,128)S(1)}, f32[2,128]{1,0:T(2,128)S(1)}) custom-call(s32[1]{0:T(128)} %bitcast.17.refs_0_, f32[4]{0:T(128)S(1)} %add_convert_fusion.2.refs_2_.refs_1_, ...), custom_call_target="tpu_custom_call", output_to_operand_aliasing={{2}: (14, {}), {0}: (15, {}), {1}: (16, {})} | custom-call | flops 1811939328 | bytes 5242880 | tf_op jit(solution)/shard_map/pallas_call | solution.py:78
  291.6 10.3 %shard_map.276.refs_1_ = bf16[512,1536]{1,0:T(8,128)(2,1)} custom-call(s32[1]{0:T(128)} %bitcast.refs_1_.refs_0_, bf16[1024,3456]{1,0:T(8,128)(2,1)} %get-tuple-element.124.refs_1_, bf16[1536,3456]{1,0:T(8,128)(2,1)} %get-tuple-element.125.refs_2_), custom_call_target="tpu_custom_call" | custom-call | flops 14495514624 | bytes 25165824 | tf_op jit(solution)/shard_map/pallas_call | solution.py:78
  302.5 1.5 collective-permute-start.35
  304.0 2.1 collective-permute-done.39
  306.1 1.3 copy-done.13
  307.4 1.3 fusion.3.refs_3_
  309.3 10.7 %shard_map.275.refs_0_.refs_1_ = f32[512,1536]{1,0:T(8,128)} custom-call(s32[1]{0:T(128)} %bitcast.refs_1_.refs_0_, bf16[1024,3456]{1,0:T(8,128)(2,1)} %get-tuple-element.124.refs_1_, bf16[1536,3456]{1,0:T(8,128)(2,1)} %get-tuple-element.125.refs_2_, bf16[4,96,896]{2,1,0:T(8,128)(2,1)S(1)} %fusion.3.refs_3_), custom_call_target="tpu_custom_call" | custom-call | flops 14495514624 | bytes 25165824 | tf_op jit(solution)/shard_map/pallas_call | solution.py:78
  320.0 5.4 %collective-permute-done.36.refs_0_ = bf16[4,96,896]{2,1,0:T(8,128)(2,1)S(1)} collective-permute-done((bf16[4,96,896]{2,1,0:T(8,128)(2,1)S(1)}, bf16[4,96,896]{2,1,0:T(8,128)(2,1)S(1)}, u32[]{:S(2)}, u32[]{:S(2)}) %collective-permute-start.36) | collective-permute-done | bytes 688160 | tf_op jit(solution)/shard_map/ppermute | solution.py:749
  325.4 2.2 fusion.1.refs_1_
  327.7 1.7 collective-permute-start.40
  329.4 2.8 collective-permute-start.41
  332.1 1.3 collective-permute-start.42
  333.5 3.5 all-to-all-start.1
  337.1 1.8 collective-permute-done.35.refs_1_
  338.9 4.9 %shard_map.277.refs_1_ = bf16[512,1536]{1,0:T(8,128)(2,1)} custom-call(f32[512,1536]{1,0:T(8,128)} %shard_map.275.refs_0_.refs_1_, bf16[512,1536]{1,0:T(8,128)(2,1)} %collective-permute-done.35.refs_1_, bf16[512,1536]{1,0:T(8,128)(2,1)} %refs_2_.3, bf16[512,1536]{1,0:T(8,128)(2,1)} %refs_3_.3, f32[1,1536]{1,0:T(1,128)S(1)} %get-tuple-element.128.refs_4_), custom_call_target="tpu_custom_call" | custom-call | flops 2359296 | bytes 9437184 | tf_op jit(solution)/shard_map/pallas_call | solution.py:78
  343.9 1.5 collective-permute-start.43
  348.2 4.9 %all-to-all-done.1.refs_0_ = bf16[4,96,896]{2,1,0:T(8,128)(2,1)S(1)} async-done(((bf16[4,96,896]{2,1,0:T(8,128)(2,1)}), bf16[4,96,896]{2,1,0:T(8,128)(2,1)S(1)}, u32[]{:S(2)}, u32[]{:S(2)}) %all-to-all-start.1) | async-done | bytes 688160 | tf_op jit(solution)/shard_map/all_to_all | solution.py:844
  354.1 1.0 multiply_reduce_fusion
  355.1 2.0 multiply_reduce_fusion.1
  359.0 3.5 collective-permute-done.37
  (217 shorter events, 26.1 us)
Async XLA Ops:
  8.1 57.6 %collective-permute-start.1 = (bf16[512,1536]{1,0:T(8,128)(2,1)}, bf16[512,1536]{1,0:T(8,128)(2,1)}, u32[]{:S(2)}, u32[]{:S(2)}) collective-permute-start(bf16[512,1536]{1,0:T(8,128)(2,1)} %refs_2_.3), channel_id=1, source_target_pairs={{0,1},{1,0},{2,3},{3,2},{4,5},{5,4},{6,7},{7,6},{8,9},{9,8},{10,11... | collective-permute-start | bytes 4718600 | tf_op jit(solution)/shard_map/ppermute | solution.py:866
  12.7 42.0 %copy-start.19 = (bf16[96,1536]{1,0:T(8,128)(2,1)S(1)}, bf16[96,1536]{1,0:T(8,128)(2,1)}, u32[]{:S(2)}) copy-start(bf16[96,1536]{1,0:T(8,128)(2,1)} %param.18) | copy-start | bytes 884740
  13.8 40.9 %copy-start.17 = (bf16[96,1920]{1,0:T(8,128)(2,1)}, bf16[96,1920]{1,0:T(8,128)(2,1)S(1)}, u32[]{:S(2)}) copy-start(bf16[96,1920]{1,0:T(8,128)(2,1)S(1)} %concatenate.28) | copy-start | bytes 1105924
  13.8 13.4 %collective-permute-start.2 = (bf16[96,1920]{1,0:T(8,128)(2,1)S(1)}, bf16[96,1920]{1,0:T(8,128)(2,1)S(1)}, u32[]{:S(2)}, u32[]{:S(2)}) collective-permute-start(bf16[96,1920]{1,0:T(8,128)(2,1)S(1)} %concatenate.28), channel_id=1, source_target_pairs={{0,8},{2,10},{4,12},{6,14},{8,16},{10,18},{12,20},{14,22},{16,24},... | collective-permute-start | bytes 1105928 | tf_op jit(solution)/shard_map/ppermute | solution.py:752
  15.4 17.7 %collective-permute-start.4 = (bf16[96,1920]{1,0:T(8,128)(2,1)S(1)}, bf16[96,1920]{1,0:T(8,128)(2,1)S(1)}, u32[]{:S(2)}, u32[]{:S(2)}) collective-permute-start(bf16[96,1920]{1,0:T(8,128)(2,1)S(1)} %concatenate.28), channel_id=1, source_target_pairs={{0,24},{2,26},{4,28},{6,30},{8,0},{10,2},{12,4},{14,6},{16,8},{18,... | collective-permute-start | bytes 1105928 | tf_op jit(solution)/shard_map/ppermute | solution.py:752
  17.7 15.4 %collective-permute-start.3 = (bf16[96,1920]{1,0:T(8,128)(2,1)S(1)}, bf16[96,1920]{1,0:T(8,128)(2,1)S(1)}, u32[]{:S(2)}, u32[]{:S(2)}) collective-permute-start(bf16[96,1920]{1,0:T(8,128)(2,1)S(1)} %concatenate.28), channel_id=1, source_target_pairs={{0,4},{2,6},{4,0},{6,2},{8,12},{10,14},{12,8},{14,10},{16,20},{18,... | collective-permute-start | bytes 1105928 | tf_op jit(solution)/shard_map/ppermute | solution.py:749
  19.2 18.1 %collective-permute-start.9 = (bf16[96,1920]{1,0:T(8,128)(2,1)S(1)}, bf16[96,1920]{1,0:T(8,128)(2,1)S(1)}, u32[]{:S(2)}, u32[]{:S(2)}) collective-permute-start(bf16[96,1920]{1,0:T(8,128)(2,1)S(1)} %concatenate.28), channel_id=1, source_target_pairs={{0,2},{2,0},{4,6},{6,4},{8,10},{10,8},{12,14},{14,12},{16,18},{18,... | collective-permute-start | bytes 1105928 | tf_op jit(solution)/shard_map/ppermute | solution.py:746
  27.2 5.9 %copy-start.23 = (bf16[96,1920]{1,0:T(8,128)(2,1)}, bf16[96,1920]{1,0:T(8,128)(2,1)S(1)}, u32[]{:S(2)}) copy-start(bf16[96,1920]{1,0:T(8,128)(2,1)S(1)} %collective-permute-done.2.refs_2_) | copy-start | bytes 1105924
  33.8 20.9 %copy-start.5 = (bf16[96,1920]{1,0:T(8,128)(2,1)}, bf16[96,1920]{1,0:T(8,128)(2,1)S(1)}, u32[]{:S(2)}) copy-start(bf16[96,1920]{1,0:T(8,128)(2,1)S(1)} %collective-permute-done.3.refs_1_) | copy-start | bytes 1105924
  33.8 18.8 %collective-permute-start.5 = (bf16[96,1920]{1,0:T(8,128)(2,1)S(1)}, bf16[96,1920]{1,0:T(8,128)(2,1)S(1)}, u32[]{:S(2)}, u32[]{:S(2)}) collective-permute-start(bf16[96,1920]{1,0:T(8,128)(2,1)S(1)} %shard_map.254), channel_id=1, source_target_pairs={{0,16},{2,18},{4,20},{6,22},{8,24},{10,26},{12,28},{14,30},{16,0},... | collective-permute-start | bytes 1105928 | tf_op jit(solution)/shard_map/ppermute | solution.py:752
  35.3 17.4 %collective-permute-start.6 = (bf16[96,1920]{1,0:T(8,128)(2,1)}, bf16[96,1920]{1,0:T(8,128)(2,1)S(1)}, u32[]{:S(2)}, u32[]{:S(2)}) collective-permute-start(bf16[96,1920]{1,0:T(8,128)(2,1)} %copy-done.23), channel_id=1, source_target_pairs={{0,4},{2,6},{4,0},{6,2},{8,12},{10,14},{12,8},{14,10},{16,20},{18,... | collective-permute-start | bytes 1105928 | tf_op jit(solution)/shard_map/ppermute | solution.py:749
  36.8 16.4 %collective-permute-start.8 = (bf16[96,1920]{1,0:T(8,128)(2,1)}, bf16[96,1920]{1,0:T(8,128)(2,1)S(1)}, u32[]{:S(2)}, u32[]{:S(2)}) collective-permute-start(bf16[96,1920]{1,0:T(8,128)(2,1)} %copy-done.24), channel_id=1, source_target_pairs={{0,4},{2,6},{4,0},{6,2},{8,12},{10,14},{12,8},{14,10},{16,20},{18,... | collective-permute-start | bytes 1105928 | tf_op jit(solution)/shard_map/ppermute | solution.py:749
  37.3 17.4 %copy-start.37 = (bf16[96,1920]{1,0:T(8,128)(2,1)}, bf16[96,1920]{1,0:T(8,128)(2,1)S(1)}, u32[]{:S(2)}) copy-start(bf16[96,1920]{1,0:T(8,128)(2,1)S(1)} %collective-permute-done.9) | copy-start | bytes 1105924
  37.3 23.6 %collective-permute-start.10 = (bf16[96,1920]{1,0:T(8,128)(2,1)}, bf16[96,1920]{1,0:T(8,128)(2,1)}, u32[]{:S(2)}, u32[]{:S(2)}) collective-permute-start(bf16[96,1920]{1,0:T(8,128)(2,1)} %copy-done.23), channel_id=1, source_target_pairs={{0,2},{2,0},{4,6},{6,4},{8,10},{10,8},{12,14},{14,12},{16,18},{18,... | collective-permute-start | bytes 1105928 | tf_op jit(solution)/shard_map/ppermute | solution.py:746
  52.6 8.2 %copy-start.6 = (bf16[96,1920]{1,0:T(8,128)(2,1)}, bf16[96,1920]{1,0:T(8,128)(2,1)S(1)}, u32[]{:S(2)}) copy-start(bf16[96,1920]{1,0:T(8,128)(2,1)S(1)} %collective-permute-done.5.refs_1_) | copy-start | bytes 1105924
  52.6 8.3 %collective-permute-start.12 = (bf16[96,1920]{1,0:T(8,128)(2,1)}, bf16[96,1920]{1,0:T(8,128)(2,1)}, u32[]{:S(2)}, u32[]{:S(2)}) collective-permute-start(bf16[96,1920]{1,0:T(8,128)(2,1)} %copy-done.24), channel_id=1, source_target_pairs={{0,2},{2,0},{4,6},{6,4},{8,10},{10,8},{12,14},{14,12},{16,18},{18,... | collective-permute-start | bytes 1105928 | tf_op jit(solution)/shard_map/ppermute | solution.py:746
  52.6 8.8 %collective-permute-start.13 = (bf16[96,1920]{1,0:T(8,128)(2,1)S(1)}, bf16[96,1920]{1,0:T(8,128)(2,1)}, u32[]{:S(2)}, u32[]{:S(2)}) collective-permute-start(bf16[96,1920]{1,0:T(8,128)(2,1)S(1)} %collective-permute-done.3.refs_1_), channel_id=1, source_target_pairs={{0,2},{2,0},{4,6},{6,4},{8,10},{10,8},{12,14},{14,12},{16,18},{18,... | collective-permute-start | bytes 1105928 | tf_op jit(solution)/shard_map/ppermute | solution.py:746
  53.1 10.7 %collective-permute-start.7 = (bf16[96,1920]{1,0:T(8,128)(2,1)S(1)}, bf16[96,1920]{1,0:T(8,128)(2,1)}, u32[]{:S(2)}, u32[]{:S(2)}) collective-permute-start(bf16[96,1920]{1,0:T(8,128)(2,1)S(1)} %collective-permute-done.5.refs_1_), channel_id=1, source_target_pairs={{0,4},{2,6},{4,0},{6,2},{8,12},{10,14},{12,8},{14,10},{16,20},{18,... | collective-permute-start | bytes 1105928 | tf_op jit(solution)/shard_map/ppermute | solution.py:749
  55.9 4.6 %copy-start.30 = (s32[1024]{0:T(1024)S(1)}, s32[1024]{0:T(1024)}, u32[]{:S(2)}) copy-start(s32[1024]{0:T(1024)} %param.16) | copy-start | bytes 12292
  55.9 4.7 %copy-start.32 = (f32[24]{0:T(128)S(1)}, f32[24]{0:T(128)}, u32[]{:S(2)}) copy-start(f32[24]{0:T(128)} %param.26) | copy-start | bytes 292
  55.9 8.1 %copy-start.33 = (f32[24]{0:T(128)S(1)}, f32[24]{0:T(128)}, u32[]{:S(2)}) copy-start(f32[24]{0:T(128)} %param.25) | copy-start | bytes 292
  55.9 8.1 %copy-start.34 = (f32[24]{0:T(128)S(1)}, f32[24]{0:T(128)}, u32[]{:S(2)}) copy-start(f32[24]{0:T(128)} %param.24) | copy-start | bytes 292
  55.9 8.1 %copy-start.12 = (bf16[512,1536]{1,0:T(8,128)(2,1)S(1)}, bf16[512,1536]{1,0:T(8,128)(2,1)}, u32[]{:S(2)}) copy-start(bf16[512,1536]{1,0:T(8,128)(2,1)} %refs_3_.3) | copy-start | bytes 4718596
  55.9 10.6 %copy-start.7 = (f32[4,256]{1,0:T(4,128)S(1)}, f32[4,256]{1,0:T(4,128)}, u32[]{:S(2)}) copy-start(f32[4,256]{1,0:T(4,128)} %refs_9_.5) | copy-start | bytes 12292
  55.9 36.0 %all-to-all-start = ((bf16[4,96,1536]{2,1,0:T(8,128)(2,1)}), bf16[4,96,1536]{2,1,0:T(8,128)(2,1)}, u32[]{:S(2)}, u32[]{:S(2)}) async-start(bf16[4,96,1536]{2,1,0:T(8,128)(2,1)} %broadcast_in_dim.94), calls=%async_computation | async-start | bytes 2359296 | tf_op jit(solution)/shard_map/all_to_all | solution.py:844
  60.4 294.7 %reduce-scatter.2.cloned.1.call-start = ((), (), s32[]{:S(2)}) async-start(), calls=%async_computation.4 | async-start | bytes 10027008 | tf_op jit(solution)/shard_map/reduce_scatter | solution.py:1226
  60.9 3.1 collective-permute-start.11
  61.0 3.7 collective-permute-start.14
  61.5 3.2 collective-permute-start.16
  63.8 1.9 collective-permute-start.15
  64.0 15.2 %copy-start.9 = (f32[1,128]{1,0:T(1,128)}, f32[1,128]{1,0:T(1,128)S(1)}, u32[]{:S(2)}) copy-start(f32[1,128]{1,0:T(1,128)S(1)} %get-tuple-element.203.refs_7_.refs_11_) | copy-start | bytes 1540
  64.0 53.4 %collective-permute-start = (bf16[512,1536]{1,0:T(8,128)(2,1)S(1)}, bf16[512,1536]{1,0:T(8,128)(2,1)}, u32[]{:S(2)}, u32[]{:S(2)}) collective-permute-start(bf16[512,1536]{1,0:T(8,128)(2,1)S(1)} %copy-done.12), channel_id=1, source_target_pairs={{0,1},{1,0},{2,3},{3,2},{4,5},{5,4},{6,7},{7,6},{8,9},{9,8},{10,11... | collective-permute-start | bytes 4718600 | tf_op jit(solution)/shard_map/ppermute | solution.py:866
  66.5 12.8 %copy-start.11 = (f32[4,1536]{1,0:T(4,128)S(1)}, f32[4,1536]{1,0:T(4,128)}, u32[]{:S(2)}) copy-start(f32[4,1536]{1,0:T(4,128)} %refs_9_.4) | copy-start | bytes 73732
  91.9 25.6 %collective-permute-start.19 = (bf16[96,1536]{1,0:T(8,128)(2,1)S(1)}, bf16[96,1536]{1,0:T(8,128)(2,1)S(1)}, u32[]{:S(2)}, u32[]{:S(2)}) collective-permute-start(bf16[96,1536]{1,0:T(8,128)(2,1)S(1)} %shard_map.259.refs_33_), channel_id=1, source_target_pairs={{0,16},{2,18},{4,20},{6,22},{8,24},{10,26},{12,28},{14,30},{16,0},... | collective-permute-start | bytes 884744 | tf_op jit(solution)/shard_map/ppermute | solution.py:752
  93.4 24.1 %collective-permute-start.20 = (bf16[96,1536]{1,0:T(8,128)(2,1)S(1)}, bf16[96,1536]{1,0:T(8,128)(2,1)S(1)}, u32[]{:S(2)}, u32[]{:S(2)}) collective-permute-start(bf16[96,1536]{1,0:T(8,128)(2,1)S(1)} %shard_map.259.refs_33_), channel_id=1, source_target_pairs={{0,24},{2,26},{4,28},{6,30},{8,0},{10,2},{12,4},{14,6},{16,8},{18,... | collective-permute-start | bytes 884744 | tf_op jit(solution)/shard_map/ppermute | solution.py:752
  94.9 22.7 %collective-permute-start.18 = (bf16[96,1536]{1,0:T(8,128)(2,1)S(1)}, bf16[96,1536]{1,0:T(8,128)(2,1)S(1)}, u32[]{:S(2)}, u32[]{:S(2)}) collective-permute-start(bf16[96,1536]{1,0:T(8,128)(2,1)S(1)} %shard_map.259.refs_33_), channel_id=1, source_target_pairs={{0,8},{2,10},{4,12},{6,14},{8,16},{10,18},{12,20},{14,22},{16,24},... | collective-permute-start | bytes 884744 | tf_op jit(solution)/shard_map/ppermute | solution.py:752
  95.9 27.4 %collective-permute-start.17 = (bf16[4,96,1536]{2,1,0:T(8,128)(2,1)}, bf16[4,96,1536]{2,1,0:T(8,128)(2,1)S(1)}, u32[]{:S(2)}, u32[]{:S(2)}) collective-permute-start(bf16[4,96,1536]{2,1,0:T(8,128)(2,1)} %shard_map.258.refs_1_.refs_32_.refs_2_), channel_id=1, source_target_pairs={{0,4},{2,6},{4,0},{6,2},{8,12},{10,14},{12,8},{14,10},{16,20},{18,... | collective-permute-start | bytes 3538952 | tf_op jit(solution)/shard_map/ppermute | solution.py:749
  117.4 9.3 %collective-permute-start.21 = (bf16[4,96,1536]{2,1,0:T(8,128)(2,1)}, bf16[4,96,1536]{2,1,0:T(8,128)(2,1)}, u32[]{:S(2)}, u32[]{:S(2)}) collective-permute-start(bf16[4,96,1536]{2,1,0:T(8,128)(2,1)} %shard_map.258.refs_1_.refs_32_.refs_2_), channel_id=1, source_target_pairs={{0,2},{2,0},{4,6},{6,4},{8,10},{10,8},{12,14},{14,12},{16,18},{18,... | collective-permute-start | bytes 3538952 | tf_op jit(solution)/shard_map/ppermute | solution.py:746
  124.3 3.2 collective-permute-start.22
  126.1 15.3 %collective-permute-start.23 = (bf16[2,96,1536]{2,1,0:T(8,128)(2,1)}, bf16[2,96,1536]{2,1,0:T(8,128)(2,1)S(1)}, u32[]{:S(2)}, u32[]{:S(2)}) collective-permute-start(bf16[2,96,1536]{2,1,0:T(8,128)(2,1)} %pad_maximum_fusion.refs_4_), channel_id=1, source_target_pairs={{0,4},{2,6},{4,0},{6,2},{8,12},{10,14},{12,8},{14,10},{16,20},{18,... | collective-permute-start | bytes 1769480 | tf_op jit(solution)/shard_map/ppermute | solution.py:749
  141.4 8.5 %collective-permute-start.24 = (f32[8,128]{1,0:T(8,128)S(1)}, f32[8,128]{1,0:T(8,128)S(1)}, u32[]{:S(2)}, u32[]{:S(2)}) collective-permute-start(f32[8,128]{1,0:T(8,128)S(1)} %shard_map.264), channel_id=1, source_target_pairs={{0,1},{1,0},{2,3},{3,2},{4,5},{5,4},{6,7},{7,6},{8,9},{9,8},{10,11... | collective-permute-start | bytes 12296 | tf_op jit(solution)/shard_map/ppermute | solution.py:866
  142.9 19.3 %collective-permute-start.25 = (bf16[2,96,1536]{2,1,0:T(8,128)(2,1)}, bf16[2,96,1536]{2,1,0:T(8,128)(2,1)S(1)}, u32[]{:S(2)}, u32[]{:S(2)}) collective-permute-start(bf16[2,96,1536]{2,1,0:T(8,128)(2,1)} %pad_maximum_fusion.1.refs_5_), channel_id=1, source_target_pairs={{0,4},{2,6},{4,0},{6,2},{8,12},{10,14},{12,8},{14,10},{16,20},{18,... | collective-permute-start | bytes 1769480 | tf_op jit(solution)/shard_map/ppermute | solution.py:749
  143.5 19.5 %collective-permute-start.27 = (bf16[2,96,1536]{2,1,0:T(8,128)(2,1)}, bf16[2,96,1536]{2,1,0:T(8,128)(2,1)}, u32[]{:S(2)}, u32[]{:S(2)}) collective-permute-start(bf16[2,96,1536]{2,1,0:T(8,128)(2,1)} %pad_maximum_fusion.1.refs_5_), channel_id=1, source_target_pairs={{0,2},{2,0},{4,6},{6,4},{8,10},{10,8},{12,14},{14,12},{16,18},{18,... | collective-permute-start | bytes 1769480 | tf_op jit(solution)/shard_map/ppermute | solution.py:746
  143.5 19.5 %collective-permute-start.26 = (bf16[2,96,1536]{2,1,0:T(8,128)(2,1)}, bf16[2,96,1536]{2,1,0:T(8,128)(2,1)}, u32[]{:S(2)}, u32[]{:S(2)}) collective-permute-start(bf16[2,96,1536]{2,1,0:T(8,128)(2,1)} %pad_maximum_fusion.refs_4_), channel_id=1, source_target_pairs={{0,2},{2,0},{4,6},{6,4},{8,10},{10,8},{12,14},{14,12},{16,18},{18,... | collective-permute-start | bytes 1769480 | tf_op jit(solution)/shard_map/ppermute | solution.py:746
  162.2 2.1 collective-permute-start.29
  163.0 2.1 collective-permute-start.28
  179.4 3.7 collective-permute-start.31
  205.0 35.6 %collective-permute-start.30 = (bf16[512,1536]{1,0:T(8,128)(2,1)}, bf16[512,1536]{1,0:T(8,128)(2,1)S(1)}, u32[]{:S(2)}, u32[]{:S(2)}) collective-permute-start(bf16[512,1536]{1,0:T(8,128)(2,1)} %get-tuple-element.96), channel_id=1, source_target_pairs={{0,1},{1,0},{2,3},{3,2},{4,5},{5,4},{6,7},{7,6},{8,9},{9,8},{10,11... | collective-permute-start | bytes 4718600 | tf_op jit(solution)/shard_map/ppermute | solution.py:866
  236.8 9.0 %collective-permute-start.32 = (bf16[8,96,1024]{2,1,0:T(8,128)(2,1)}, bf16[8,96,1024]{2,1,0:T(8,128)(2,1)}, u32[]{:S(2)}, u32[]{:S(2)}) collective-permute-start(bf16[8,96,1024]{2,1,0:T(8,128)(2,1)} %get-tuple-element.113), channel_id=1, source_target_pairs={{0,2},{2,0},{4,6},{6,4},{8,10},{10,8},{12,14},{14,12},{16,18},{18,... | collective-permute-start | bytes 4718600 | tf_op jit(solution)/shard_map/ppermute | solution.py:746
  247.3 22.3 %collective-permute-start.33 = (bf16[4,96,1024]{2,1,0:T(8,128)(2,1)S(1)}, bf16[4,96,1024]{2,1,0:T(8,128)(2,1)S(1)}, u32[]{:S(2)}, u32[]{:S(2)}) collective-permute-start(bf16[4,96,1024]{2,1,0:T(8,128)(2,1)S(1)} %fusion.2.refs_20_), channel_id=1, source_target_pairs={{0,4},{2,6},{4,0},{6,2},{8,12},{10,14},{12,8},{14,10},{16,20},{18,... | collective-permute-start | bytes 2359304 | tf_op jit(solution)/shard_map/ppermute | solution.py:749
  272.1 5.0 %copy-start.8 = (f32[4,256]{1,0:T(4,128)S(1)}, f32[4,256]{1,0:T(4,128)}, u32[]{:S(2)}) copy-start(f32[4,256]{1,0:T(4,128)} %refs_9_.5) | copy-start | bytes 12292
  272.1 5.0 %copy-start.10 = (f32[1,128]{1,0:T(1,128)S(1)}, f32[1,128]{1,0:T(1,128)}, u32[]{:S(2)}) copy-start(f32[1,128]{1,0:T(1,128)} %copy-done.9) | copy-start | bytes 1540
  272.1 34.0 %all-to-all-start.2 = ((bf16[4,96,1024]{2,1,0:T(8,128)(2,1)}), bf16[4,96,1024]{2,1,0:T(8,128)(2,1)S(1)}, u32[]{:S(2)}, u32[]{:S(2)}) async-start(bf16[4,96,1024]{2,1,0:T(8,128)(2,1)} %fusion.refs_17_.refs_1_), calls=%async_computation.3 | async-start | bytes 1572864 | tf_op jit(solution)/shard_map/all_to_all | solution.py:844
  291.0 10.8 %collective-permute-start.38 = (f32[6,1536]{1,0:T(8,128)S(1)}, f32[6,1536]{1,0:T(8,128)S(1)}, u32[]{:S(2)}, u32[]{:S(2)}) collective-permute-start(f32[6,1536]{1,0:T(8,128)S(1)} %pad_maximum_fusion.4), channel_id=1, source_target_pairs={{0,2},{2,0},{4,6},{6,4},{8,10},{10,8},{12,14},{14,12},{16,18},{18,... | collective-permute-start | bytes 110600 | tf_op jit(solution)/shard_map/ppermute | solution.py:746
  291.1 15.0 %collective-permute-start.34 = (bf16[8,96,896]{2,1,0:T(8,128)(2,1)}, bf16[8,96,896]{2,1,0:T(8,128)(2,1)}, u32[]{:S(2)}, u32[]{:S(2)}) collective-permute-start(bf16[8,96,896]{2,1,0:T(8,128)(2,1)} %shard_map.274), channel_id=1, source_target_pairs={{0,2},{2,0},{4,6},{6,4},{8,10},{10,8},{12,14},{14,12},{16,18},{18,... | collective-permute-start | bytes 4128776 | tf_op jit(solution)/shard_map/ppermute | solution.py:746
  301.9 4.2 %collective-permute-start.39 = (f32[6,1536]{1,0:T(8,128)S(1)}, f32[6,1536]{1,0:T(8,128)S(1)}, u32[]{:S(2)}, u32[]{:S(2)}) collective-permute-start(f32[6,1536]{1,0:T(8,128)S(1)} %shard_map.281), channel_id=1, source_target_pairs={{0,4},{2,6},{4,0},{6,2},{8,12},{10,14},{12,8},{14,10},{16,20},{18,... | collective-permute-start | bytes 110600 | tf_op jit(solution)/shard_map/ppermute | solution.py:749
  302.5 36.4 %collective-permute-start.35 = (bf16[512,1536]{1,0:T(8,128)(2,1)}, bf16[512,1536]{1,0:T(8,128)(2,1)}, u32[]{:S(2)}, u32[]{:S(2)}) collective-permute-start(bf16[512,1536]{1,0:T(8,128)(2,1)} %shard_map.276.refs_1_), channel_id=1, source_target_pairs={{0,1},{1,0},{2,3},{3,2},{4,5},{5,4},{6,7},{7,6},{8,9},{9,8},{10,11... | collective-permute-start | bytes 4718600 | tf_op jit(solution)/shard_map/ppermute | solution.py:866
  308.7 16.8 %collective-permute-start.36 = (bf16[4,96,896]{2,1,0:T(8,128)(2,1)S(1)}, bf16[4,96,896]{2,1,0:T(8,128)(2,1)S(1)}, u32[]{:S(2)}, u32[]{:S(2)}) collective-permute-start(bf16[4,96,896]{2,1,0:T(8,128)(2,1)S(1)} %fusion.3.refs_3_), channel_id=1, source_target_pairs={{0,4},{2,6},{4,0},{6,2},{8,12},{10,14},{12,8},{14,10},{16,20},{18,... | collective-permute-start | bytes 2064392 | tf_op jit(solution)/shard_map/ppermute | solution.py:749
  327.7 16.2 %collective-permute-start.40 = (f32[6,1536]{1,0:T(8,128)S(1)}, f32[6,1536]{1,0:T(8,128)S(1)}, u32[]{:S(2)}, u32[]{:S(2)}) collective-permute-start(f32[6,1536]{1,0:T(8,128)S(1)} %shard_map.282), channel_id=1, source_target_pairs={{0,8},{2,10},{4,12},{6,14},{8,16},{10,18},{12,20},{14,22},{16,24},... | collective-permute-start | bytes 110600 | tf_op jit(solution)/shard_map/ppermute | solution.py:752
  329.4 14.4 %collective-permute-start.41 = (f32[6,1536]{1,0:T(8,128)S(1)}, f32[6,1536]{1,0:T(8,128)S(1)}, u32[]{:S(2)}, u32[]{:S(2)}) collective-permute-start(f32[6,1536]{1,0:T(8,128)S(1)} %shard_map.282), channel_id=1, source_target_pairs={{0,16},{2,18},{4,20},{6,22},{8,24},{10,26},{12,28},{14,30},{16,0},... | collective-permute-start | bytes 110600 | tf_op jit(solution)/shard_map/ppermute | solution.py:752
  332.1 11.7 %collective-permute-start.42 = (f32[6,1536]{1,0:T(8,128)S(1)}, f32[6,1536]{1,0:T(8,128)S(1)}, u32[]{:S(2)}, u32[]{:S(2)}) collective-permute-start(f32[6,1536]{1,0:T(8,128)S(1)} %shard_map.282), channel_id=1, source_target_pairs={{0,24},{2,26},{4,28},{6,30},{8,0},{10,2},{12,4},{14,6},{16,8},{18,... | collective-permute-start | bytes 110600 | tf_op jit(solution)/shard_map/ppermute | solution.py:752
  333.5 19.6 %all-to-all-start.1 = ((bf16[4,96,896]{2,1,0:T(8,128)(2,1)}), bf16[4,96,896]{2,1,0:T(8,128)(2,1)S(1)}, u32[]{:S(2)}, u32[]{:S(2)}) async-start(bf16[4,96,896]{2,1,0:T(8,128)(2,1)} %fusion.1.refs_1_), calls=%async_computation.1 | async-start | bytes 1376256 | tf_op jit(solution)/shard_map/all_to_all | solution.py:844
  343.9 3.7 collective-permute-start.43
  357.3 5.2 %collective-permute-start.37 = (f32[96,384]{1,0:T(8,128)S(1)}, f32[96,384]{1,0:T(8,128)S(1)}, u32[]{:S(2)}, u32[]{:S(2)}) collective-permute-start(f32[96,384]{1,0:T(8,128)S(1)} %pad_maximum_fusion.3), channel_id=1, source_target_pairs={{0,1},{1,0},{2,3},{3,2},{4,5},{5,4},{6,7},{7,6},{8,9},{9,8},{10,11... | collective-permute-start | bytes 442376 | tf_op jit(solution)/shard_map/ppermute | solution.py:866
  (27 other events, 44.6 us)
Sparse Core Ops, SparseCore 0:
  205.1 112.1 reduce-scatter.1
